TPU v7x, 512 devices: a whole 4x4x16 slice. The times are simulated.
512 devices in a mesh: expert: 128 (over z, y, core), dp: 4 (over x).
Axes of the slice: x: 4, y: 4, z: 16, core: 2. Of those that a mesh axis runs over, the one named last changes fastest.
Arguments:
- tokens: bfloat16 [16384, 2048], P('expert', 'dp'), may hold values from -6 to 6
- grad_out: bfloat16 [16384, 2048], P('expert', 'dp'), may hold values from -6 to 6
- routes: int32 [16384, 8], P('expert'), may hold values from 0 to 127, all different within a row; in each aligned block of 128 rows (0 to 127, 128 to 255, ...) at most 12 rows name the same one
- gates: float32 [16384, 8], P('expert'), may hold values from 0.1 to 1
- w_gate: bfloat16 [128, 2048, 384], P('expert', 'dp'), may hold values from -0.125 to 0.125
- w_up: bfloat16 [128, 2048, 384], P('expert', 'dp'), may hold values from -0.125 to 0.125
- w_down: bfloat16 [128, 384, 2048], P('expert', None, 'dp'), may hold values from -0.3125 to 0.3125
Outputs:
- d_tokens: bfloat16 [16384, 2048], P('expert', 'dp')
- grad_gate: bfloat16 [128, 2048, 384], P('expert', 'dp')
- grad_up: bfloat16 [128, 2048, 384], P('expert', 'dp')
- grad_down: bfloat16 [128, 384, 2048], P('expert', None, 'dp')
Inputs may be any that keep to these rules, and one draw needn't show every extreme that they name: `routes`: each row names 8 different experts; in each aligned block of 128 rows no expert is named by more than 12 rows, a bound that some block reaches.
All inputs are finite; a program needn't handle non-finite values.
Results may differ from a plain program's by a relative error of at most 0.013.
Values may be sent and summed in bfloat16 or wider, within the bound.
No kernel may reach another device: no remote copies, remote signals or barrier semaphores. Data moves between devices by JAX's collectives and lax.ppermute only.
A program may use at most 64 MiB of HBM per device.

v0:
```python
import jax
import jax.numpy as jnp
from jax import lax
from jax.sharding import PartitionSpec as P


def contract_rows(left_rows, right_rows):
    return lax.dot_general(
        left_rows, right_rows, (((0,), (0,)), ((), ())), preferred_element_type=jnp.float32
    )


def contract_cols(left_rows, right_rows):
    return lax.dot_general(
        left_rows, right_rows, (((1,), (1,)), ((), ())), preferred_element_type=jnp.float32
    )


def per_source(left_rows, right_rows, dp_count):
    left_split = left_rows.reshape(dp_count, -1, left_rows.shape[1])
    right_split = right_rows.reshape(dp_count, -1, right_rows.shape[1])
    partial_value = jnp.einsum(
        "jra,jrb->jab", left_split, right_split, preferred_element_type=jnp.float32
    )
    rounded = lax.optimization_barrier(partial_value.astype(jnp.bfloat16))
    return jnp.sum(rounded.astype(jnp.float32), axis=0).astype(jnp.bfloat16)


def shards(tokens, grad_out, routes, gates, w_gate, w_up, w_down):
    experts = lax.axis_size("expert")
    dp_count = lax.axis_size("dp")
    tok_count = tokens.shape[0]
    top_count = routes.shape[1]
    slot_cap = min(tok_count, max(2, 3 * tok_count * top_count // (2 * experts)))
    row_total = tok_count * top_count
    flat_routes = routes.reshape(-1)
    flat_gates = gates.reshape(-1)
    onehot = (flat_routes[:, None] == jnp.arange(experts, dtype=jnp.int32)[None, :]).astype(
        jnp.int32
    )
    slot_rank = jnp.sum((jnp.cumsum(onehot, axis=0) - onehot) * onehot, axis=1)
    slot_index = flat_routes * slot_cap + slot_rank
    slot_source = (
        jnp.full((experts * slot_cap,), row_total, jnp.int32)
        .at[slot_index]
        .set(jnp.arange(row_total, dtype=jnp.int32))
    )
    valid = slot_source < row_total
    safe_rows = jnp.where(valid, slot_source, 0)
    token_ids = safe_rows // top_count
    token_slots = jnp.where(valid[:, None], tokens[token_ids], jnp.zeros((), tokens.dtype))
    scaled_slots = jnp.where(
        valid[:, None],
        grad_out[token_ids].astype(jnp.float32) * flat_gates[safe_rows][:, None],
        0.0,
    ).astype(jnp.bfloat16)
    input_cols, scaled_cols = (
        lax.all_to_all(token_slots, "expert", split_axis=0, concat_axis=0, tiled=True),
        lax.all_to_all(scaled_slots, "expert", split_axis=0, concat_axis=0, tiled=True),
    )
    inputs, scaled = (
        lax.all_to_all(input_cols, "dp", split_axis=0, concat_axis=1, tiled=True),
        lax.all_to_all(scaled_cols, "dp", split_axis=0, concat_axis=1, tiled=True),
    )
    full_gate, full_up, full_down = (
        lax.all_gather(w_gate, "dp", axis=1, tiled=True),
        lax.all_gather(w_up, "dp", axis=1, tiled=True),
        lax.all_gather(w_down, "dp", axis=2, tiled=True),
    )
    full_gate = full_gate[0]
    full_up = full_up[0]
    full_down = full_down[0]
    pre_gate = jnp.dot(inputs, full_gate, preferred_element_type=jnp.float32)
    pre_up = jnp.dot(inputs, full_up, preferred_element_type=jnp.float32)
    sigmoid_gate = jax.nn.sigmoid(pre_gate)
    activated = pre_gate * sigmoid_gate
    hidden = (activated * pre_up).astype(jnp.bfloat16)
    back_hidden = contract_cols(scaled, full_down)
    d_up = (back_hidden * activated).astype(jnp.bfloat16)
    d_gate = (back_hidden * pre_up * sigmoid_gate * (1.0 + pre_gate * (1.0 - sigmoid_gate))).astype(
        jnp.bfloat16
    )
    row_grad = (contract_cols(d_gate, full_gate) + contract_cols(d_up, full_up)).astype(
        jnp.bfloat16
    )
    came_back = lax.all_to_all(
        lax.all_to_all(row_grad, "dp", split_axis=1, concat_axis=0, tiled=True),
        "expert",
        split_axis=0,
        concat_axis=0,
        tiled=True,
    )
    picked = came_back[slot_index].astype(jnp.float32)
    d_tokens = jnp.sum(picked.reshape(tok_count, top_count, -1), axis=1).astype(jnp.bfloat16)
    hidden_all = lax.all_gather(hidden, "dp", axis=0, tiled=True)
    grad_down = per_source(hidden_all, scaled_cols, dp_count)
    gate_part = contract_rows(inputs, d_gate).astype(jnp.bfloat16).astype(jnp.float32)
    up_part = contract_rows(inputs, d_up).astype(jnp.bfloat16).astype(jnp.float32)
    gate_sum, up_sum = (
        lax.psum_scatter(
            gate_part.astype(jnp.bfloat16), "dp", scatter_dimension=0, tiled=True
        ).astype(jnp.float32),
        lax.psum_scatter(
            up_part.astype(jnp.bfloat16), "dp", scatter_dimension=0, tiled=True
        ).astype(jnp.float32),
    )
    grad_gate = gate_sum.astype(jnp.bfloat16)
    grad_up = up_sum.astype(jnp.bfloat16)
    return (d_tokens, grad_gate[None], grad_up[None], grad_down[None])


def solution(mesh):
    return jax.shard_map(
        shards,
        mesh=mesh,
        in_specs=(
            P("expert", "dp"),
            P("expert", "dp"),
            P("expert", None),
            P("expert", None),
            P("expert", "dp", None),
            P("expert", "dp", None),
            P("expert", None, "dp"),
        ),
        out_specs=(
            P("expert", "dp"),
            P("expert", "dp", None),
            P("expert", "dp", None),
            P("expert", None, "dp"),
        ),
        check_vma=False,
    )
```

profile of v0, /device:TPU:6, one launch (start us, length us, event | category | flops | bytes accessed | tf_op | source)
XLA Modules:
  0.0 484.4 jit_solution(17705652545422683702)
XLA Ops:
  10.0 4.3 scatter_custom_fusion
  14.4 4.8 gather_fusion
  21.6 5.9 %gather_fusion.1 = f32[1536]{0:T(1024)S(1)} fusion(f32[1024]{0:T(1024)S(1)} %reshape.103, s32[2048]{0:T(1024)S(1)} %get-tuple-element.9), kind=kCustom, calls=%fused_computation.1 | custom fusion | bytes 18432 | tf_op jit(solution)/shard_map/gather | solution.py:54
  27.7 3.6 select_convert_fusion
  31.3 20.1 %all-to-all-start = ((bf16[128,12,512]{2,1,0:T(8,128)(2,1)}), bf16[128,12,512]{2,1,0:T(8,128)(2,1)S(1)}, u32[]{:S(2)}, u32[]{:S(2)}) async-start(bf16[128,12,512]{2,1,0:T(8,128)(2,1)} %select_convert_fusion), calls=%async_computation | async-start | bytes 4194304 | tf_op jit(solution)/shard_map/all_to_all | solution.py:59
  51.4 5.4 %gather_fusion.2 = bf16[1536,512]{1,0:T(8,128)(2,1)} fusion(bf16[128,512]{1,0:T(8,128)(2,1)S(1)} %copy-done.1, s32[2048]{0:T(1024)S(1)} %get-tuple-element.10), kind=kCustom, calls=%fused_computation.2 | custom fusion | bytes 3151872 | tf_op jit(solution)/shard_map/gather | solution.py:51
  56.8 3.7 gather.19
  60.4 2.8 broadcast_select_fusion
  63.2 86.4 %all-to-all-done = bf16[128,12,512]{2,1,0:T(8,128)(2,1)S(1)} async-done(((bf16[128,12,512]{2,1,0:T(8,128)(2,1)}), bf16[128,12,512]{2,1,0:T(8,128)(2,1)S(1)}, u32[]{:S(2)}, u32[]{:S(2)}) %all-to-all-start) | async-done | bytes 1572896 | tf_op jit(solution)/shard_map/all_to_all | solution.py:59
  151.0 8.7 %all-to-all-start.2 = ((bf16[128,12,512]{2,1,0:T(8,128)(2,1)}), bf16[128,12,512]{2,1,0:T(8,128)(2,1)S(1)}, u32[]{:S(2)}, u32[]{:S(2)}) async-start(bf16[128,12,512]{2,1,0:T(8,128)(2,1)} %broadcast_select_fusion), calls=%async_computation.2 | async-start | bytes 4194304 | tf_op jit(solution)/shard_map/all_to_all | solution.py:58
  161.2 3.7 all_to_all.57
  164.8 93.1 %all-to-all-done.2 = bf16[128,12,512]{2,1,0:T(8,128)(2,1)S(1)} async-done(((bf16[128,12,512]{2,1,0:T(8,128)(2,1)}), bf16[128,12,512]{2,1,0:T(8,128)(2,1)S(1)}, u32[]{:S(2)}, u32[]{:S(2)}) %all-to-all-start.2) | async-done | bytes 1572896 | tf_op jit(solution)/shard_map/all_to_all | solution.py:58
  257.9 4.8 all-to-all-start.1
  264.8 17.4 %all-to-all-done.1 = bf16[4,384,512]{2,1,0:T(8,128)(2,1)} async-done(((bf16[4,384,512]{2,1,0:T(8,128)(2,1)}), bf16[4,384,512]{2,1,0:T(8,128)(2,1)}, u32[]{:S(2)}, u32[]{:S(2)}) %all-to-all-start.1) | async-done | bytes 1572896 | tf_op jit(solution)/shard_map/all_to_all | solution.py:63
  282.2 6.0 %all-to-all-start.3 = ((bf16[4,384,512]{2,1,0:T(8,128)(2,1)}), bf16[4,384,512]{2,1,0:T(8,128)(2,1)S(1)}, u32[]{:S(2)}, u32[]{:S(2)}) async-start(bf16[4,384,512]{2,1,0:T(8,128)(2,1)} %all_to_all.62), calls=%async_computation.3 | async-start | bytes 3145728 | tf_op jit(solution)/shard_map/all_to_all | solution.py:62
  290.8 18.8 %all-to-all-done.3 = bf16[4,384,512]{2,1,0:T(8,128)(2,1)S(1)} async-done(((bf16[4,384,512]{2,1,0:T(8,128)(2,1)}), bf16[4,384,512]{2,1,0:T(8,128)(2,1)S(1)}, u32[]{:S(2)}, u32[]{:S(2)}) %all-to-all-start.3) | async-done | bytes 1572896 | tf_op jit(solution)/shard_map/all_to_all | solution.py:62
  310.5 3.8 fusion.7
  314.3 3.2 fusion.2
  317.5 3.9 multiply_convert_fusion
  324.7 29.0 %all_to_all.78 = bf16[384,4,512]{2,0,1:T(8,128)(2,1)S(1)} all-to-all(bf16[384,4,512]{2,0,1:T(8,128)(2,1)S(1)} %bitcast.58), channel_id=1, replica_groups=mesh['expert'=128,'dp'=4] {'dp'}, dimensions={1} | all-to-all | bytes 3145728 | tf_op jit(solution)/shard_map/all_to_all | solution.py:87
  355.2 16.7 %all-to-all-start.5 = ((bf16[128,12,512]{2,1,0:T(8,128)(2,1)}), bf16[128,12,512]{2,1,0:T(8,128)(2,1)}, u32[]{:S(2)}, u32[]{:S(2)}) async-start(bf16[128,12,512]{2,1,0:T(8,128)(2,1)} %all_to_all.69), calls=%async_computation.5 | async-start | bytes 4194304 | tf_op jit(solution)/shard_map/all_to_all | solution.py:86
  377.6 2.8 convolution_convert_fusion.2
  381.5 88.2 %all-to-all-done.5 = bf16[128,12,512]{2,1,0:T(8,128)(2,1)} async-done(((bf16[128,12,512]{2,1,0:T(8,128)(2,1)}), bf16[128,12,512]{2,1,0:T(8,128)(2,1)}, u32[]{:S(2)}, u32[]{:S(2)}) %all-to-all-start.5) | async-done | bytes 1572896 | tf_op jit(solution)/shard_map/all_to_all | solution.py:86
  472.2 4.0 gather_fusion.3
  (73 shorter events, 29.1 us)
Async XLA Ops:
  7.2 7.2 %copy-start = (bf16[128,512]{1,0:T(8,128)(2,1)S(1)}, bf16[128,512]{1,0:T(8,128)(2,1)}, u32[]{:S(2)}) copy-start(bf16[128,512]{1,0:T(8,128)(2,1)} %param.8) | copy-start | bytes 393220
  19.2 2.2 copy-start.8
  31.3 20.1 %copy-start.1 = (bf16[128,512]{1,0:T(8,128)(2,1)S(1)}, bf16[128,512]{1,0:T(8,128)(2,1)}, u32[]{:S(2)}) copy-start(bf16[128,512]{1,0:T(8,128)(2,1)} %param.7) | copy-start | bytes 393220
  31.3 118.3 %all-to-all-start = ((bf16[128,12,512]{2,1,0:T(8,128)(2,1)}), bf16[128,12,512]{2,1,0:T(8,128)(2,1)S(1)}, u32[]{:S(2)}, u32[]{:S(2)}) async-start(bf16[128,12,512]{2,1,0:T(8,128)(2,1)} %select_convert_fusion), calls=%async_computation | async-start | bytes 4194304 | tf_op jit(solution)/shard_map/all_to_all | solution.py:59
  149.6 1.4 copy-start.2
  151.0 106.9 %all-to-all-start.2 = ((bf16[128,12,512]{2,1,0:T(8,128)(2,1)}), bf16[128,12,512]{2,1,0:T(8,128)(2,1)S(1)}, u32[]{:S(2)}, u32[]{:S(2)}) async-start(bf16[128,12,512]{2,1,0:T(8,128)(2,1)} %broadcast_select_fusion), calls=%async_computation.2 | async-start | bytes 4194304 | tf_op jit(solution)/shard_map/all_to_all | solution.py:58
  159.7 150.8 %all-gather.5.cloned.1.call-start = ((), (), s32[]{:S(2)}) async-start(), calls=%async_computation.8 | async-start | bytes 1966080 | tf_op jit(solution)/shard_map/all_gather | solution.py:68
  160.4 153.8 %all-gather.9.cloned.1.call-start = ((), (), s32[]{:S(2)}) async-start(), calls=%async_computation.10 | async-start | bytes 1966080 | tf_op jit(solution)/shard_map/all_gather | solution.py:66
  257.9 24.3 %all-to-all-start.1 = ((bf16[4,384,512]{2,1,0:T(8,128)(2,1)}), bf16[4,384,512]{2,1,0:T(8,128)(2,1)}, u32[]{:S(2)}, u32[]{:S(2)}) async-start(bf16[4,384,512]{2,1,0:T(8,128)(2,1)} %all_to_all.57), calls=%async_computation.1 | async-start | bytes 3145728 | tf_op jit(solution)/shard_map/all_to_all | solution.py:63
  262.7 54.7 %all-gather.7.cloned.1.call-start = ((), (), s32[]{:S(2)}) async-start(), calls=%async_computation.9 | async-start | bytes 1966080 | tf_op jit(solution)/shard_map/all_gather | solution.py:67
  282.2 27.4 %all-to-all-start.3 = ((bf16[4,384,512]{2,1,0:T(8,128)(2,1)}), bf16[4,384,512]{2,1,0:T(8,128)(2,1)S(1)}, u32[]{:S(2)}, u32[]{:S(2)}) async-start(bf16[4,384,512]{2,1,0:T(8,128)(2,1)} %all_to_all.62), calls=%async_computation.3 | async-start | bytes 3145728 | tf_op jit(solution)/shard_map/all_to_all | solution.py:62
  288.2 89.4 %all-gather.11.cloned.1.call-start = ((), (), s32[]{:S(2)}) async-start(), calls=%async_computation.13 | async-start | bytes 1474560 | tf_op jit(solution)/shard_map/all_gather | solution.py:95
  317.5 3.9 copy-start.3
  321.4 2.1 copy-start.4
  321.4 2.1 copy-start.5
  355.2 16.8 %copy-start.7 = (bf16[384,384]{1,0:T(8,128)(2,1)S(1)}, bf16[384,384]{1,0:T(8,128)(2,1)}, u32[]{:S(2)}) copy-start(bf16[384,384]{1,0:T(8,128)(2,1)} %get-tuple-element.5) | copy-start | bytes 884740
  355.2 114.5 %all-to-all-start.5 = ((bf16[128,12,512]{2,1,0:T(8,128)(2,1)}), bf16[128,12,512]{2,1,0:T(8,128)(2,1)}, u32[]{:S(2)}, u32[]{:S(2)}) async-start(bf16[128,12,512]{2,1,0:T(8,128)(2,1)} %all_to_all.69), calls=%async_computation.5 | async-start | bytes 4194304 | tf_op jit(solution)/shard_map/all_to_all | solution.py:86
  371.9 105.6 %reduce-scatter.3.cloned.1.call-start = ((), (), s32[]{:S(2)}) async-start(), calls=%async_computation.11 | async-start | bytes 1966080 | tf_op jit(solution)/shard_map/reduce_scatter | solution.py:100
  374.3 1.0 copy-start.6
  374.4 103.2 %reduce-scatter.5.cloned.1.call-start = ((), (), s32[]{:S(2)}) async-start(), calls=%async_computation.12 | async-start | bytes 1966080 | tf_op jit(solution)/shard_map/reduce_scatter | solution.py:103
Sparse Core Ops, SparseCore 0:
  162.6 33.6 all-gather.4
  198.4 34.3 all-gather.8
  265.7 34.5 all-gather.6
  321.5 35.2 all-gather.10
  375.8 32.5 reduce-scatter.2
  411.8 33.1 reduce-scatter.4
where the time goes:
time: 488 us; the launch traced here: 484 us
  waiting for transfers between devices  306 us (63%)
  starting transfers between devices  56.5 us (12%)
  local copies, waits for them, and re-layouts  46.9 us (10%)
  blocking collectives  29 us (6%)
  matrix products  21.4 us (4%)
  between operations  14.4 us (3%)
  other arithmetic  10.1 us (2%)
    all_to_all x1, waiting for transfers between devices, shards(): lax.all_to_all(token_slots, 'expert', split_axis=0, concat_axis=0, tiled=...  93.1 us
    all_to_all x1, waiting for transfers between devices, shards(): lax.all_to_all(lax.all_to_all(row_grad, 'dp', split_axis=1, concat_axis=0...  88.2 us
    all_to_all x1, waiting for transfers between devices, shards(): lax.all_to_all(scaled_slots, 'expert', split_axis=0, concat_axis=0, tiled...  86.4 us
    all_to_all x1, blocking collectives, shards(): lax.all_to_all(row_grad, 'dp', split_axis=1, concat_axis=0, tiled=True)  29 us
    all_to_all x1, starting transfers between devices, shards(): lax.all_to_all(scaled_slots, 'expert', split_axis=0, concat_axis=0, tiled...  20.1 us
    all_to_all x1, waiting for transfers between devices, shards(): lax.all_to_all(input_cols, 'dp', split_axis=0, concat_axis=1, tiled=True)  18.8 us
    all_to_all x1, waiting for transfers between devices, shards(): lax.all_to_all(scaled_cols, 'dp', split_axis=0, concat_axis=1, tiled=True)  17.4 us
    all_to_all x1, starting transfers between devices, shards(): lax.all_to_all(lax.all_to_all(row_grad, 'dp', split_axis=1, concat_axis=0...  16.7 us
  transfers between devices with their start and end apart: 11, of which 5 were waited for; matrix products, arithmetic and copies ran while one was open for 8% of the time, Pallas kernels for 0%

commit v1 on v0

v1 whole, which is shorter than its diff:
```python
import jax
import jax.numpy as jnp
from jax import lax
from jax.sharding import Mesh
from jax.sharding import PartitionSpec as P

MOST = 12
N_Z, N_Y, N_C, N_X = 16, 4, 2, 4
PLANE = ("x", "y", "c")
F32 = jnp.float32
BF16 = jnp.bfloat16


def dot(left, right, contract, batch=((), ())):
    return lax.dot_general(left, right, (contract, batch), preferred_element_type=F32)


def shift(value, by):
    return lax.ppermute(value, "x", [(i, (i + by) % N_X) for i in range(N_X)])


def gather_x(value, me):
    whole = jnp.zeros((N_X,) + value.shape, value.dtype)
    for by in range(N_X):
        piece = value if by == 0 else shift(value, by)
        whole = lax.dynamic_update_slice_in_dim(whole, piece[None], (me - by) % N_X, 0)
    return whole


def plan(routes, gates, me_z):
    tok = routes.shape[0]
    mine = jnp.concatenate([routes.T.astype(F32), gates.T], axis=0)
    every = lax.all_to_all(
        jnp.broadcast_to(mine[None], (N_Z,) + mine.shape), "z", split_axis=0, concat_axis=0, tiled=True
    )
    top = routes.shape[1]
    near = N_Y * N_C
    named = every[:, :top].reshape(N_Z, top, 1, tok)
    weight = every[:, top:].reshape(N_Z, top, 1, tok)
    wanted = (me_z * near + jnp.arange(near, dtype=jnp.int32)).astype(F32)
    hit = named == wanted[None, None, :, None]
    member = jnp.sum(hit.astype(F32), axis=1)
    gate = jnp.sum(jnp.where(hit, weight, 0.0), axis=1)
    before = (jnp.arange(tok)[:, None] < jnp.arange(tok)[None, :]).astype(BF16)
    rank = dot(member.astype(BF16), before, ((2,), (0,)))
    within = (jnp.arange(N_Z) % (N_Z // N_X) * MOST).astype(F32)
    slot = jnp.where(member > 0.5, rank + within[:, None, None], -1.0)

    def by_group(value):
        value = value.reshape(N_X, N_Z // N_X, near, tok)
        return value.transpose(0, 2, 1, 3).reshape(N_X, near, 1, N_Z // N_X * tok)

    slots = N_Z // N_X * MOST
    pick = by_group(slot) == jnp.arange(slots, dtype=jnp.int32).astype(F32)[None, None, :, None]
    row_gate = jnp.sum(jnp.where(pick, by_group(gate), 0.0), axis=3)
    return (
        pick.astype(BF16).reshape(N_X, near * slots, N_Z // N_X * tok),
        row_gate.reshape(N_X, near * slots, 1),
    )


def shards(tokens, grad_out, routes, gates, w_gate, w_up, w_down):
    me_z, me_x = lax.axis_index("z"), lax.axis_index("x")
    tok, cols = tokens.shape
    both = jnp.concatenate([tokens, grad_out], axis=1)
    column = lax.all_gather(both, "z", axis=0, tiled=True).reshape(N_X, N_Z // N_X * tok, 2 * cols)
    pick, row_gate = plan(routes, gates, me_z)
    full_gate = gather_x(w_gate[0], me_x)
    full_up = gather_x(w_up[0], me_x)
    full_down = gather_x(w_down[0], me_x)

    rows = dot(pick, column, ((2,), (1,)), ((0,), (0,)))
    scale = jnp.where(jnp.arange(2 * cols)[None, None, :] < cols, 1.0, row_gate)
    rows = (rows * scale).astype(BF16)
    count = rows.shape[1]
    slots = count // (N_Y * N_C)
    rows = lax.all_to_all(
        rows.reshape(-1, slots, 2 * cols), PLANE, split_axis=0, concat_axis=0, tiled=True
    ).reshape(N_X, count, 2 * cols)
    inputs, scaled = rows[:, :, :cols], rows[:, :, cols:]

    def over_features(left, right, axis):
        return sum(dot(left[j], right[j], ((1,), (axis,))) for j in range(N_X))

    pre_gate = over_features(inputs, full_gate, 0)
    pre_up = over_features(inputs, full_up, 0)
    back_hidden = over_features(scaled, full_down, 1)
    sigmoid_gate = jax.nn.sigmoid(pre_gate)
    activated = pre_gate * sigmoid_gate
    hidden = (activated * pre_up).astype(BF16)
    d_up = (back_hidden * activated).astype(BF16)
    d_gate = (back_hidden * pre_up * sigmoid_gate * (1.0 + pre_gate * (1.0 - sigmoid_gate))).astype(BF16)

    row_grad = jnp.stack(
        [
            (dot(d_gate, full_gate[j], ((1,), (1,))) + dot(d_up, full_up[j], ((1,), (1,)))).astype(BF16)
            for j in range(N_X)
        ]
    )
    came_back = lax.all_to_all(
        row_grad.reshape(-1, slots, cols), PLANE, split_axis=0, concat_axis=0, tiled=True
    ).reshape(N_X, count, cols)
    token_grad = dot(pick, came_back, ((1,), (1,)), ((0,), (0,))).astype(BF16)
    d_tokens = lax.psum_scatter(token_grad.reshape(-1, cols), "z", scatter_dimension=0, tiled=True)

    totals = [None, None, None]
    for by in (1, 3, 2, 0):
        to = (me_x + by) % N_X
        ins = lax.dynamic_index_in_dim(inputs, to, 0, keepdims=False)
        outs = lax.dynamic_index_in_dim(scaled, to, 0, keepdims=False)
        for k, (left, right) in enumerate(((ins, d_gate), (ins, d_up), (hidden, outs))):
            part = dot(left, right, ((0,), (0,))).astype(BF16)
            part = (shift(part, by) if by else part).astype(F32)
            totals[k] = part if totals[k] is None else totals[k] + part
    grads = [total.astype(BF16)[None] for total in totals]
    return (d_tokens, *grads)


def solution(mesh):
    fine = Mesh(mesh.devices.reshape(N_Z, N_Y, N_C, N_X), ("z", "y", "c", "x"))
    expert = ("z", "y", "c")
    return jax.shard_map(
        shards,
        mesh=fine,
        in_specs=(
            P(expert, "x"),
            P(expert, "x"),
            P(expert, None),
            P(expert, None),
            P(expert, "x", None),
            P(expert, "x", None),
            P(expert, None, "x"),
        ),
        out_specs=(
            P(expert, "x"),
            P(expert, "x", None),
            P(expert, "x", None),
            P(expert, None, "x"),
        ),
        check_vma=False,
    )
```

time: 488 us -> 334 us (0.68)
  waiting for transfers between devices: 306 us -> 142 us
  local copies, waits for them, and re-layouts: 46.9 us -> 19.6 us
  matrix products: 21.4 us -> 44.4 us
  starting transfers between devices: 56.5 us -> 79.2 us
  other arithmetic: 10.1 us -> 4.4 us
    all_to_all x5 -> x2, waiting for transfers between devices: 304 us -> 14.6 us  [the longest x1 14.6 us: plan(): lax.all_to_all(jnp.broadcast_to(mine[None], (N_Z,) + mine.shape), 'z', sp...]
    ppermute x0 -> x18, waiting for transfers between devices: none -> 66.3 us  [shift(): return lax.ppermute(value, 'x', [(i, (i + by) % N_X) for i in range(N_X)])]
    ppermute x0 -> x18, starting transfers between devices: none -> 56.2 us  [shift(): return lax.ppermute(value, 'x', [(i, (i + by) % N_X) for i in range(N_X)])]
    all_gather x4 -> x1, waiting for transfers between devices: 0.05 us -> 52.1 us  [shards(): lax.all_gather(both, 'z', axis=0, tiled=True)]
    all_to_all x5 -> x2, starting transfers between devices: 56.3 us -> 22.8 us  [the longest x1 15.2 us: plan(): lax.all_to_all(jnp.broadcast_to(mine[None], (N_Z,) + mine.shape), 'z', sp...]
    gather x5 -> x0, local copies, waits for them, and re-layouts: 23.7 us -> none  [the longest x2 9.07 us: shards(): tokens[token_ids]]
    dot_general x8 -> x35, matrix products: 21.4 us -> 44.4 us  [dot(): lax.dot_general(left, right, (contract, batch), preferred_element_type=F32)]
    dynamic_update_slice x0 -> x12, local copies, waits for them, and re-layouts: none -> 14.5 us  [gather_x(): lax.dynamic_update_slice_in_dim(whole, piece[None], (me - by) % N_X, 0)]
  transfers between devices with their start and end apart: 11 -> 22, of which waited for: 5 -> 11; matrix products, arithmetic and copies ran while one was open for 8% -> 9% of each run, Pallas kernels for 0% -> 0%
where the time goes in v1:
time: 334 us; the launch traced here: 332 us
  waiting for transfers between devices  142 us (43%)
  starting transfers between devices  79.2 us (24%)
  matrix products  44.4 us (13%)
  blocking collectives  27.8 us (8%)
  local copies, waits for them, and re-layouts  19.6 us (6%)
  between operations  14.7 us (4%)
  other arithmetic  4.4 us (1%)
    ppermute x18, waiting for transfers between devices, shift(): return lax.ppermute(value, 'x', [(i, (i + by) % N_X) for i in range(N_X)])  66.3 us
    ppermute x18, starting transfers between devices, shift(): return lax.ppermute(value, 'x', [(i, (i + by) % N_X) for i in range(N_X)])  56.2 us
    all_gather x1, waiting for transfers between devices, shards(): lax.all_gather(both, 'z', axis=0, tiled=True)  52.1 us
    dot_general x35, matrix products, dot(): lax.dot_general(left, right, (contract, batch), preferred_element_type=F32)  44.4 us
    all_to_all x1, blocking collectives, shards(): lax.all_to_all(row_grad.reshape(-1, slots, cols), PLANE, split_axis=0, co...  27.8 us
    all_to_all x1, starting transfers between devices, plan(): lax.all_to_all(jnp.broadcast_to(mine[None], (N_Z,) + mine.shape), 'z', sp...  15.2 us
    all_to_all x1, waiting for transfers between devices, plan(): lax.all_to_all(jnp.broadcast_to(mine[None], (N_Z,) + mine.shape), 'z', sp...  14.6 us
    dynamic_update_slice x12, local copies, waits for them, and re-layouts, gather_x(): lax.dynamic_update_slice_in_dim(whole, piece[None], (me - by) % N_X, 0)  14.5 us
  transfers between devices with their start and end apart: 22, of which 11 were waited for; matrix products, arithmetic and copies ran while one was open for 9% of the time, Pallas kernels for 0%

profile of v1, /device:TPU:6, one launch (start us, length us, event | category | flops | bytes accessed | tf_op | source)
XLA Modules:
  0.0 331.9 jit_solution(9735553200323661937)
XLA Ops:
  11.0 15.2 %all-to-all-start = ((f32[16,16,128]{2,1,0:T(8,128)}), f32[16,16,128]{2,1,0:T(8,128)S(1)}, u32[]{:S(2)}, u32[]{:S(2)}) async-start(f32[16,16,128]{2,1,0:T(8,128)} %broadcast_in_dim.103), calls=%async_computation | async-start | bytes 262144 | tf_op jit(solution)/shard_map/all_to_all | solution.py:33
  26.3 14.6 %all-to-all-done = f32[16,16,128]{2,1,0:T(8,128)S(1)} async-done(((f32[16,16,128]{2,1,0:T(8,128)}), f32[16,16,128]{2,1,0:T(8,128)S(1)}, u32[]{:S(2)}, u32[]{:S(2)}) %all-to-all-start) | async-done | bytes 131104 | tf_op jit(solution)/shard_map/all_to_all | solution.py:33
  42.3 52.1 %all-gather.2.cloned.1.call-done = bf16[2048,1024]{1,0:T(8,128)(2,1)} async-done(((bf16[128,1024]{1,0:T(8,128)(2,1)}), bf16[2048,1024]{1,0:T(8,128)(2,1)}) %all-gather.2.cloned.1.call-update) | async-done | bytes 4194320 | tf_op jit(solution)/shard_map/all_gather | solution.py:66
  94.4 5.6 %multiply_convert_fusion = bf16[4,384,1024]{2,1,0:T(8,128)(2,1)} fusion(f32[4,384]{1,0:T(4,128)S(1)} %broadcast_in_dim.112, pred[1024]{0:T(1024)(128)(4,1)S(1)} %iota_compare_fusion.1, pred[4,384,512]{2,1,0:T(32,128)(4,1)S(1)} %bitcast_compare_fusion, bf16[4,512,1024]{2,1,0:T(8,128)(2,1)} %bitcast.227), kind=kOutput, calls=%fused_computation | convolution fusion | flops 1615331328 | bytes 8133632 | tf_op jit(solution)/shard_map/dot_general | solution.py:15
  100.0 7.6 %all-to-all-start.1 = ((bf16[32,48,1024]{2,1,0:T(8,128)(2,1)}), bf16[32,48,1024]{2,1,0:T(8,128)(2,1)S(1)}, u32[]{:S(2)}, u32[]{:S(2)}) async-start(bf16[32,48,1024]{2,1,0:T(8,128)(2,1)} %bitcast.213), calls=%async_computation.1 | async-start | bytes 6291456 | tf_op jit(solution)/shard_map/all_to_all | solution.py:77
  109.9 4.6 %collective-permute-start.7 = (bf16[512,384]{1,0:T(8,128)(2,1)S(1)}, bf16[512,384]{1,0:T(8,128)(2,1)}, u32[]{:S(2)}, u32[]{:S(2)}) collective-permute-start(bf16[512,384]{1,0:T(8,128)(2,1)S(1)} %bitcast.217), channel_id=1, source_target_pairs={{0,2},{1,3},{2,0},{3,1},{4,6},{5,7},{6,4},{7,5},{8,10},{9,11},{10,... | collective-permute-start | bytes 1179656 | tf_op jit(solution)/shard_map/ppermute | solution.py:19
  116.4 5.1 %collective-permute-start = (bf16[384,512]{1,0:T(8,128)(2,1)}, bf16[384,512]{1,0:T(8,128)(2,1)}, u32[]{:S(2)}, u32[]{:S(2)}) collective-permute-start(bf16[384,512]{1,0:T(8,128)(2,1)} %bitcast.219), channel_id=1, source_target_pairs={{0,1},{1,2},{2,3},{3,0},{4,5},{5,6},{6,7},{7,4},{8,9},{9,10},{10,1... | collective-permute-start | bytes 1179656 | tf_op jit(solution)/shard_map/ppermute | solution.py:19
  129.9 24.3 %collective-permute-done.6 = bf16[512,384]{1,0:T(8,128)(2,1)} collective-permute-done((bf16[512,384]{1,0:T(8,128)(2,1)S(1)}, bf16[512,384]{1,0:T(8,128)(2,1)}, u32[]{:S(2)}, u32[]{:S(2)}) %collective-permute-start.6) | collective-permute-done | bytes 393248 | tf_op jit(solution)/shard_map/ppermute | solution.py:19
  157.9 13.2 %collective-permute-done = bf16[384,512]{1,0:T(8,128)(2,1)} collective-permute-done((bf16[384,512]{1,0:T(8,128)(2,1)}, bf16[384,512]{1,0:T(8,128)(2,1)}, u32[]{:S(2)}, u32[]{:S(2)}) %collective-permute-start) | collective-permute-done | bytes 393248 | tf_op jit(solution)/shard_map/ppermute | solution.py:19
  174.8 3.5 %collective-permute-start.4 = (bf16[512,384]{1,0:T(8,128)(2,1)S(1)}, bf16[512,384]{1,0:T(8,128)(2,1)S(1)}, u32[]{:S(2)}, u32[]{:S(2)}) collective-permute-start(bf16[512,384]{1,0:T(8,128)(2,1)S(1)} %bitcast.223), channel_id=1, source_target_pairs={{0,2},{1,3},{2,0},{3,1},{4,6},{5,7},{6,4},{7,5},{8,10},{9,11},{10,... | collective-permute-start | bytes 1179656 | tf_op jit(solution)/shard_map/ppermute | solution.py:19
  191.1 5.9 %collective-permute-done.5 = bf16[512,384]{1,0:T(8,128)(2,1)S(1)} collective-permute-done((bf16[512,384]{1,0:T(8,128)(2,1)S(1)}, bf16[512,384]{1,0:T(8,128)(2,1)S(1)}, u32[]{:S(2)}, u32[]{:S(2)}) %collective-permute-start.5) | collective-permute-done | bytes 393248 | tf_op jit(solution)/shard_map/ppermute | solution.py:19
  226.7 27.8 %all_to_all.15 = bf16[32,48,512]{2,1,0:T(8,128)(2,1)S(1)} all-to-all(bf16[32,48,512]{2,1,0:T(8,128)(2,1)S(1)} %bitcast.211), channel_id=1, replica_groups=mesh['z'=16,'y'=4,'c'=2,'x'=4] {'x','y','c'}, dimensions={0} | all-to-all | bytes 3145728 | tf_op jit(solution)/shard_map/all_to_all | solution.py:100
  254.5 2.6 convolution_convert_fusion
  257.9 3.7 %collective-permute-start.11 = (bf16[512,384]{1,0:T(8,128)(2,1)S(1)}, bf16[512,384]{1,0:T(8,128)(2,1)S(1)}, u32[]{:S(2)}, u32[]{:S(2)}) collective-permute-start(bf16[512,384]{1,0:T(8,128)(2,1)S(1)} %convolution_convert_fusion.10), channel_id=1, source_target_pairs={{0,2},{1,3},{2,0},{3,1},{4,6},{5,7},{6,4},{7,5},{8,10},{9,11},{10,... | collective-permute-start | bytes 1179656 | tf_op jit(solution)/shard_map/ppermute | solution.py:19
  262.1 3.0 collective-permute-start.10
  265.6 4.3 %collective-permute-start.17 = (bf16[384,512]{1,0:T(8,128)(2,1)S(1)}, bf16[384,512]{1,0:T(8,128)(2,1)S(1)}, u32[]{:S(2)}, u32[]{:S(2)}) collective-permute-start(bf16[384,512]{1,0:T(8,128)(2,1)S(1)} %convolution_convert_fusion.2), channel_id=1, source_target_pairs={{0,2},{1,3},{2,0},{3,1},{4,6},{5,7},{6,4},{7,5},{8,10},{9,11},{10,... | collective-permute-start | bytes 1179656 | tf_op jit(solution)/shard_map/ppermute | solution.py:19
  270.3 2.6 collective-permute-start.16
  273.3 4.4 %collective-permute-start.15 = (bf16[384,512]{1,0:T(8,128)(2,1)S(1)}, bf16[384,512]{1,0:T(8,128)(2,1)S(1)}, u32[]{:S(2)}, u32[]{:S(2)}) collective-permute-start(bf16[384,512]{1,0:T(8,128)(2,1)S(1)} %convolution_convert_fusion.4), channel_id=1, source_target_pairs={{0,1},{1,2},{2,3},{3,0},{4,5},{5,6},{6,7},{7,4},{8,9},{9,10},{10,1... | collective-permute-start | bytes 1179656 | tf_op jit(solution)/shard_map/ppermute | solution.py:19
  281.6 8.6 %collective-permute-done.17 = bf16[384,512]{1,0:T(8,128)(2,1)S(1)} collective-permute-done((bf16[384,512]{1,0:T(8,128)(2,1)S(1)}, bf16[384,512]{1,0:T(8,128)(2,1)S(1)}, u32[]{:S(2)}, u32[]{:S(2)}) %collective-permute-start.17) | collective-permute-done | bytes 393248 | tf_op jit(solution)/shard_map/ppermute | solution.py:19
  290.2 3.8 %collective-permute-start.14 = (bf16[512,384]{1,0:T(8,128)(2,1)S(1)}, bf16[512,384]{1,0:T(8,128)(2,1)S(1)}, u32[]{:S(2)}, u32[]{:S(2)}) collective-permute-start(bf16[512,384]{1,0:T(8,128)(2,1)S(1)} %convolution_convert_fusion.6), channel_id=1, source_target_pairs={{0,2},{1,3},{2,0},{3,1},{4,6},{5,7},{6,4},{7,5},{8,10},{9,11},{10,... | collective-permute-start | bytes 1179656 | tf_op jit(solution)/shard_map/ppermute | solution.py:19
  294.0 4.4 %collective-permute-done.16 = bf16[384,512]{1,0:T(8,128)(2,1)S(1)} collective-permute-done((bf16[384,512]{1,0:T(8,128)(2,1)S(1)}, bf16[384,512]{1,0:T(8,128)(2,1)S(1)}, u32[]{:S(2)}, u32[]{:S(2)}) %collective-permute-start.16) | collective-permute-done | bytes 393248 | tf_op jit(solution)/shard_map/ppermute | solution.py:19
  300.9 4.6 %collective-permute-start.12 = (bf16[512,384]{1,0:T(8,128)(2,1)S(1)}, bf16[512,384]{1,0:T(8,128)(2,1)S(1)}, u32[]{:S(2)}, u32[]{:S(2)}) collective-permute-start(bf16[512,384]{1,0:T(8,128)(2,1)S(1)} %convolution_convert_fusion.8), channel_id=1, source_target_pairs={{0,1},{1,2},{2,3},{3,0},{4,5},{5,6},{6,7},{7,4},{8,9},{9,10},{10,1... | collective-permute-start | bytes 1179656 | tf_op jit(solution)/shard_map/ppermute | solution.py:19
  307.9 7.2 %collective-permute-done.13 = bf16[512,384]{1,0:T(8,128)(2,1)S(1)} collective-permute-done((bf16[512,384]{1,0:T(8,128)(2,1)S(1)}, bf16[512,384]{1,0:T(8,128)(2,1)S(1)}, u32[]{:S(2)}, u32[]{:S(2)}) %collective-permute-start.13) | collective-permute-done | bytes 393248 | tf_op jit(solution)/shard_map/ppermute | solution.py:19
  316.3 8.8 %reduce-scatter.2.cloned.1.call-done = bf16[128,512]{1,0:T(8,128)(2,1)} async-done(((bf16[2048,512]{1,0:T(8,128)(2,1)}), bf16[128,512]{1,0:T(8,128)(2,1)}) %reduce-scatter.2.cloned.1.call-update) | async-done | bytes 131088 | tf_op jit(solution)/shard_map/reduce_scatter | solution.py:104
  (108 shorter events, 79.5 us)
Async XLA Ops:
  7.2 87.2 %all-gather.2.cloned.1.call-start = ((), (), s32[]{:S(2)}) async-start(), calls=%async_computation.4 | async-start | bytes 4456448 | tf_op jit(solution)/shard_map/all_gather | solution.py:66
  11.0 29.9 %all-to-all-start = ((f32[16,16,128]{2,1,0:T(8,128)}), f32[16,16,128]{2,1,0:T(8,128)S(1)}, u32[]{:S(2)}, u32[]{:S(2)}) async-start(f32[16,16,128]{2,1,0:T(8,128)} %broadcast_in_dim.103), calls=%async_computation | async-start | bytes 262144 | tf_op jit(solution)/shard_map/all_to_all | solution.py:33
  41.7 58.3 %copy-start.3 = (pred[4,384,512]{2,1,0:T(32,128)(4,1)}, pred[4,384,512]{2,1,0:T(32,128)(4,1)S(1)}, u32[]{:S(2)}) copy-start(pred[4,384,512]{2,1,0:T(32,128)(4,1)S(1)} %bitcast_compare_fusion) | copy-start | bytes 2359300
  100.0 97.7 %all-to-all-start.1 = ((bf16[32,48,1024]{2,1,0:T(8,128)(2,1)}), bf16[32,48,1024]{2,1,0:T(8,128)(2,1)S(1)}, u32[]{:S(2)}, u32[]{:S(2)}) async-start(bf16[32,48,1024]{2,1,0:T(8,128)(2,1)} %bitcast.213), calls=%async_computation.1 | async-start | bytes 6291456 | tf_op jit(solution)/shard_map/all_to_all | solution.py:77
  107.7 217.4 %reduce-scatter.2.cloned.1.call-start = ((), (), s32[]{:S(2)}) async-start(), calls=%async_computation.5 | async-start | bytes 2228224 | tf_op jit(solution)/shard_map/reduce_scatter | solution.py:104
  107.7 46.5 %collective-permute-start.6 = (bf16[512,384]{1,0:T(8,128)(2,1)S(1)}, bf16[512,384]{1,0:T(8,128)(2,1)}, u32[]{:S(2)}, u32[]{:S(2)}) collective-permute-start(bf16[512,384]{1,0:T(8,128)(2,1)S(1)} %bitcast.216), channel_id=1, source_target_pairs={{0,1},{1,2},{2,3},{3,0},{4,5},{5,6},{6,7},{7,4},{8,9},{9,10},{10,1... | collective-permute-start | bytes 1179656 | tf_op jit(solution)/shard_map/ppermute | solution.py:19
  109.9 65.0 %collective-permute-start.7 = (bf16[512,384]{1,0:T(8,128)(2,1)S(1)}, bf16[512,384]{1,0:T(8,128)(2,1)}, u32[]{:S(2)}, u32[]{:S(2)}) collective-permute-start(bf16[512,384]{1,0:T(8,128)(2,1)S(1)} %bitcast.217), channel_id=1, source_target_pairs={{0,2},{1,3},{2,0},{3,1},{4,6},{5,7},{6,4},{7,5},{8,10},{9,11},{10,... | collective-permute-start | bytes 1179656 | tf_op jit(solution)/shard_map/ppermute | solution.py:19
  114.5 69.7 %collective-permute-start.8 = (bf16[512,384]{1,0:T(8,128)(2,1)S(1)}, bf16[512,384]{1,0:T(8,128)(2,1)}, u32[]{:S(2)}, u32[]{:S(2)}) collective-permute-start(bf16[512,384]{1,0:T(8,128)(2,1)S(1)} %bitcast.218), channel_id=1, source_target_pairs={{0,3},{1,0},{2,1},{3,2},{4,7},{5,4},{6,5},{7,6},{8,11},{9,8},{10,9... | collective-permute-start | bytes 1179656 | tf_op jit(solution)/shard_map/ppermute | solution.py:19
  116.4 54.7 %collective-permute-start = (bf16[384,512]{1,0:T(8,128)(2,1)}, bf16[384,512]{1,0:T(8,128)(2,1)}, u32[]{:S(2)}, u32[]{:S(2)}) collective-permute-start(bf16[384,512]{1,0:T(8,128)(2,1)} %bitcast.219), channel_id=1, source_target_pairs={{0,1},{1,2},{2,3},{3,0},{4,5},{5,6},{6,7},{7,4},{8,9},{9,10},{10,1... | collective-permute-start | bytes 1179656 | tf_op jit(solution)/shard_map/ppermute | solution.py:19
  121.5 58.6 %collective-permute-start.1 = (bf16[384,512]{1,0:T(8,128)(2,1)}, bf16[384,512]{1,0:T(8,128)(2,1)}, u32[]{:S(2)}, u32[]{:S(2)}) collective-permute-start(bf16[384,512]{1,0:T(8,128)(2,1)} %bitcast.220), channel_id=1, source_target_pairs={{0,2},{1,3},{2,0},{3,1},{4,6},{5,7},{6,4},{7,5},{8,10},{9,11},{10,... | collective-permute-start | bytes 1179656 | tf_op jit(solution)/shard_map/ppermute | solution.py:19
  154.2 31.8 %collective-permute-start.2 = (bf16[384,512]{1,0:T(8,128)(2,1)S(1)}, bf16[384,512]{1,0:T(8,128)(2,1)S(1)}, u32[]{:S(2)}, u32[]{:S(2)}) collective-permute-start(bf16[384,512]{1,0:T(8,128)(2,1)S(1)} %bitcast.221), channel_id=1, source_target_pairs={{0,3},{1,0},{2,1},{3,2},{4,7},{5,4},{6,5},{7,6},{8,11},{9,8},{10,9... | collective-permute-start | bytes 1179656 | tf_op jit(solution)/shard_map/ppermute | solution.py:19
  171.1 16.8 %collective-permute-start.3 = (bf16[512,384]{1,0:T(8,128)(2,1)S(1)}, bf16[512,384]{1,0:T(8,128)(2,1)S(1)}, u32[]{:S(2)}, u32[]{:S(2)}) collective-permute-start(bf16[512,384]{1,0:T(8,128)(2,1)S(1)} %bitcast.222), channel_id=1, source_target_pairs={{0,1},{1,2},{2,3},{3,0},{4,5},{5,6},{6,7},{7,4},{8,9},{9,10},{10,1... | collective-permute-start | bytes 1179656 | tf_op jit(solution)/shard_map/ppermute | solution.py:19
  174.8 15.5 %collective-permute-start.4 = (bf16[512,384]{1,0:T(8,128)(2,1)S(1)}, bf16[512,384]{1,0:T(8,128)(2,1)S(1)}, u32[]{:S(2)}, u32[]{:S(2)}) collective-permute-start(bf16[512,384]{1,0:T(8,128)(2,1)S(1)} %bitcast.223), channel_id=1, source_target_pairs={{0,2},{1,3},{2,0},{3,1},{4,6},{5,7},{6,4},{7,5},{8,10},{9,11},{10,... | collective-permute-start | bytes 1179656 | tf_op jit(solution)/shard_map/ppermute | solution.py:19
  180.1 16.9 %collective-permute-start.5 = (bf16[512,384]{1,0:T(8,128)(2,1)S(1)}, bf16[512,384]{1,0:T(8,128)(2,1)S(1)}, u32[]{:S(2)}, u32[]{:S(2)}) collective-permute-start(bf16[512,384]{1,0:T(8,128)(2,1)S(1)} %bitcast.224), channel_id=1, source_target_pairs={{0,3},{1,0},{2,1},{3,2},{4,7},{5,4},{6,5},{7,6},{8,11},{9,8},{10,9... | collective-permute-start | bytes 1179656 | tf_op jit(solution)/shard_map/ppermute | solution.py:19
  226.7 27.8 %copy-start.4 = (pred[4,384,512]{2,1,0:T(32,128)(4,1)S(1)}, pred[4,384,512]{2,1,0:T(32,128)(4,1)}, u32[]{:S(2)}) copy-start(pred[4,384,512]{2,1,0:T(32,128)(4,1)} %copy-done.3) | copy-start | bytes 2359300
  257.9 21.2 %collective-permute-start.11 = (bf16[512,384]{1,0:T(8,128)(2,1)S(1)}, bf16[512,384]{1,0:T(8,128)(2,1)S(1)}, u32[]{:S(2)}, u32[]{:S(2)}) collective-permute-start(bf16[512,384]{1,0:T(8,128)(2,1)S(1)} %convolution_convert_fusion.10), channel_id=1, source_target_pairs={{0,2},{1,3},{2,0},{3,1},{4,6},{5,7},{6,4},{7,5},{8,10},{9,11},{10,... | collective-permute-start | bytes 1179656 | tf_op jit(solution)/shard_map/ppermute | solution.py:19
  262.1 44.5 %collective-permute-start.10 = (bf16[512,384]{1,0:T(8,128)(2,1)S(1)}, bf16[512,384]{1,0:T(8,128)(2,1)S(1)}, u32[]{:S(2)}, u32[]{:S(2)}) collective-permute-start(bf16[512,384]{1,0:T(8,128)(2,1)S(1)} %convolution_convert_fusion.11), channel_id=1, source_target_pairs={{0,3},{1,0},{2,1},{3,2},{4,7},{5,4},{6,5},{7,6},{8,11},{9,8},{10,9... | collective-permute-start | bytes 1179656 | tf_op jit(solution)/shard_map/ppermute | solution.py:19
  265.6 24.6 %collective-permute-start.17 = (bf16[384,512]{1,0:T(8,128)(2,1)S(1)}, bf16[384,512]{1,0:T(8,128)(2,1)S(1)}, u32[]{:S(2)}, u32[]{:S(2)}) collective-permute-start(bf16[384,512]{1,0:T(8,128)(2,1)S(1)} %convolution_convert_fusion.2), channel_id=1, source_target_pairs={{0,2},{1,3},{2,0},{3,1},{4,6},{5,7},{6,4},{7,5},{8,10},{9,11},{10,... | collective-permute-start | bytes 1179656 | tf_op jit(solution)/shard_map/ppermute | solution.py:19
  270.3 28.1 %collective-permute-start.16 = (bf16[384,512]{1,0:T(8,128)(2,1)S(1)}, bf16[384,512]{1,0:T(8,128)(2,1)S(1)}, u32[]{:S(2)}, u32[]{:S(2)}) collective-permute-start(bf16[384,512]{1,0:T(8,128)(2,1)S(1)} %convolution_convert_fusion.3), channel_id=1, source_target_pairs={{0,3},{1,0},{2,1},{3,2},{4,7},{5,4},{6,5},{7,6},{8,11},{9,8},{10,9... | collective-permute-start | bytes 1179656 | tf_op jit(solution)/shard_map/ppermute | solution.py:19
  273.3 27.6 %collective-permute-start.15 = (bf16[384,512]{1,0:T(8,128)(2,1)S(1)}, bf16[384,512]{1,0:T(8,128)(2,1)S(1)}, u32[]{:S(2)}, u32[]{:S(2)}) collective-permute-start(bf16[384,512]{1,0:T(8,128)(2,1)S(1)} %convolution_convert_fusion.4), channel_id=1, source_target_pairs={{0,1},{1,2},{2,3},{3,0},{4,5},{5,6},{6,7},{7,4},{8,9},{9,10},{10,1... | collective-permute-start | bytes 1179656 | tf_op jit(solution)/shard_map/ppermute | solution.py:19
  279.2 27.5 %collective-permute-start.9 = (bf16[512,384]{1,0:T(8,128)(2,1)S(1)}, bf16[512,384]{1,0:T(8,128)(2,1)S(1)}, u32[]{:S(2)}, u32[]{:S(2)}) collective-permute-start(bf16[512,384]{1,0:T(8,128)(2,1)S(1)} %convolution_convert_fusion.12), channel_id=1, source_target_pairs={{0,1},{1,2},{2,3},{3,0},{4,5},{5,6},{6,7},{7,4},{8,9},{9,10},{10,1... | collective-permute-start | bytes 1179656 | tf_op jit(solution)/shard_map/ppermute | solution.py:19
  290.2 17.7 %collective-permute-start.14 = (bf16[512,384]{1,0:T(8,128)(2,1)S(1)}, bf16[512,384]{1,0:T(8,128)(2,1)S(1)}, u32[]{:S(2)}, u32[]{:S(2)}) collective-permute-start(bf16[512,384]{1,0:T(8,128)(2,1)S(1)} %convolution_convert_fusion.6), channel_id=1, source_target_pairs={{0,2},{1,3},{2,0},{3,1},{4,6},{5,7},{6,4},{7,5},{8,10},{9,11},{10,... | collective-permute-start | bytes 1179656 | tf_op jit(solution)/shard_map/ppermute | solution.py:19
  298.4 16.6 %collective-permute-start.13 = (bf16[512,384]{1,0:T(8,128)(2,1)S(1)}, bf16[512,384]{1,0:T(8,128)(2,1)S(1)}, u32[]{:S(2)}, u32[]{:S(2)}) collective-permute-start(bf16[512,384]{1,0:T(8,128)(2,1)S(1)} %convolution_convert_fusion.7), channel_id=1, source_target_pairs={{0,3},{1,0},{2,1},{3,2},{4,7},{5,4},{6,5},{7,6},{8,11},{9,8},{10,9... | collective-permute-start | bytes 1179656 | tf_op jit(solution)/shard_map/ppermute | solution.py:19
  300.9 14.1 %collective-permute-start.12 = (bf16[512,384]{1,0:T(8,128)(2,1)S(1)}, bf16[512,384]{1,0:T(8,128)(2,1)S(1)}, u32[]{:S(2)}, u32[]{:S(2)}) collective-permute-start(bf16[512,384]{1,0:T(8,128)(2,1)S(1)} %convolution_convert_fusion.8), channel_id=1, source_target_pairs={{0,1},{1,2},{2,3},{3,0},{4,5},{5,6},{6,7},{7,4},{8,9},{9,10},{10,1... | collective-permute-start | bytes 1179656 | tf_op jit(solution)/shard_map/ppermute | solution.py:19
  (7 other events, 62.3 us)
Sparse Core Ops, SparseCore 0:
  10.7 83.7 all-gather.1
  257.3 67.7 reduce-scatter.1

commit v2 on v1

v2 whole, which is shorter than its diff:
```python
import jax
import jax.numpy as jnp
from jax import lax
from jax.experimental import pallas as pl
from jax.experimental.pallas import tpu as pltpu
from jax.sharding import Mesh
from jax.sharding import PartitionSpec as P

MOST = 12
N_FAR, N_NEAR, N_Y, N_C, N_X = 8, 2, 4, 2, 4
PLANE = ("x", "near", "y", "c")
LOCAL = N_NEAR * N_Y * N_C
GROUP = N_FAR // N_X
F32 = jnp.float32
BF16 = jnp.bfloat16


def dot(left, right, contract, batch=((), ())):
    return lax.dot_general(left, right, (contract, batch), preferred_element_type=F32)


def shift(value, by):
    return lax.ppermute(value, "x", [(i, (i + by) % N_X) for i in range(N_X)])


def gather_x(value, me):
    whole = jnp.zeros((N_X,) + value.shape, value.dtype)
    for by in range(N_X):
        piece = value if by == 0 else shift(value, by)
        whole = lax.dynamic_update_slice_in_dim(whole, piece[None], (me - by) % N_X, 0)
    return whole


def plan(routes, gates, me_far):
    tok, top = routes.shape
    mine = jnp.concatenate([routes.T.astype(F32), gates.T], axis=0)
    every = lax.all_to_all(
        jnp.broadcast_to(mine[None], (N_FAR,) + mine.shape), "far", split_axis=0, concat_axis=0, tiled=True
    )
    named = every[:, :top].reshape(N_FAR, top, 1, tok)
    weight = every[:, top:].reshape(N_FAR, top, 1, tok)
    wanted = (me_far * LOCAL + jnp.arange(LOCAL, dtype=jnp.int32)).astype(F32)
    hit = named == wanted[None, None, :, None]
    member = jnp.sum(hit.astype(F32), axis=1)
    gate = jnp.sum(jnp.where(hit, weight, 0.0), axis=1)
    before = (jnp.arange(tok)[:, None] < jnp.arange(tok)[None, :]).astype(BF16)
    rank = dot(member.astype(BF16), before, ((2,), (0,)))
    within = (jnp.arange(N_FAR) % GROUP * MOST).astype(F32)
    slot = jnp.where(member > 0.5, rank + within[:, None, None], -1.0)

    def by_group(value):
        value = value.reshape(N_X, GROUP, LOCAL, tok)
        return value.transpose(0, 2, 1, 3).reshape(N_X, LOCAL, 1, GROUP * tok)

    slots = GROUP * MOST
    pick = by_group(slot) == jnp.arange(slots, dtype=jnp.int32).astype(F32)[None, None, :, None]
    row_gate = jnp.sum(jnp.where(pick, by_group(gate), 0.0), axis=3)
    return (
        pick.astype(BF16).reshape(N_X, LOCAL * slots, GROUP * tok),
        row_gate.reshape(N_X, LOCAL * slots, 1),
    )


def expert_kernel(rows, both_in, down, row_grad, hidden, d_gate, d_up, pre_gate, pre_up, back):
    step = pl.program_id(0)
    width, cols = down.shape[1:]

    @pl.when(step == 0)
    def _():
        pre_gate[...] = jnp.zeros_like(pre_gate)
        pre_up[...] = jnp.zeros_like(pre_up)
        back[...] = jnp.zeros_like(back)

    ins = rows[0, :, :cols]
    pre_gate[...] += dot(ins, both_in[step, :, :width], ((1,), (0,)))
    pre_up[...] += dot(ins, both_in[step, :, width:], ((1,), (0,)))
    back[...] += dot(rows[0, :, cols:], down[0], ((1,), (1,)))

    @pl.when(step == N_X - 1)
    def _():
        g, u, b = pre_gate[...], pre_up[...], back[...]
        s = jax.nn.sigmoid(g)
        activated = g * s
        hidden[...] = (activated * u).astype(BF16)
        du = (b * activated).astype(BF16)
        dg = (b * u * s * (1.0 + g * (1.0 - s))).astype(BF16)
        d_up[...] = du
        d_gate[...] = dg
        for j in range(N_X):
            from_gate = dot(dg, both_in[j, :, :width], ((1,), (1,)))
            from_up = dot(du, both_in[j, :, width:], ((1,), (1,)))
            row_grad[j] = (from_gate + from_up).astype(BF16)


def expert(rows, both_in, down):
    parts, count, both = rows.shape
    width, cols = down.shape[1:]
    whole = lambda shape: pl.BlockSpec(shape, lambda j: (0,) * len(shape))
    square = jax.ShapeDtypeStruct((count, width), BF16)
    return pl.pallas_call(
        expert_kernel,
        grid=(parts,),
        in_specs=[
            pl.BlockSpec((1, count, both), lambda j: (j, 0, 0)),
            whole(both_in.shape),
            pl.BlockSpec((1, width, cols), lambda j: (j, 0, 0)),
        ],
        out_specs=[whole((parts, count, cols)), *[whole((count, width))] * 3],
        out_shape=[jax.ShapeDtypeStruct((parts, count, cols), BF16), square, square, square],
        scratch_shapes=[pltpu.VMEM((count, width), F32)] * 3,
        compiler_params=pltpu.CompilerParams(
            dimension_semantics=("arbitrary",), vmem_limit_bytes=32 * 1024 * 1024
        ),
        cost_estimate=pl.CostEstimate(
            flops=10 * parts * count * cols * width, bytes_accessed=11_000_000, transcendentals=count * width
        ),
    )(rows, both_in, down)


def shards(tokens, grad_out, routes, gates, w_gate, w_up, w_down):
    me_far, me_x = lax.axis_index("far"), lax.axis_index("x")
    tok, cols = tokens.shape
    both = jnp.concatenate([tokens, grad_out], axis=1)
    w_in = jnp.concatenate([w_gate[0], w_up[0]], axis=1)
    both, w_in, w_down = lax.optimization_barrier((both, w_in, w_down[0]))
    column = lax.all_gather(both, "far", axis=0, tiled=True).reshape(N_X, GROUP * tok, 2 * cols)
    pick, row_gate = plan(routes, gates, me_far)
    full_in = gather_x(w_in, me_x)
    full_down = gather_x(w_down, me_x)
    column, full_in, full_down = lax.optimization_barrier((column, full_in, full_down))

    rows = dot(pick, column, ((2,), (1,)), ((0,), (0,)))
    scale = jnp.where(jnp.arange(2 * cols)[None, None, :] < cols, 1.0, row_gate)
    rows = (rows * scale).astype(BF16)
    count = rows.shape[1]
    slots = count // LOCAL
    rows = lax.all_to_all(
        rows.reshape(-1, slots, 2 * cols), PLANE, split_axis=0, concat_axis=0, tiled=True
    ).reshape(N_X, count, 2 * cols)
    inputs, scaled = rows[:, :, :cols], rows[:, :, cols:]
    row_grad, hidden, d_gate, d_up = expert(rows, full_in, full_down)
    came_back = lax.all_to_all(
        row_grad.reshape(-1, slots, cols), PLANE, split_axis=0, concat_axis=0, tiled=True
    ).reshape(N_X, count, cols)
    token_grad = dot(pick, came_back, ((1,), (1,)), ((0,), (0,))).astype(BF16)
    d_tokens = lax.psum_scatter(token_grad.reshape(-1, cols), "far", scatter_dimension=0, tiled=True)

    totals = [None, None, None]
    for by in (1, 3, 2, 0):
        to = (me_x + by) % N_X
        ins = lax.dynamic_index_in_dim(inputs, to, 0, keepdims=False)
        outs = lax.dynamic_index_in_dim(scaled, to, 0, keepdims=False)
        for k, (left, right) in enumerate(((ins, d_gate), (ins, d_up), (hidden, outs))):
            part = dot(left, right, ((0,), (0,))).astype(BF16)
            part = (shift(part, by) if by else part).astype(F32)
            totals[k] = part if totals[k] is None else totals[k] + part
    grads = [total.astype(BF16)[None] for total in totals]
    return (d_tokens, *grads)


def solution(mesh):
    sizes = (N_FAR, N_NEAR, N_Y, N_C, N_X)
    fine = Mesh(mesh.devices.reshape(sizes), ("far", "near", "y", "c", "x"))
    expert_axes = ("far", "near", "y", "c")
    return jax.shard_map(
        shards,
        mesh=fine,
        in_specs=(
            P(expert_axes, "x"),
            P(expert_axes, "x"),
            P(expert_axes, None),
            P(expert_axes, None),
            P(expert_axes, "x", None),
            P(expert_axes, "x", None),
            P(expert_axes, None, "x"),
        ),
        out_specs=(
            P(expert_axes, "x"),
            P(expert_axes, "x", None),
            P(expert_axes, "x", None),
            P(expert_axes, None, "x"),
        ),
        check_vma=False,
    )
```

time: 334 us -> 237 us (0.71)
  waiting for transfers between devices: 142 us -> 51.6 us
  matrix products: 44.4 us -> 15 us
  blocking collectives: 27.8 us -> 49.1 us
  Pallas kernels: 0 us -> 6.4 us
  starting transfers between devices: 79.2 us -> 74.3 us
    all_gather x1, waiting for transfers between devices: 52.1 us -> 2.51 us  [shards(): lax.all_gather(both, 'far', axis=0, tiled=True)]
    ppermute x18 -> x15, waiting for transfers between devices: 66.3 us -> 21 us  [shift(): return lax.ppermute(value, 'x', [(i, (i + by) % N_X) for i in range(N_X)])]
    dot_general x35 -> x15, matrix products: 44.4 us -> 15 us  [dot(): lax.dot_general(left, right, (contract, batch), preferred_element_type=F32)]
    all_to_all x1, blocking collectives: 27.8 us -> 49.1 us  [shards(): lax.all_to_all(rows.reshape(-1, slots, 2 * cols), PLANE, split_axis=0, co...]
    all_to_all x2, waiting for transfers between devices: 14.6 us -> 22.6 us  [the longest x1 12.3 us: shards(): lax.all_to_all(row_grad.reshape(-1, slots, cols), PLANE, split_axis=0, co...]
    pallas_call x0 -> x1, Pallas kernels: none -> 6.4 us  [expert(): pl.pallas_call(expert_kernel, grid=(parts,), in_specs=[pl.BlockSpec((1, c...]
    all_to_all x2, starting transfers between devices: 22.8 us -> 17.2 us  [the longest x1 9.86 us: plan(): lax.all_to_all(jnp.broadcast_to(mine[None], (N_FAR,) + mine.shape), 'far'...]
    dynamic_update_slice x12 -> x8, local copies, waits for them, and re-layouts: 14.5 us -> 10.9 us  [gather_x(): lax.dynamic_update_slice_in_dim(whole, piece[None], (me - by) % N_X, 0)]
  transfers between devices with their start and end apart: 22 -> 19, of which waited for: 11 -> 9; matrix products, arithmetic and copies ran while one was open for 9% -> 13% of each run, Pallas kernels for 0% -> 0%
where the time goes in v2:
time: 237 us; the launch traced here: 236 us
  starting transfers between devices  74.3 us (31%)
  waiting for transfers between devices  51.6 us (22%)
  blocking collectives  49.1 us (21%)
  local copies, waits for them, and re-layouts  18.8 us (8%)
  matrix products  15 us (6%)
  between operations  14.6 us (6%)
  Pallas kernels  6.4 us (3%)
  other arithmetic  6.05 us (3%)
    ppermute x15, starting transfers between devices, shift(): return lax.ppermute(value, 'x', [(i, (i + by) % N_X) for i in range(N_X)])  57 us
    all_to_all x1, blocking collectives, shards(): lax.all_to_all(rows.reshape(-1, slots, 2 * cols), PLANE, split_axis=0, co...  49.1 us
    ppermute x15, waiting for transfers between devices, shift(): return lax.ppermute(value, 'x', [(i, (i + by) % N_X) for i in range(N_X)])  21 us
    dot_general x15, matrix products, dot(): lax.dot_general(left, right, (contract, batch), preferred_element_type=F32)  15 us
    all_to_all x1, waiting for transfers between devices, shards(): lax.all_to_all(row_grad.reshape(-1, slots, cols), PLANE, split_axis=0, co...  12.3 us
    dynamic_update_slice x8, local copies, waits for them, and re-layouts, gather_x(): lax.dynamic_update_slice_in_dim(whole, piece[None], (me - by) % N_X, 0)  10.9 us
    all_to_all x1, waiting for transfers between devices, plan(): lax.all_to_all(jnp.broadcast_to(mine[None], (N_FAR,) + mine.shape), 'far'...  10.3 us
    all_to_all x1, starting transfers between devices, plan(): lax.all_to_all(jnp.broadcast_to(mine[None], (N_FAR,) + mine.shape), 'far'...  9.86 us
  transfers between devices with their start and end apart: 19, of which 9 were waited for; matrix products, arithmetic and copies ran while one was open for 13% of the time, Pallas kernels for 0%

profile of v2, /device:TPU:6, one launch (start us, length us, event | category | flops | bytes accessed | tf_op | source)
XLA Modules:
  0.0 236.0 jit_solution(3778956583835058799)
XLA Ops:
  11.0 7.8 %collective-permute-start = (bf16[512,768]{1,0:T(8,128)(2,1)}, bf16[512,768]{1,0:T(8,128)(2,1)}, u32[]{:S(2)}, u32[]{:S(2)}) collective-permute-start(bf16[512,768]{1,0:T(8,128)(2,1)} %pad_maximum_fusion), channel_id=1, source_target_pairs={{0,1},{1,2},{2,3},{3,0},{4,5},{5,6},{6,7},{7,4},{8,9},{9,10},{10,1... | collective-permute-start | bytes 2359304 | tf_op jit(solution)/shard_map/ppermute | solution.py:23
  20.7 2.8 %collective-permute-start.2 = (bf16[512,768]{1,0:T(8,128)(2,1)}, bf16[512,768]{1,0:T(8,128)(2,1)}, u32[]{:S(2)}, u32[]{:S(2)}) collective-permute-start(bf16[512,768]{1,0:T(8,128)(2,1)} %pad_maximum_fusion), channel_id=1, source_target_pairs={{0,3},{1,0},{2,1},{3,2},{4,7},{5,4},{6,5},{7,6},{8,11},{9,8},{10,9... | collective-permute-start | bytes 2359304 | tf_op jit(solution)/shard_map/ppermute | solution.py:23
  23.5 4.3 %collective-permute-start.3 = (bf16[384,512]{1,0:T(8,128)(2,1)}, bf16[384,512]{1,0:T(8,128)(2,1)}, u32[]{:S(2)}, u32[]{:S(2)}) collective-permute-start(bf16[384,512]{1,0:T(8,128)(2,1)} %bitcast.8), channel_id=1, source_target_pairs={{0,1},{1,2},{2,3},{3,0},{4,5},{5,6},{6,7},{7,4},{8,9},{9,10},{10,1... | collective-permute-start | bytes 1179656 | tf_op jit(solution)/shard_map/ppermute | solution.py:23
  27.8 4.2 %collective-permute-start.4 = (bf16[384,512]{1,0:T(8,128)(2,1)}, bf16[384,512]{1,0:T(8,128)(2,1)}, u32[]{:S(2)}, u32[]{:S(2)}) collective-permute-start(bf16[384,512]{1,0:T(8,128)(2,1)} %bitcast.8), channel_id=1, source_target_pairs={{0,2},{1,3},{2,0},{3,1},{4,6},{5,7},{6,4},{7,5},{8,10},{9,11},{10,... | collective-permute-start | bytes 1179656 | tf_op jit(solution)/shard_map/ppermute | solution.py:23
  32.7 9.9 %all-to-all-start = ((f32[8,16,128]{2,1,0:T(8,128)}), f32[8,16,128]{2,1,0:T(8,128)S(1)}, u32[]{:S(2)}, u32[]{:S(2)}) async-start(f32[8,16,128]{2,1,0:T(8,128)} %broadcast_in_dim.103), calls=%async_computation | async-start | bytes 131072 | tf_op jit(solution)/shard_map/all_to_all | solution.py:37
  47.2 10.3 %all-to-all-done = f32[8,16,128]{2,1,0:T(8,128)S(1)} async-done(((f32[8,16,128]{2,1,0:T(8,128)}), f32[8,16,128]{2,1,0:T(8,128)S(1)}, u32[]{:S(2)}, u32[]{:S(2)}) %all-to-all-start) | async-done | bytes 65568 | tf_op jit(solution)/shard_map/all_to_all | solution.py:37
  61.6 3.2 %collective-permute-start.5 = (bf16[384,512]{1,0:T(8,128)(2,1)}, bf16[384,512]{1,0:T(8,128)(2,1)S(1)}, u32[]{:S(2)}, u32[]{:S(2)}) collective-permute-start(bf16[384,512]{1,0:T(8,128)(2,1)} %bitcast.8), channel_id=1, source_target_pairs={{0,3},{1,0},{2,1},{3,2},{4,7},{5,4},{6,5},{7,6},{8,11},{9,8},{10,9... | collective-permute-start | bytes 1179656 | tf_op jit(solution)/shard_map/ppermute | solution.py:23
  68.3 5.9 %collective-permute-done.5 = bf16[384,512]{1,0:T(8,128)(2,1)S(1)} collective-permute-done((bf16[384,512]{1,0:T(8,128)(2,1)}, bf16[384,512]{1,0:T(8,128)(2,1)S(1)}, u32[]{:S(2)}, u32[]{:S(2)}) %collective-permute-start.5) | collective-permute-done | bytes 393248 | tf_op jit(solution)/shard_map/ppermute | solution.py:23
  81.2 2.6 %multiply_convert_fusion = bf16[4,384,1024]{2,1,0:T(8,128)(2,1)S(1)} fusion(f32[4,384]{1,0:T(4,128)S(1)} %broadcast_in_dim.122, pred[1024]{0:T(1024)(128)(4,1)S(1)} %iota_compare_fusion.1, pred[4,384,256]{2,1,0:T(32,128)(4,1)S(1)} %bitcast_compare_fusion, bf16[4,256,1024]{2,1,0:T(8,128)(2,1)} %bitcast.116), kind=kOutput, calls=%fused_computation | convolution fusion | flops 810024960 | bytes 5643264 | tf_op jit(solution)/shard_map/dot_general | solution.py:19
  83.8 49.1 %all_to_all.15 = bf16[64,24,1024]{2,1,0:T(8,128)(2,1)S(1)} all-to-all(bf16[64,24,1024]{2,1,0:T(8,128)(2,1)S(1)} %bitcast.108), channel_id=1, replica_groups=mesh['far'=8,'near'=2,'y'=4,'c'=2,'x'=4] {'x','near','y','c'}, dimensions={0} | all-to-all | bytes 6291456 | tf_op jit(solution)/shard_map/all_to_all | solution.py:137
  133.0 6.4 %shard_map.102 = (bf16[4,384,512]{2,1,0:T(8,128)(2,1)S(1)}, bf16[384,384]{1,0:T(8,128)(2,1)S(1)}, bf16[384,384]{1,0:T(8,128)(2,1)S(1)}, bf16[384,384]{1,0:T(8,128)(2,1)S(1)}) custom-call(bf16[4,384,1024]{2,1,0:T(8,128)(2,1)S(1)} %bitcast.104, bf16[4,512,768]{2,1,0:T(8,128)(2,1)S(1)} %copy-done.6, bf16[4,384,512]{2,1,0:T(8,128)(2,1)} %bitcast_dynamic-update-slice_fusion.4.down), custom_call_target="tpu_custom_call" | custom-call | flops 3019898880 | bytes 11000000 | tf_op jit(solution)/shard_map/pallas_call | solution.py:100
  142.0 7.4 %all-to-all-start.2 = ((bf16[64,24,512]{2,1,0:T(8,128)(2,1)}), bf16[64,24,512]{2,1,0:T(8,128)(2,1)}, u32[]{:S(2)}, u32[]{:S(2)}) async-start(bf16[64,24,512]{2,1,0:T(8,128)(2,1)} %bitcast.106), calls=%async_computation.2 | async-start | bytes 3145728 | tf_op jit(solution)/shard_map/all_to_all | solution.py:142
  152.1 3.1 %collective-permute-start.8 = (bf16[512,384]{1,0:T(8,128)(2,1)}, bf16[512,384]{1,0:T(8,128)(2,1)S(1)}, u32[]{:S(2)}, u32[]{:S(2)}) collective-permute-start(bf16[512,384]{1,0:T(8,128)(2,1)} %convolution_convert_fusion.10), channel_id=1, source_target_pairs={{0,2},{1,3},{2,0},{3,1},{4,6},{5,7},{6,4},{7,5},{8,10},{9,11},{10,... | collective-permute-start | bytes 1179656 | tf_op jit(solution)/shard_map/ppermute | solution.py:23
  158.4 12.3 %all-to-all-done.2 = bf16[64,24,512]{2,1,0:T(8,128)(2,1)} async-done(((bf16[64,24,512]{2,1,0:T(8,128)(2,1)}), bf16[64,24,512]{2,1,0:T(8,128)(2,1)}, u32[]{:S(2)}, u32[]{:S(2)}) %all-to-all-start.2) | async-done | bytes 1572896 | tf_op jit(solution)/shard_map/all_to_all | solution.py:142
  170.7 3.3 %convolution_convert_fusion = bf16[4,256,512]{2,1,0:T(8,128)(2,1)} fusion(pred[4,384,256]{2,1,0:T(32,128)(4,1)S(1)} %copy-done.12, bf16[4,384,512]{2,1,0:T(8,128)(2,1)} %bitcast.23), kind=kOutput, calls=%fused_computation.3 | convolution fusion | flops 403177472 | bytes 3014656 | tf_op jit(solution)/shard_map/dot_general | solution.py:19
  174.5 7.5 %collective-permute-start.14 = (bf16[384,512]{1,0:T(8,128)(2,1)S(1)}, bf16[384,512]{1,0:T(8,128)(2,1)S(1)}, u32[]{:S(2)}, u32[]{:S(2)}) collective-permute-start(bf16[384,512]{1,0:T(8,128)(2,1)S(1)} %convolution_convert_fusion.2), channel_id=1, source_target_pairs={{0,2},{1,3},{2,0},{3,1},{4,6},{5,7},{6,4},{7,5},{8,10},{9,11},{10,... | collective-permute-start | bytes 1179656 | tf_op jit(solution)/shard_map/ppermute | solution.py:23
  184.7 5.3 %collective-permute-start.12 = (bf16[384,512]{1,0:T(8,128)(2,1)S(1)}, bf16[384,512]{1,0:T(8,128)(2,1)S(1)}, u32[]{:S(2)}, u32[]{:S(2)}) collective-permute-start(bf16[384,512]{1,0:T(8,128)(2,1)S(1)} %convolution_convert_fusion.4), channel_id=1, source_target_pairs={{0,1},{1,2},{2,3},{3,0},{4,5},{5,6},{6,7},{7,4},{8,9},{9,10},{10,1... | collective-permute-start | bytes 1179656 | tf_op jit(solution)/shard_map/ppermute | solution.py:23
  194.0 4.2 %collective-permute-start.11 = (bf16[512,384]{1,0:T(8,128)(2,1)S(1)}, bf16[512,384]{1,0:T(8,128)(2,1)S(1)}, u32[]{:S(2)}, u32[]{:S(2)}) collective-permute-start(bf16[512,384]{1,0:T(8,128)(2,1)S(1)} %convolution_convert_fusion.6), channel_id=1, source_target_pairs={{0,2},{1,3},{2,0},{3,1},{4,6},{5,7},{6,4},{7,5},{8,10},{9,11},{10,... | collective-permute-start | bytes 1179656 | tf_op jit(solution)/shard_map/ppermute | solution.py:23
  198.2 3.7 %collective-permute-done.13 = bf16[384,512]{1,0:T(8,128)(2,1)S(1)} collective-permute-done((bf16[384,512]{1,0:T(8,128)(2,1)S(1)}, bf16[384,512]{1,0:T(8,128)(2,1)S(1)}, u32[]{:S(2)}, u32[]{:S(2)}) %collective-permute-start.13) | collective-permute-done | bytes 393248 | tf_op jit(solution)/shard_map/ppermute | solution.py:23
  201.8 3.3 %collective-permute-start.10 = (bf16[512,384]{1,0:T(8,128)(2,1)S(1)}, bf16[512,384]{1,0:T(8,128)(2,1)S(1)}, u32[]{:S(2)}, u32[]{:S(2)}) collective-permute-start(bf16[512,384]{1,0:T(8,128)(2,1)S(1)} %convolution_convert_fusion.7), channel_id=1, source_target_pairs={{0,3},{1,0},{2,1},{3,2},{4,7},{5,4},{6,5},{7,6},{8,11},{9,8},{10,9... | collective-permute-start | bytes 1179656 | tf_op jit(solution)/shard_map/ppermute | solution.py:23
  205.1 3.8 %collective-permute-start.9 = (bf16[512,384]{1,0:T(8,128)(2,1)S(1)}, bf16[512,384]{1,0:T(8,128)(2,1)S(1)}, u32[]{:S(2)}, u32[]{:S(2)}) collective-permute-start(bf16[512,384]{1,0:T(8,128)(2,1)S(1)} %convolution_convert_fusion.8), channel_id=1, source_target_pairs={{0,1},{1,2},{2,3},{3,0},{4,5},{5,6},{6,7},{7,4},{8,9},{9,10},{10,1... | collective-permute-start | bytes 1179656 | tf_op jit(solution)/shard_map/ppermute | solution.py:23
  211.3 7.5 %collective-permute-done.10 = bf16[512,384]{1,0:T(8,128)(2,1)S(1)} collective-permute-done((bf16[512,384]{1,0:T(8,128)(2,1)S(1)}, bf16[512,384]{1,0:T(8,128)(2,1)S(1)}, u32[]{:S(2)}, u32[]{:S(2)}) %collective-permute-start.10) | collective-permute-done | bytes 393248 | tf_op jit(solution)/shard_map/ppermute | solution.py:23
  218.8 3.7 %collective-permute-done.9 = bf16[512,384]{1,0:T(8,128)(2,1)S(1)} collective-permute-done((bf16[512,384]{1,0:T(8,128)(2,1)S(1)}, bf16[512,384]{1,0:T(8,128)(2,1)S(1)}, u32[]{:S(2)}, u32[]{:S(2)}) %collective-permute-start.9) | collective-permute-done | bytes 393248 | tf_op jit(solution)/shard_map/ppermute | solution.py:23
  223.7 5.4 %reduce-scatter.2.cloned.1.call-done = bf16[128,512]{1,0:T(8,128)(2,1)} async-done(((bf16[1024,512]{1,0:T(8,128)(2,1)}), bf16[128,512]{1,0:T(8,128)(2,1)}) %reduce-scatter.2.cloned.1.call-update) | async-done | bytes 131088 | tf_op jit(solution)/shard_map/reduce_scatter | solution.py:146
  (95 shorter events, 44.5 us)
Async XLA Ops:
  7.2 24.9 %copy-start.14 = (s32[128,8]{0,1:T(8,128)S(1)}, s32[128,8]{0,1:T(8,128)}, u32[]{:S(2)}) copy-start(s32[128,8]{0,1:T(8,128)} %param.9) | copy-start | bytes 12292
  7.2 24.9 %copy-start.15 = (f32[128,8]{0,1:T(8,128)S(1)}, f32[128,8]{0,1:T(8,128)}, u32[]{:S(2)}) copy-start(f32[128,8]{0,1:T(8,128)} %param.10) | copy-start | bytes 12292
  7.2 74.0 %all-gather.2.cloned.1.call-start = ((), (), s32[]{:S(2)}) async-start(), calls=%async_computation.4 | async-start | bytes 2359296 | tf_op jit(solution)/shard_map/all_gather | solution.py:126
  11.0 64.0 %collective-permute-start = (bf16[512,768]{1,0:T(8,128)(2,1)}, bf16[512,768]{1,0:T(8,128)(2,1)}, u32[]{:S(2)}, u32[]{:S(2)}) collective-permute-start(bf16[512,768]{1,0:T(8,128)(2,1)} %pad_maximum_fusion), channel_id=1, source_target_pairs={{0,1},{1,2},{2,3},{3,0},{4,5},{5,6},{6,7},{7,4},{8,9},{9,10},{10,1... | collective-permute-start | bytes 2359304 | tf_op jit(solution)/shard_map/ppermute | solution.py:23
  18.8 57.4 %collective-permute-start.1 = (bf16[512,768]{1,0:T(8,128)(2,1)}, bf16[512,768]{1,0:T(8,128)(2,1)}, u32[]{:S(2)}, u32[]{:S(2)}) collective-permute-start(bf16[512,768]{1,0:T(8,128)(2,1)} %pad_maximum_fusion), channel_id=1, source_target_pairs={{0,2},{1,3},{2,0},{3,1},{4,6},{5,7},{6,4},{7,5},{8,10},{9,11},{10,... | collective-permute-start | bytes 2359304 | tf_op jit(solution)/shard_map/ppermute | solution.py:23
  20.7 56.7 %collective-permute-start.2 = (bf16[512,768]{1,0:T(8,128)(2,1)}, bf16[512,768]{1,0:T(8,128)(2,1)}, u32[]{:S(2)}, u32[]{:S(2)}) collective-permute-start(bf16[512,768]{1,0:T(8,128)(2,1)} %pad_maximum_fusion), channel_id=1, source_target_pairs={{0,3},{1,0},{2,1},{3,2},{4,7},{5,4},{6,5},{7,6},{8,11},{9,8},{10,9... | collective-permute-start | bytes 2359304 | tf_op jit(solution)/shard_map/ppermute | solution.py:23
  23.5 38.1 %collective-permute-start.3 = (bf16[384,512]{1,0:T(8,128)(2,1)}, bf16[384,512]{1,0:T(8,128)(2,1)}, u32[]{:S(2)}, u32[]{:S(2)}) collective-permute-start(bf16[384,512]{1,0:T(8,128)(2,1)} %bitcast.8), channel_id=1, source_target_pairs={{0,1},{1,2},{2,3},{3,0},{4,5},{5,6},{6,7},{7,4},{8,9},{9,10},{10,1... | collective-permute-start | bytes 1179656 | tf_op jit(solution)/shard_map/ppermute | solution.py:23
  27.8 38.8 %collective-permute-start.4 = (bf16[384,512]{1,0:T(8,128)(2,1)}, bf16[384,512]{1,0:T(8,128)(2,1)}, u32[]{:S(2)}, u32[]{:S(2)}) collective-permute-start(bf16[384,512]{1,0:T(8,128)(2,1)} %bitcast.8), channel_id=1, source_target_pairs={{0,2},{1,3},{2,0},{3,1},{4,6},{5,7},{6,4},{7,5},{8,10},{9,11},{10,... | collective-permute-start | bytes 1179656 | tf_op jit(solution)/shard_map/ppermute | solution.py:23
  32.7 24.8 %all-to-all-start = ((f32[8,16,128]{2,1,0:T(8,128)}), f32[8,16,128]{2,1,0:T(8,128)S(1)}, u32[]{:S(2)}, u32[]{:S(2)}) async-start(f32[8,16,128]{2,1,0:T(8,128)} %broadcast_in_dim.103), calls=%async_computation | async-start | bytes 131072 | tf_op jit(solution)/shard_map/all_to_all | solution.py:37
  60.7 20.5 %copy-start.11 = (pred[4,384,256]{2,1,0:T(32,128)(4,1)}, pred[4,384,256]{2,1,0:T(32,128)(4,1)S(1)}, u32[]{:S(2)}) copy-start(pred[4,384,256]{2,1,0:T(32,128)(4,1)S(1)} %bitcast_compare_fusion) | copy-start | bytes 1179652
  61.6 12.7 %collective-permute-start.5 = (bf16[384,512]{1,0:T(8,128)(2,1)}, bf16[384,512]{1,0:T(8,128)(2,1)S(1)}, u32[]{:S(2)}, u32[]{:S(2)}) collective-permute-start(bf16[384,512]{1,0:T(8,128)(2,1)} %bitcast.8), channel_id=1, source_target_pairs={{0,3},{1,0},{2,1},{3,2},{4,7},{5,4},{6,5},{7,6},{8,11},{9,8},{10,9... | collective-permute-start | bytes 1179656 | tf_op jit(solution)/shard_map/ppermute | solution.py:23
  83.8 49.2 %copy-start.6 = (bf16[4,512,768]{2,1,0:T(8,128)(2,1)S(1)}, bf16[4,512,768]{2,1,0:T(8,128)(2,1)}, u32[]{:S(2)}) copy-start(bf16[4,512,768]{2,1,0:T(8,128)(2,1)} %copy-done.5) | copy-start | bytes 9437188
  142.0 28.7 %all-to-all-start.2 = ((bf16[64,24,512]{2,1,0:T(8,128)(2,1)}), bf16[64,24,512]{2,1,0:T(8,128)(2,1)}, u32[]{:S(2)}, u32[]{:S(2)}) async-start(bf16[64,24,512]{2,1,0:T(8,128)(2,1)} %bitcast.106), calls=%async_computation.2 | async-start | bytes 3145728 | tf_op jit(solution)/shard_map/all_to_all | solution.py:142
  149.4 79.7 %reduce-scatter.2.cloned.1.call-start = ((), (), s32[]{:S(2)}) async-start(), calls=%async_computation.5 | async-start | bytes 1179648 | tf_op jit(solution)/shard_map/reduce_scatter | solution.py:146
  150.9 19.9 %copy-start.12 = (pred[4,384,256]{2,1,0:T(32,128)(4,1)S(1)}, pred[4,384,256]{2,1,0:T(32,128)(4,1)}, u32[]{:S(2)}) copy-start(pred[4,384,256]{2,1,0:T(32,128)(4,1)} %copy-done.11) | copy-start | bytes 1179652
  152.1 39.3 %collective-permute-start.8 = (bf16[512,384]{1,0:T(8,128)(2,1)}, bf16[512,384]{1,0:T(8,128)(2,1)S(1)}, u32[]{:S(2)}, u32[]{:S(2)}) collective-permute-start(bf16[512,384]{1,0:T(8,128)(2,1)} %convolution_convert_fusion.10), channel_id=1, source_target_pairs={{0,2},{1,3},{2,0},{3,1},{4,6},{5,7},{6,4},{7,5},{8,10},{9,11},{10,... | collective-permute-start | bytes 1179656 | tf_op jit(solution)/shard_map/ppermute | solution.py:23
  156.5 53.6 %collective-permute-start.7 = (bf16[512,384]{1,0:T(8,128)(2,1)}, bf16[512,384]{1,0:T(8,128)(2,1)S(1)}, u32[]{:S(2)}, u32[]{:S(2)}) collective-permute-start(bf16[512,384]{1,0:T(8,128)(2,1)} %convolution_convert_fusion.11), channel_id=1, source_target_pairs={{0,3},{1,0},{2,1},{3,2},{4,7},{5,4},{6,5},{7,6},{8,11},{9,8},{10,9... | collective-permute-start | bytes 1179656 | tf_op jit(solution)/shard_map/ppermute | solution.py:23
  174.5 19.5 %collective-permute-start.14 = (bf16[384,512]{1,0:T(8,128)(2,1)S(1)}, bf16[384,512]{1,0:T(8,128)(2,1)S(1)}, u32[]{:S(2)}, u32[]{:S(2)}) collective-permute-start(bf16[384,512]{1,0:T(8,128)(2,1)S(1)} %convolution_convert_fusion.2), channel_id=1, source_target_pairs={{0,2},{1,3},{2,0},{3,1},{4,6},{5,7},{6,4},{7,5},{8,10},{9,11},{10,... | collective-permute-start | bytes 1179656 | tf_op jit(solution)/shard_map/ppermute | solution.py:23
  182.4 19.5 %collective-permute-start.13 = (bf16[384,512]{1,0:T(8,128)(2,1)S(1)}, bf16[384,512]{1,0:T(8,128)(2,1)S(1)}, u32[]{:S(2)}, u32[]{:S(2)}) collective-permute-start(bf16[384,512]{1,0:T(8,128)(2,1)S(1)} %convolution_convert_fusion.3), channel_id=1, source_target_pairs={{0,3},{1,0},{2,1},{3,2},{4,7},{5,4},{6,5},{7,6},{8,11},{9,8},{10,9... | collective-permute-start | bytes 1179656 | tf_op jit(solution)/shard_map/ppermute | solution.py:23
  184.7 20.4 %collective-permute-start.12 = (bf16[384,512]{1,0:T(8,128)(2,1)S(1)}, bf16[384,512]{1,0:T(8,128)(2,1)S(1)}, u32[]{:S(2)}, u32[]{:S(2)}) collective-permute-start(bf16[384,512]{1,0:T(8,128)(2,1)S(1)} %convolution_convert_fusion.4), channel_id=1, source_target_pairs={{0,1},{1,2},{2,3},{3,0},{4,5},{5,6},{6,7},{7,4},{8,9},{9,10},{10,1... | collective-permute-start | bytes 1179656 | tf_op jit(solution)/shard_map/ppermute | solution.py:23
  191.4 18.6 %collective-permute-start.6 = (bf16[512,384]{1,0:T(8,128)(2,1)S(1)}, bf16[512,384]{1,0:T(8,128)(2,1)S(1)}, u32[]{:S(2)}, u32[]{:S(2)}) collective-permute-start(bf16[512,384]{1,0:T(8,128)(2,1)S(1)} %convolution_convert_fusion.12), channel_id=1, source_target_pairs={{0,1},{1,2},{2,3},{3,0},{4,5},{5,6},{6,7},{7,4},{8,9},{9,10},{10,1... | collective-permute-start | bytes 1179656 | tf_op jit(solution)/shard_map/ppermute | solution.py:23
  194.0 17.3 %collective-permute-start.11 = (bf16[512,384]{1,0:T(8,128)(2,1)S(1)}, bf16[512,384]{1,0:T(8,128)(2,1)S(1)}, u32[]{:S(2)}, u32[]{:S(2)}) collective-permute-start(bf16[512,384]{1,0:T(8,128)(2,1)S(1)} %convolution_convert_fusion.6), channel_id=1, source_target_pairs={{0,2},{1,3},{2,0},{3,1},{4,6},{5,7},{6,4},{7,5},{8,10},{9,11},{10,... | collective-permute-start | bytes 1179656 | tf_op jit(solution)/shard_map/ppermute | solution.py:23
  201.8 17.0 %collective-permute-start.10 = (bf16[512,384]{1,0:T(8,128)(2,1)S(1)}, bf16[512,384]{1,0:T(8,128)(2,1)S(1)}, u32[]{:S(2)}, u32[]{:S(2)}) collective-permute-start(bf16[512,384]{1,0:T(8,128)(2,1)S(1)} %convolution_convert_fusion.7), channel_id=1, source_target_pairs={{0,3},{1,0},{2,1},{3,2},{4,7},{5,4},{6,5},{7,6},{8,11},{9,8},{10,9... | collective-permute-start | bytes 1179656 | tf_op jit(solution)/shard_map/ppermute | solution.py:23
  205.1 17.4 %collective-permute-start.9 = (bf16[512,384]{1,0:T(8,128)(2,1)S(1)}, bf16[512,384]{1,0:T(8,128)(2,1)S(1)}, u32[]{:S(2)}, u32[]{:S(2)}) collective-permute-start(bf16[512,384]{1,0:T(8,128)(2,1)S(1)} %convolution_convert_fusion.8), channel_id=1, source_target_pairs={{0,1},{1,2},{2,3},{3,0},{4,5},{5,6},{6,7},{7,4},{8,9},{9,10},{10,1... | collective-permute-start | bytes 1179656 | tf_op jit(solution)/shard_map/ppermute | solution.py:23
  (11 other events, 53.9 us)
Sparse Core Ops, SparseCore 0:
  11.2 69.9 all-gather.1
  174.2 54.9 reduce-scatter.1

commit v3 on v2

v3 whole, which is shorter than its diff:
```python
import functools

import jax
import jax.numpy as jnp
from jax import lax
from jax.experimental import pallas as pl
from jax.experimental.pallas import tpu as pltpu
from jax.sharding import Mesh
from jax.sharding import PartitionSpec as P

MOST = 12
TILE = 128
N_FAR, N_NEAR, N_Y, N_C, N_X = 8, 2, 4, 2, 4
PLANE = ("x", "near", "y", "c")
LOCAL = N_NEAR * N_Y * N_C
GROUP = N_FAR // N_X
F32 = jnp.float32
BF16 = jnp.bfloat16


def dot(left, right, contract, batch=((), ())):
    return lax.dot_general(left, right, (contract, batch), preferred_element_type=F32)


def hop(value, by):
    return lax.ppermute(value, "far", [(i, (i + by) % N_FAR) for i in range(N_FAR)])


def ring_gather(value, me):
    half = value.shape[0] // 32 * 16
    whole = jnp.zeros((N_FAR,) + value.shape, value.dtype)

    def put(whole, block, by, row=0):
        return lax.dynamic_update_slice(whole, block[None], ((me + by) & (N_FAR - 1), row, 0))

    whole = put(whole, value, 0)
    up = down = value
    for step in range(1, N_FAR // 2):
        up, down = hop(up, 1), hop(down, -1)
        whole = put(put(whole, up, -step), down, step)
    up, down = hop(up[:half], 1), hop(down[half:], -1)
    return put(put(whole, up, N_FAR // 2), down, N_FAR // 2, half)


def choices(routes, gates):
    high = lax.reduce_precision(gates, 8, 7)
    mid = lax.reduce_precision(gates - high, 8, 7)
    low = gates - high - mid
    kinds = [value.T.astype(BF16) for value in (routes.astype(F32), high, mid, low)]
    rows = jnp.concatenate(kinds, axis=1)
    return jnp.pad(rows, ((0, 16 - rows.shape[0]), (0, 0)))


def pick_kernel(me, tokens, cotangents, rows, pick, *, top):
    tok, cols = cotangents.shape[1:]
    count = rows.shape[1]
    slots = GROUP * MOST
    before = lax.broadcasted_iota(jnp.int32, (tok, tok), 0) < lax.broadcasted_iota(jnp.int32, (tok, tok), 1)
    before = before.astype(F32).astype(BF16)
    wanted = (lax.broadcasted_iota(jnp.int32, (LOCAL, tok), 0) + me[0] * LOCAL).astype(F32)
    slot, gate = [], []
    for u in range(GROUP):
        choice = tokens[u, tok:, :].astype(F32)
        member = jnp.zeros((LOCAL, tok), F32)
        chosen = jnp.zeros((LOCAL, tok), F32)
        for k in range(top):
            kinds = [choice[k : k + 1, tok * i : tok * (i + 1)] for i in range(4)]
            hit = kinds[0] == wanted
            member = jnp.where(hit, 1.0, member)
            chosen = jnp.where(hit, kinds[1] + kinds[2] + kinds[3], chosen)
        rank = dot(member.astype(BF16), before, ((1,), (0,)))
        slot.append(jnp.where(member > 0.5, rank + float(MOST * u), -1.0))
        gate.append(chosen)
    slot, gate = jnp.concatenate(slot, axis=1), jnp.concatenate(gate, axis=1)
    place = lax.broadcasted_iota(jnp.int32, (LOCAL, slots, GROUP * tok), 1).astype(F32)
    hit = slot[:, None, :] == place
    onehot = jnp.where(hit, 1.0, 0.0).reshape(count, GROUP * tok).astype(BF16)
    row_gate = jnp.where(hit, gate[:, None, :], 0.0).reshape(count, GROUP * tok)
    row_gate = jnp.sum(row_gate, axis=1, keepdims=True)
    pick[0] = onehot

    def select(blocks):
        return sum(
            dot(onehot[:, tok * u : tok * (u + 1)], blocks[u, :tok, :], ((1,), (0,))) for u in range(GROUP)
        )

    rows[0, :, :cols] = select(tokens).astype(BF16)
    rows[0, :, cols:] = (select(cotangents) * row_gate).astype(BF16)


def pick_rows(me, tokens, cotangents, top):
    tok, cols = cotangents.shape[1:]
    count = LOCAL * GROUP * MOST
    grouped = lambda shape: pl.BlockSpec(shape, lambda i: (i, 0, 0))
    return pl.pallas_call(
        functools.partial(pick_kernel, top=top),
        grid=(N_X,),
        in_specs=[
            pl.BlockSpec(memory_space=pltpu.SMEM),
            grouped((GROUP,) + tokens.shape[1:]),
            grouped((GROUP, tok, cols)),
        ],
        out_specs=[grouped((1, count, 2 * cols)), grouped((1, count, GROUP * tok))],
        out_shape=[
            in_hbm(N_X, count, 2 * cols),
            in_hbm(N_X, count, GROUP * tok),
        ],
        compiler_params=params(),
        cost_estimate=pl.CostEstimate(
            flops=4 * N_X * count * GROUP * tok * cols, bytes_accessed=7_000_000, transcendentals=0
        ),
    )(me[None], tokens, cotangents)


def expert_kernel(rows, w_in, w_out, row_grad, backs, hidden, pre_gate, pre_up, back):
    step = pl.program_id(0)
    cols = row_grad.shape[2]
    width = hidden.shape[1]

    @pl.when(step == 0)
    def _():
        pre_gate[...] = jnp.zeros_like(pre_gate)
        pre_up[...] = jnp.zeros_like(pre_up)
        back[...] = jnp.zeros_like(back)

    ins = rows[0, :, :cols]
    pre_gate[...] += dot(ins, w_in[step, :, :width], ((1,), (0,)))
    pre_up[...] += dot(ins, w_in[step, :, width:], ((1,), (0,)))
    back[...] += dot(rows[0, :, cols:], w_out[0], ((1,), (1,)))

    @pl.when(step == N_X - 1)
    def _():
        g, u, b = pre_gate[...], pre_up[...], back[...]
        s = jax.nn.sigmoid(g)
        activated = g * s
        hidden[...] = (activated * u).astype(BF16)
        d_up = (b * activated).astype(BF16)
        d_gate = (b * u * s * (1.0 + g * (1.0 - s))).astype(BF16)
        backs[:, :width] = d_gate
        backs[:, width:] = d_up
        for j in range(N_X):
            from_gate = dot(d_gate, w_in[j, :, :width], ((1,), (1,)))
            from_up = dot(d_up, w_in[j, :, width:], ((1,), (1,)))
            row_grad[j] = (from_gate + from_up).astype(BF16)


def whole(shape):
    return pl.BlockSpec(shape, lambda *_: (0,) * len(shape))


def params():
    return pltpu.CompilerParams(dimension_semantics=("arbitrary",), vmem_limit_bytes=32 * 1024 * 1024)


def in_hbm(*shape):
    return pltpu.HBM(shape, BF16)


def expert(rows, w_in, w_out):
    parts, count, both = rows.shape
    width, cols = w_out.shape[1:]
    shapes = (parts, count, cols), (count, 2 * width), (count, width)
    return pl.pallas_call(
        expert_kernel,
        grid=(parts,),
        in_specs=[
            pl.BlockSpec((1, count, both), lambda j: (j, 0, 0)),
            whole(w_in.shape),
            pl.BlockSpec((1, width, cols), lambda j: (j, 0, 0)),
        ],
        out_specs=[whole(shape) for shape in shapes],
        out_shape=[in_hbm(*shapes[0]), *[jax.ShapeDtypeStruct(shape, BF16) for shape in shapes[1:]]],
        scratch_shapes=[pltpu.VMEM((count, width), F32)] * 3,
        compiler_params=params(),
        cost_estimate=pl.CostEstimate(
            flops=10 * parts * count * cols * width, bytes_accessed=11_000_000, transcendentals=count * width
        ),
    )(rows, w_in, w_out)


def tiles(height, breadth, wide):
    for n in range(height * breadth // TILE**2):
        there, here = divmod(n, wide // TILE), divmod(n, breadth // TILE)
        yield tuple(pl.ds(TILE * i, TILE) for i in here), tuple(TILE * i for i in there)


def parts_kernel(rows, backs, hidden, out, down):
    cols = rows.shape[2] // 2
    out[0, :cols] = dot(rows[0, :, :cols], backs[...], ((0,), (0,))).astype(BF16)
    down[...] = dot(hidden[...], rows[0, :, cols:], ((0,), (0,)))
    for here, there in tiles(*down.shape, out.shape[2]):
        out[0, cols + there[0] : cols + there[0] + TILE, there[1] : there[1] + TILE] = down[here].astype(BF16)


def weight_parts(rows, backs, hidden):
    parts, count, both = rows.shape
    cols, width, wide = both // 2, hidden.shape[1], backs.shape[1]
    shape = parts, cols + width * cols // wide, wide
    return pl.pallas_call(
        parts_kernel,
        grid=(parts,),
        in_specs=[
            pl.BlockSpec((1, count, both), lambda j: (j, 0, 0)),
            whole(backs.shape),
            whole(hidden.shape),
        ],
        out_specs=pl.BlockSpec((1, *shape[1:]), lambda j: (j, 0, 0)),
        out_shape=in_hbm(*shape),
        scratch_shapes=[pltpu.VMEM((width, cols), F32)],
        compiler_params=params(),
        cost_estimate=pl.CostEstimate(
            flops=parts * count * both * width * 3, bytes_accessed=9_000_000, transcendentals=0
        ),
    )(rows, backs, hidden)


def unpack_kernel(sums, gate, up, down):
    cols, width = gate.shape
    gate[...] = sums[:cols, :width]
    up[...] = sums[:cols, width:]
    for here, there in tiles(*down.shape, sums.shape[1]):
        down[here] = sums[cols + there[0] : cols + there[0] + TILE, there[1] : there[1] + TILE]


def unpack(sums, cols, width):
    shapes = (cols, width), (cols, width), (width, cols)
    return pl.pallas_call(
        unpack_kernel,
        out_shape=[jax.ShapeDtypeStruct(shape, BF16) for shape in shapes],
        compiler_params=pltpu.CompilerParams(vmem_limit_bytes=32 * 1024 * 1024),
        cost_estimate=pl.CostEstimate(flops=0, bytes_accessed=2_400_000, transcendentals=0),
    )(sums)


def tokens_kernel(me, pick, back, own, up, down, two):
    tok = own.shape[1]
    for target, steps in ((up, (1, 5)), (down, (7, 3)), (two, (2, 6)), (own, (0, 4))):
        for place, step in enumerate(steps):
            far = lax.rem(me[0] + step, N_FAR)
            group, within = lax.div(far, GROUP), lax.rem(far, GROUP)
            chosen = pick[group, :, pl.ds(pl.multiple_of(within * tok, tok), tok)]
            target[place] = dot(chosen, back[group], ((0,), (0,))).astype(BF16)


def token_parts(me, pick, back):
    tok = pick.shape[2] // GROUP
    pair = (2, tok, back.shape[2])
    return pl.pallas_call(
        tokens_kernel,
        in_specs=[pl.BlockSpec(memory_space=pltpu.SMEM)] + [pl.BlockSpec(memory_space=pltpu.VMEM)] * 2,
        out_specs=[pl.BlockSpec(memory_space=pltpu.VMEM)] * 4,
        out_shape=[jax.ShapeDtypeStruct(pair, BF16)] * 4,
        compiler_params=pltpu.CompilerParams(vmem_limit_bytes=32 * 1024 * 1024),
        cost_estimate=pl.CostEstimate(
            flops=2 * back.size * tok * GROUP, bytes_accessed=4_000_000, transcendentals=0
        ),
    )(me[None], pick, back)


def scatter_sum(me, pick, back):
    own, up, down, two = token_parts(me, pick, back)
    half = own.shape[2] // 2
    up, down = hop(up, 1), hop(down, -1)
    left, right = hop(two[:, :, :half], 2), hop(two[::-1, :, half:], -2)
    total = own.astype(F32) + up.astype(F32) + down.astype(F32)
    total = total + jnp.concatenate([left, right], axis=2).astype(F32)
    opposite = hop(total[1].astype(BF16), N_FAR // 2)
    return (total[0] + opposite.astype(F32)).astype(BF16)


def shards(tokens, grad_out, routes, gates, w_gate, w_up, w_down):
    me_far = lax.axis_index("far")
    cols = tokens.shape[1]
    width = w_gate.shape[2]
    w_in = lax.all_gather(jnp.concatenate([w_gate[0], w_up[0]], axis=1), "x", axis=0)
    w_out = lax.all_gather(w_down[0], "x", axis=0)
    marked = jnp.concatenate([tokens, choices(routes, gates)], axis=0)
    cotangents = ring_gather(grad_out, me_far)
    marked = ring_gather(marked, me_far)
    w_in, marked, cotangents = lax.optimization_barrier((w_in, marked, cotangents))
    rows, pick = pick_rows(me_far, marked, cotangents, routes.shape[1])
    count = rows.shape[1]
    slots = count // LOCAL
    rows = lax.all_to_all(
        rows.reshape(-1, slots, 2 * cols), PLANE, split_axis=0, concat_axis=0, tiled=True
    ).reshape(N_X, count, 2 * cols)
    row_grad, backs, hidden = expert(rows, w_in, w_out)
    came_back = lax.all_to_all(
        row_grad.reshape(-1, slots, cols), PLANE, split_axis=0, concat_axis=0, tiled=True
    ).reshape(N_X, count, cols)
    parts = weight_parts(rows, backs, hidden)
    grads = lax.psum_scatter(parts, "x", scatter_dimension=0, tiled=False)
    d_tokens = scatter_sum(me_far, pick, came_back)
    grads = unpack(grads, cols, width)
    return (d_tokens, *[grad[None] for grad in grads])


def solution(mesh):
    sizes = (N_FAR, N_NEAR, N_Y, N_C, N_X)
    fine = Mesh(mesh.devices.reshape(sizes), ("far", "near", "y", "c", "x"))
    expert_axes = ("far", "near", "y", "c")
    return jax.shard_map(
        shards,
        mesh=fine,
        in_specs=(
            P(expert_axes, "x"),
            P(expert_axes, "x"),
            P(expert_axes, None),
            P(expert_axes, None),
            P(expert_axes, "x", None),
            P(expert_axes, "x", None),
            P(expert_axes, None, "x"),
        ),
        out_specs=(
            P(expert_axes, "x"),
            P(expert_axes, "x", None),
            P(expert_axes, "x", None),
            P(expert_axes, None, "x"),
        ),
        check_vma=False,
    )
```

time: 237 us -> 272 us (1.15); the launches traced: 236 us -> 268 us
  waiting for transfers between devices: 51.6 us -> 94.9 us
  starting transfers between devices: 74.3 us -> 100 us
  blocking collectives: 49.1 us -> 32.2 us
  matrix products: 15 us -> 0 us
  local copies, waits for them, and re-layouts: 18.8 us -> 6.48 us
  Pallas kernels: 6.4 us -> 16.6 us
  other arithmetic: 6.05 us -> 2.95 us
    all_gather x1 -> x2, waiting for transfers between devices: 2.51 us -> 48.2 us  [the longest x1 48.2 us: shards(): w_out = lax.all_gather(w_down[0], 'x', axis=0)]
    ppermute x15 -> x21, starting transfers between devices: 57 us -> 92.2 us  [hop(): lax.ppermute(value, 'far', [(i, (i + by) % N_FAR) for i in range(N_FAR)])]
    ppermute x15 -> x21, waiting for transfers between devices: 21 us -> 46 us  [hop(): lax.ppermute(value, 'far', [(i, (i + by) % N_FAR) for i in range(N_FAR)])]
    all_to_all x2 -> x1, waiting for transfers between devices: 22.6 us -> 0.01 us  [shards(): lax.all_to_all(rows.reshape(-1, slots, 2 * cols), PLANE, split_axis=0, co...]
    all_to_all x1, blocking collectives: 49.1 us -> 32.2 us  [shards(): lax.all_to_all(row_grad.reshape(-1, slots, cols), PLANE, split_axis=0, co...]
    dot_general x15 -> x0, matrix products: 15 us -> none  [dot(): lax.dot_general(left, right, (contract, batch), preferred_element_type=F32)]
    dynamic_update_slice x8 -> x17, local copies, waits for them, and re-layouts: 10.9 us -> 0.26 us  [put(): lax.dynamic_update_slice(whole, block[None], (me + by & N_FAR - 1, row, 0))]
    pallas_call x0 -> x4, Pallas kernels: none -> 10.3 us  [the longest x1 4.53 us: weight_parts(): pl.pallas_call(parts_kernel, grid=(parts,), in_specs=[pl.BlockSpec((1, co...]
  transfers between devices with their start and end apart: 19 -> 25, of which waited for: 9 -> 7; matrix products, arithmetic and copies ran while one was open for 13% -> 1% of each run, Pallas kernels for 0% -> 0%
where the time goes in v3:
time: 272 us; the launch traced here: 268 us
  starting transfers between devices  100 us (37%)
  waiting for transfers between devices  94.9 us (35%)
  blocking collectives  32.2 us (12%)
  Pallas kernels  16.6 us (6%)
  between operations  14.4 us (5%)
  local copies, waits for them, and re-layouts  6.48 us (2%)
  other arithmetic  2.95 us (1%)
    ppermute x21, starting transfers between devices, hop(): lax.ppermute(value, 'far', [(i, (i + by) % N_FAR) for i in range(N_FAR)])  92.2 us
    all_gather x1, waiting for transfers between devices, shards(): w_out = lax.all_gather(w_down[0], 'x', axis=0)  48.2 us
    ppermute x21, waiting for transfers between devices, hop(): lax.ppermute(value, 'far', [(i, (i + by) % N_FAR) for i in range(N_FAR)])  46 us
    all_to_all x1, blocking collectives, shards(): lax.all_to_all(row_grad.reshape(-1, slots, cols), PLANE, split_axis=0, co...  32.2 us
    all_to_all x1, starting transfers between devices, shards(): lax.all_to_all(rows.reshape(-1, slots, 2 * cols), PLANE, split_axis=0, co...  8.17 us
    pallas_call x1, Pallas kernels, expert(): pl.pallas_call(expert_kernel, grid=(parts,), in_specs=[pl.BlockSpec((1, c...  6.36 us
    unnamed x18, local copies, waits for them, and re-layouts  5.97 us
  transfers between devices with their start and end apart: 25, of which 7 were waited for; matrix products, arithmetic and copies ran while one was open for 1% of the time, Pallas kernels for 0%

profile of v3, /device:TPU:6, one launch (start us, length us, event | category | flops | bytes accessed | tf_op | source)
XLA Modules:
  0.0 268.0 jit_solution(7699930310747434456)
XLA Ops:
  9.5 5.2 %collective-permute-start = (bf16[144,512]{1,0:T(8,128)(2,1)S(1)}, bf16[144,512]{1,0:T(8,128)(2,1)S(1)}, u32[]{:S(2)}, u32[]{:S(2)}) collective-permute-start(bf16[144,512]{1,0:T(8,128)(2,1)S(1)} %pad_maximum_fusion.1), channel_id=1, source_target_pairs={{0,64},{64,128},{128,192},{192,256},{256,320},{320,384},{384,448},... | collective-permute-start | bytes 442376 | tf_op jit(solution)/shard_map/ppermute | solution.py:26
  14.6 8.6 %collective-permute-start.1 = (bf16[144,512]{1,0:T(8,128)(2,1)S(1)}, bf16[144,512]{1,0:T(8,128)(2,1)S(1)}, u32[]{:S(2)}, u32[]{:S(2)}) collective-permute-start(bf16[144,512]{1,0:T(8,128)(2,1)S(1)} %pad_maximum_fusion.1), channel_id=1, source_target_pairs={{0,448},{64,0},{128,64},{192,128},{256,192},{320,256},{384,320},{4... | collective-permute-start | bytes 442376 | tf_op jit(solution)/shard_map/ppermute | solution.py:26
  25.2 6.0 %collective-permute-start.9 = (bf16[128,512]{1,0:T(8,128)(2,1)S(1)}, bf16[128,512]{1,0:T(8,128)(2,1)S(1)}, u32[]{:S(2)}, u32[]{:S(2)}) collective-permute-start(bf16[128,512]{1,0:T(8,128)(2,1)S(1)} %copy-done.6), channel_id=1, source_target_pairs={{0,448},{64,0},{128,64},{192,128},{256,192},{320,256},{384,320},{4... | collective-permute-start | bytes 393224 | tf_op jit(solution)/shard_map/ppermute | solution.py:26
  31.5 3.2 %collective-permute-done.8 = bf16[128,512]{1,0:T(8,128)(2,1)S(1)} collective-permute-done((bf16[128,512]{1,0:T(8,128)(2,1)S(1)}, bf16[128,512]{1,0:T(8,128)(2,1)S(1)}, u32[]{:S(2)}, u32[]{:S(2)}) %collective-permute-start.8) | collective-permute-done | bytes 131104 | tf_op jit(solution)/shard_map/ppermute | solution.py:26
  34.7 2.7 collective-permute-start.10
  37.3 5.3 %collective-permute-start.11 = (bf16[128,512]{1,0:T(8,128)(2,1)S(1)}, bf16[128,512]{1,0:T(8,128)(2,1)S(1)}, u32[]{:S(2)}, u32[]{:S(2)}) collective-permute-start(bf16[128,512]{1,0:T(8,128)(2,1)S(1)} %collective-permute-done.9), channel_id=1, source_target_pairs={{0,448},{64,0},{128,64},{192,128},{256,192},{320,256},{384,320},{4... | collective-permute-start | bytes 393224 | tf_op jit(solution)/shard_map/ppermute | solution.py:26
  44.7 6.0 %collective-permute-start.3 = (bf16[144,512]{1,0:T(8,128)(2,1)S(1)}, bf16[144,512]{1,0:T(8,128)(2,1)S(1)}, u32[]{:S(2)}, u32[]{:S(2)}) collective-permute-start(bf16[144,512]{1,0:T(8,128)(2,1)S(1)} %collective-permute-done.1), channel_id=1, source_target_pairs={{0,448},{64,0},{128,64},{192,128},{256,192},{320,256},{384,320},{4... | collective-permute-start | bytes 442376 | tf_op jit(solution)/shard_map/ppermute | solution.py:26
  52.7 6.0 %collective-permute-start.13 = (bf16[128,512]{1,0:T(8,128)(2,1)S(1)}, bf16[128,512]{1,0:T(8,128)(2,1)S(1)}, u32[]{:S(2)}, u32[]{:S(2)}) collective-permute-start(bf16[128,512]{1,0:T(8,128)(2,1)S(1)} %collective-permute-done.11), channel_id=1, source_target_pairs={{0,448},{64,0},{128,64},{192,128},{256,192},{320,256},{384,320},{4... | collective-permute-start | bytes 393224 | tf_op jit(solution)/shard_map/ppermute | solution.py:26
  60.8 6.0 %collective-permute-start.5 = (bf16[144,512]{1,0:T(8,128)(2,1)S(1)}, bf16[144,512]{1,0:T(8,128)(2,1)S(1)}, u32[]{:S(2)}, u32[]{:S(2)}) collective-permute-start(bf16[144,512]{1,0:T(8,128)(2,1)S(1)} %collective-permute-done.3), channel_id=1, source_target_pairs={{0,448},{64,0},{128,64},{192,128},{256,192},{320,256},{384,320},{4... | collective-permute-start | bytes 442376 | tf_op jit(solution)/shard_map/ppermute | solution.py:26
  68.8 6.0 %collective-permute-start.15 = (bf16[64,512]{1,0:T(8,128)(2,1)S(1)}, bf16[64,512]{1,0:T(8,128)(2,1)S(1)}, u32[]{:S(2)}, u32[]{:S(2)}) collective-permute-start(bf16[64,512]{1,0:T(8,128)(2,1)S(1)} %slice.36), channel_id=1, source_target_pairs={{0,448},{64,0},{128,64},{192,128},{256,192},{320,256},{384,320},{4... | collective-permute-start | bytes 196616 | tf_op jit(solution)/shard_map/ppermute | solution.py:26
  76.9 6.0 %collective-permute-start.7 = (bf16[80,512]{1,0:T(8,128)(2,1)S(1)}, bf16[80,512]{1,0:T(8,128)(2,1)S(1)}, u32[]{:S(2)}, u32[]{:S(2)}) collective-permute-start(bf16[80,512]{1,0:T(8,128)(2,1)S(1)} %slice.34), channel_id=1, source_target_pairs={{0,448},{64,0},{128,64},{192,128},{256,192},{320,256},{384,320},{4... | collective-permute-start | bytes 245768 | tf_op jit(solution)/shard_map/ppermute | solution.py:26
  85.8 3.9 %shard_map.102 = (bf16[4,384,1024]{2,1,0:T(8,128)(2,1)}, bf16[4,384,256]{2,1,0:T(8,128)(2,1)}) custom-call(s32[1]{0:T(128)} %bitcast.me, bf16[8,144,512]{2,1,0:T(8,128)(2,1)S(1)} %bitcast_dynamic-update-slice_fusion.14.tokens, bf16[8,128,512]{2,1,0:T(8,128)(2,1)S(1)} %bitcast_dynamic-update-slice_fusion.15.cotangents), custom_call_target="tpu_custom_call" | custom-call | flops 805306368 | bytes 7000000 | tf_op jit(solution)/shard_map/pallas_call | solution.py:95
  89.7 8.2 %all-to-all-start = ((bf16[64,24,1024]{2,1,0:T(8,128)(2,1)}), bf16[64,24,1024]{2,1,0:T(8,128)(2,1)S(1)}, u32[]{:S(2)}, u32[]{:S(2)}) async-start(bf16[64,24,1024]{2,1,0:T(8,128)(2,1)} %bitcast.69), calls=%async_computation | async-start | bytes 6291456 | tf_op jit(solution)/shard_map/all_to_all | solution.py:284
  98.7 48.2 %all-gather.4.cloned.1.call-done.w_out = bf16[4,384,512]{2,1,0:T(8,128)(2,1)} async-done(((bf16[1,384,512]{2,1,0:T(8,128)(2,1)}), bf16[4,384,512]{2,1,0:T(8,128)(2,1)}) %all-gather.4.cloned.1.call-update) | async-done | bytes 1572880 | tf_op jit(solution)/shard_map/all_gather | solution.py:276
  150.2 6.4 %shard_map.103 = (bf16[4,384,512]{2,1,0:T(8,128)(2,1)}, bf16[384,768]{1,0:T(8,128)(2,1)S(1)}, bf16[384,384]{1,0:T(8,128)(2,1)S(1)}) custom-call(bf16[4,384,1024]{2,1,0:T(8,128)(2,1)S(1)} %bitcast.64, bf16[4,512,768]{2,1,0:T(8,128)(2,1)S(1)} %bitcast.68, bf16[4,384,512]{2,1,0:T(8,128)(2,1)S(1)} %copy-done.3), custom_call_target="tpu_custom_call" | custom-call | flops 3019898880 | bytes 11000000 | tf_op jit(solution)/shard_map/pallas_call | solution.py:163
  156.6 4.5 %shard_map.105 = bf16[4,768,768]{2,1,0:T(8,128)(2,1)} custom-call(bf16[4,384,1024]{2,1,0:T(8,128)(2,1)S(1)} %bitcast.65, bf16[384,768]{1,0:T(8,128)(2,1)S(1)} %get-tuple-element.29.backs, bf16[384,384]{1,0:T(8,128)(2,1)S(1)} %get-tuple-element.30.hidden), custom_call_target="tpu_custom_call" | custom-call | flops 1811939328 | bytes 9000000 | tf_op jit(solution)/shard_map/pallas_call | solution.py:199
  162.5 32.2 %all_to_all.10 = bf16[64,24,512]{2,1,0:T(8,128)(2,1)S(1)} all-to-all(bf16[64,24,512]{2,1,0:T(8,128)(2,1)S(1)} %bitcast.70), channel_id=1, replica_groups=mesh['far'=8,'near'=2,'y'=4,'c'=2,'x'=4] {'x','near','y','c'}, dimensions={0} | all-to-all | bytes 3145728 | tf_op jit(solution)/shard_map/all_to_all | solution.py:288
  195.4 6.2 %collective-permute-start.17 = (bf16[2,128,512]{2,1,0:T(8,128)(2,1)S(1)}, bf16[2,128,512]{2,1,0:T(8,128)(2,1)S(1)}, u32[]{:S(2)}, u32[]{:S(2)}) collective-permute-start(bf16[2,128,512]{2,1,0:T(8,128)(2,1)S(1)} %get-tuple-element.27), channel_id=1, source_target_pairs={{0,448},{64,0},{128,64},{192,128},{256,192},{320,256},{384,320},{4... | collective-permute-start | bytes 786440 | tf_op jit(solution)/shard_map/ppermute | solution.py:26
  203.6 7.2 %collective-permute-start.19 = (bf16[2,128,256]{2,1,0:T(8,128)(2,1)S(1)}, bf16[2,128,256]{2,1,0:T(8,128)(2,1)S(1)}, u32[]{:S(2)}, u32[]{:S(2)}) collective-permute-start(bf16[2,128,256]{2,1,0:T(8,128)(2,1)S(1)} %rev.3), channel_id=1, source_target_pairs={{0,384},{64,448},{128,0},{192,64},{256,128},{320,192},{384,256},{4... | collective-permute-start | bytes 393224 | tf_op jit(solution)/shard_map/ppermute | solution.py:26
  210.8 2.6 collective-permute-start.18
  213.4 11.6 %collective-permute-done.19 = bf16[2,128,256]{2,1,0:T(8,128)(2,1)S(1)} collective-permute-done((bf16[2,128,256]{2,1,0:T(8,128)(2,1)S(1)}, bf16[2,128,256]{2,1,0:T(8,128)(2,1)S(1)}, u32[]{:S(2)}, u32[]{:S(2)}) %collective-permute-start.19) | collective-permute-done | bytes 131104 | tf_op jit(solution)/shard_map/ppermute | solution.py:26
  225.0 9.8 %collective-permute-done.18 = bf16[2,128,256]{2,1,0:T(8,128)(2,1)S(1)} collective-permute-done((bf16[2,128,256]{2,1,0:T(8,128)(2,1)S(1)}, bf16[2,128,256]{2,1,0:T(8,128)(2,1)S(1)}, u32[]{:S(2)}, u32[]{:S(2)}) %collective-permute-start.18) | collective-permute-done | bytes 131104 | tf_op jit(solution)/shard_map/ppermute | solution.py:26
  234.9 4.8 %collective-permute-start.20 = (bf16[128,512]{1,0:T(8,128)(2,1)S(1)}, bf16[128,512]{1,0:T(8,128)(2,1)S(1)}, u32[]{:S(2)}, u32[]{:S(2)}) collective-permute-start(bf16[128,512]{1,0:T(8,128)(2,1)S(1)} %fusion.2), channel_id=1, source_target_pairs={{0,256},{64,320},{128,384},{192,448},{256,0},{320,64},{384,128},{4... | collective-permute-start | bytes 393224 | tf_op jit(solution)/shard_map/ppermute | solution.py:26
  239.8 18.6 %collective-permute-done.20 = bf16[128,512]{1,0:T(8,128)(2,1)S(1)} collective-permute-done((bf16[128,512]{1,0:T(8,128)(2,1)S(1)}, bf16[128,512]{1,0:T(8,128)(2,1)S(1)}, u32[]{:S(2)}, u32[]{:S(2)}) %collective-permute-start.20) | collective-permute-done | bytes 131104 | tf_op jit(solution)/shard_map/ppermute | solution.py:26
  (87 shorter events, 28.4 us)
Async XLA Ops:
  7.2 78.7 %all-gather.6.cloned.1.call-start = ((), (), s32[]{:S(2)}) async-start(), calls=%async_computation.5 | async-start | bytes 3932160 | tf_op jit(solution)/shard_map/all_gather | solution.py:275
  9.5 33.3 %collective-permute-start = (bf16[144,512]{1,0:T(8,128)(2,1)S(1)}, bf16[144,512]{1,0:T(8,128)(2,1)S(1)}, u32[]{:S(2)}, u32[]{:S(2)}) collective-permute-start(bf16[144,512]{1,0:T(8,128)(2,1)S(1)} %pad_maximum_fusion.1), channel_id=1, source_target_pairs={{0,64},{64,128},{128,192},{192,256},{256,320},{320,384},{384,448},... | collective-permute-start | bytes 442376 | tf_op jit(solution)/shard_map/ppermute | solution.py:26
  14.6 30.0 %collective-permute-start.1 = (bf16[144,512]{1,0:T(8,128)(2,1)S(1)}, bf16[144,512]{1,0:T(8,128)(2,1)S(1)}, u32[]{:S(2)}, u32[]{:S(2)}) collective-permute-start(bf16[144,512]{1,0:T(8,128)(2,1)S(1)} %pad_maximum_fusion.1), channel_id=1, source_target_pairs={{0,448},{64,0},{128,64},{192,128},{256,192},{320,256},{384,320},{4... | collective-permute-start | bytes 442376 | tf_op jit(solution)/shard_map/ppermute | solution.py:26
  23.2 11.4 %collective-permute-start.8 = (bf16[128,512]{1,0:T(8,128)(2,1)S(1)}, bf16[128,512]{1,0:T(8,128)(2,1)S(1)}, u32[]{:S(2)}, u32[]{:S(2)}) collective-permute-start(bf16[128,512]{1,0:T(8,128)(2,1)S(1)} %copy-done.6), channel_id=1, source_target_pairs={{0,64},{64,128},{128,192},{192,256},{256,320},{320,384},{384,448},... | collective-permute-start | bytes 393224 | tf_op jit(solution)/shard_map/ppermute | solution.py:26
  25.2 12.2 %collective-permute-start.9 = (bf16[128,512]{1,0:T(8,128)(2,1)S(1)}, bf16[128,512]{1,0:T(8,128)(2,1)S(1)}, u32[]{:S(2)}, u32[]{:S(2)}) collective-permute-start(bf16[128,512]{1,0:T(8,128)(2,1)S(1)} %copy-done.6), channel_id=1, source_target_pairs={{0,448},{64,0},{128,64},{192,128},{256,192},{320,256},{384,320},{4... | collective-permute-start | bytes 393224 | tf_op jit(solution)/shard_map/ppermute | solution.py:26
  34.7 16.1 %collective-permute-start.10 = (bf16[128,512]{1,0:T(8,128)(2,1)S(1)}, bf16[128,512]{1,0:T(8,128)(2,1)S(1)}, u32[]{:S(2)}, u32[]{:S(2)}) collective-permute-start(bf16[128,512]{1,0:T(8,128)(2,1)S(1)} %collective-permute-done.8), channel_id=1, source_target_pairs={{0,64},{64,128},{128,192},{192,256},{256,320},{320,384},{384,448},... | collective-permute-start | bytes 393224 | tf_op jit(solution)/shard_map/ppermute | solution.py:26
  37.3 15.4 %collective-permute-start.11 = (bf16[128,512]{1,0:T(8,128)(2,1)S(1)}, bf16[128,512]{1,0:T(8,128)(2,1)S(1)}, u32[]{:S(2)}, u32[]{:S(2)}) collective-permute-start(bf16[128,512]{1,0:T(8,128)(2,1)S(1)} %collective-permute-done.9), channel_id=1, source_target_pairs={{0,448},{64,0},{128,64},{192,128},{256,192},{320,256},{384,320},{4... | collective-permute-start | bytes 393224 | tf_op jit(solution)/shard_map/ppermute | solution.py:26
  42.8 16.1 %collective-permute-start.2 = (bf16[144,512]{1,0:T(8,128)(2,1)S(1)}, bf16[144,512]{1,0:T(8,128)(2,1)S(1)}, u32[]{:S(2)}, u32[]{:S(2)}) collective-permute-start(bf16[144,512]{1,0:T(8,128)(2,1)S(1)} %collective-permute-done), channel_id=1, source_target_pairs={{0,64},{64,128},{128,192},{192,256},{256,320},{320,384},{384,448},... | collective-permute-start | bytes 442376 | tf_op jit(solution)/shard_map/ppermute | solution.py:26
  44.7 16.1 %collective-permute-start.3 = (bf16[144,512]{1,0:T(8,128)(2,1)S(1)}, bf16[144,512]{1,0:T(8,128)(2,1)S(1)}, u32[]{:S(2)}, u32[]{:S(2)}) collective-permute-start(bf16[144,512]{1,0:T(8,128)(2,1)S(1)} %collective-permute-done.1), channel_id=1, source_target_pairs={{0,448},{64,0},{128,64},{192,128},{256,192},{320,256},{384,320},{4... | collective-permute-start | bytes 442376 | tf_op jit(solution)/shard_map/ppermute | solution.py:26
  50.8 16.1 %collective-permute-start.12 = (bf16[128,512]{1,0:T(8,128)(2,1)S(1)}, bf16[128,512]{1,0:T(8,128)(2,1)S(1)}, u32[]{:S(2)}, u32[]{:S(2)}) collective-permute-start(bf16[128,512]{1,0:T(8,128)(2,1)S(1)} %collective-permute-done.10), channel_id=1, source_target_pairs={{0,64},{64,128},{128,192},{192,256},{256,320},{320,384},{384,448},... | collective-permute-start | bytes 393224 | tf_op jit(solution)/shard_map/ppermute | solution.py:26
  52.7 16.1 %collective-permute-start.13 = (bf16[128,512]{1,0:T(8,128)(2,1)S(1)}, bf16[128,512]{1,0:T(8,128)(2,1)S(1)}, u32[]{:S(2)}, u32[]{:S(2)}) collective-permute-start(bf16[128,512]{1,0:T(8,128)(2,1)S(1)} %collective-permute-done.11), channel_id=1, source_target_pairs={{0,448},{64,0},{128,64},{192,128},{256,192},{320,256},{384,320},{4... | collective-permute-start | bytes 393224 | tf_op jit(solution)/shard_map/ppermute | solution.py:26
  58.8 16.1 %collective-permute-start.4 = (bf16[144,512]{1,0:T(8,128)(2,1)S(1)}, bf16[144,512]{1,0:T(8,128)(2,1)S(1)}, u32[]{:S(2)}, u32[]{:S(2)}) collective-permute-start(bf16[144,512]{1,0:T(8,128)(2,1)S(1)} %collective-permute-done.2), channel_id=1, source_target_pairs={{0,64},{64,128},{128,192},{192,256},{256,320},{320,384},{384,448},... | collective-permute-start | bytes 442376 | tf_op jit(solution)/shard_map/ppermute | solution.py:26
  60.8 16.1 %collective-permute-start.5 = (bf16[144,512]{1,0:T(8,128)(2,1)S(1)}, bf16[144,512]{1,0:T(8,128)(2,1)S(1)}, u32[]{:S(2)}, u32[]{:S(2)}) collective-permute-start(bf16[144,512]{1,0:T(8,128)(2,1)S(1)} %collective-permute-done.3), channel_id=1, source_target_pairs={{0,448},{64,0},{128,64},{192,128},{256,192},{320,256},{384,320},{4... | collective-permute-start | bytes 442376 | tf_op jit(solution)/shard_map/ppermute | solution.py:26
  66.9 16.1 %collective-permute-start.14 = (bf16[64,512]{1,0:T(8,128)(2,1)S(1)}, bf16[64,512]{1,0:T(8,128)(2,1)S(1)}, u32[]{:S(2)}, u32[]{:S(2)}) collective-permute-start(bf16[64,512]{1,0:T(8,128)(2,1)S(1)} %slice.35), channel_id=1, source_target_pairs={{0,64},{64,128},{128,192},{192,256},{256,320},{320,384},{384,448},... | collective-permute-start | bytes 196616 | tf_op jit(solution)/shard_map/ppermute | solution.py:26
  68.8 14.2 %collective-permute-start.15 = (bf16[64,512]{1,0:T(8,128)(2,1)S(1)}, bf16[64,512]{1,0:T(8,128)(2,1)S(1)}, u32[]{:S(2)}, u32[]{:S(2)}) collective-permute-start(bf16[64,512]{1,0:T(8,128)(2,1)S(1)} %slice.36), channel_id=1, source_target_pairs={{0,448},{64,0},{128,64},{192,128},{256,192},{320,256},{384,320},{4... | collective-permute-start | bytes 196616 | tf_op jit(solution)/shard_map/ppermute | solution.py:26
  74.9 9.0 %collective-permute-start.6 = (bf16[64,512]{1,0:T(8,128)(2,1)S(1)}, bf16[64,512]{1,0:T(8,128)(2,1)S(1)}, u32[]{:S(2)}, u32[]{:S(2)}) collective-permute-start(bf16[64,512]{1,0:T(8,128)(2,1)S(1)} %slice.33), channel_id=1, source_target_pairs={{0,64},{64,128},{128,192},{192,256},{256,320},{320,384},{384,448},... | collective-permute-start | bytes 196616 | tf_op jit(solution)/shard_map/ppermute | solution.py:26
  89.7 57.2 %all-to-all-start = ((bf16[64,24,1024]{2,1,0:T(8,128)(2,1)}), bf16[64,24,1024]{2,1,0:T(8,128)(2,1)S(1)}, u32[]{:S(2)}, u32[]{:S(2)}) async-start(bf16[64,24,1024]{2,1,0:T(8,128)(2,1)} %bitcast.69), calls=%async_computation | async-start | bytes 6291456 | tf_op jit(solution)/shard_map/all_to_all | solution.py:284
  97.9 49.0 %all-gather.4.cloned.1.call-start = ((), (), s32[]{:S(2)}) async-start(), calls=%async_computation.3 | async-start | bytes 1966080 | tf_op jit(solution)/shard_map/all_gather | solution.py:276
  98.7 160.4 %reduce-scatter.2.cloned.1.call-start = ((), (), s32[]{:S(2)}) async-start(), calls=%async_computation.4 | async-start | bytes 5898240 | tf_op jit(solution)/shard_map/reduce_scatter | solution.py:292
  195.4 39.3 %collective-permute-start.17 = (bf16[2,128,512]{2,1,0:T(8,128)(2,1)S(1)}, bf16[2,128,512]{2,1,0:T(8,128)(2,1)S(1)}, u32[]{:S(2)}, u32[]{:S(2)}) collective-permute-start(bf16[2,128,512]{2,1,0:T(8,128)(2,1)S(1)} %get-tuple-element.27), channel_id=1, source_target_pairs={{0,448},{64,0},{128,64},{192,128},{256,192},{320,256},{384,320},{4... | collective-permute-start | bytes 786440 | tf_op jit(solution)/shard_map/ppermute | solution.py:26
  201.6 33.2 %collective-permute-start.16 = (bf16[2,128,512]{2,1,0:T(8,128)(2,1)S(1)}, bf16[2,128,512]{2,1,0:T(8,128)(2,1)S(1)}, u32[]{:S(2)}, u32[]{:S(2)}) collective-permute-start(bf16[2,128,512]{2,1,0:T(8,128)(2,1)S(1)} %get-tuple-element.26), channel_id=1, source_target_pairs={{0,64},{64,128},{128,192},{192,256},{256,320},{320,384},{384,448},... | collective-permute-start | bytes 786440 | tf_op jit(solution)/shard_map/ppermute | solution.py:26
  203.6 21.4 %collective-permute-start.19 = (bf16[2,128,256]{2,1,0:T(8,128)(2,1)S(1)}, bf16[2,128,256]{2,1,0:T(8,128)(2,1)S(1)}, u32[]{:S(2)}, u32[]{:S(2)}) collective-permute-start(bf16[2,128,256]{2,1,0:T(8,128)(2,1)S(1)} %rev.3), channel_id=1, source_target_pairs={{0,384},{64,448},{128,0},{192,64},{256,128},{320,192},{384,256},{4... | collective-permute-start | bytes 393224 | tf_op jit(solution)/shard_map/ppermute | solution.py:26
  210.8 24.0 %collective-permute-start.18 = (bf16[2,128,256]{2,1,0:T(8,128)(2,1)S(1)}, bf16[2,128,256]{2,1,0:T(8,128)(2,1)S(1)}, u32[]{:S(2)}, u32[]{:S(2)}) collective-permute-start(bf16[2,128,256]{2,1,0:T(8,128)(2,1)S(1)} %get-tuple-element.34), channel_id=1, source_target_pairs={{0,128},{64,192},{128,256},{192,320},{256,384},{320,448},{384,0},{... | collective-permute-start | bytes 393224 | tf_op jit(solution)/shard_map/ppermute | solution.py:26
  234.9 23.5 %collective-permute-start.20 = (bf16[128,512]{1,0:T(8,128)(2,1)S(1)}, bf16[128,512]{1,0:T(8,128)(2,1)S(1)}, u32[]{:S(2)}, u32[]{:S(2)}) collective-permute-start(bf16[128,512]{1,0:T(8,128)(2,1)S(1)} %fusion.2), channel_id=1, source_target_pairs={{0,256},{64,320},{128,384},{192,448},{256,0},{320,64},{384,128},{4... | collective-permute-start | bytes 393224 | tf_op jit(solution)/shard_map/ppermute | solution.py:26
  (10 other events, 69.5 us)
Sparse Core Ops, SparseCore 0:
  10.1 49.7 all-gather.5
  100.9 46.0 all-gather.3
  161.3 68.0 reduce-scatter.1

commit v4 on v2

--- a/solution.py
+++ b/solution.py
@@ -96,7 +96,7 @@
     parts, count, both = rows.shape
     width, cols = down.shape[1:]
     whole = lambda shape: pl.BlockSpec(shape, lambda j: (0,) * len(shape))
-    square = jax.ShapeDtypeStruct((count, width), BF16)
+    square = pltpu.HBM((count, width), BF16)
     return pl.pallas_call(
         expert_kernel,
         grid=(parts,),
@@ -106,7 +106,7 @@
             pl.BlockSpec((1, width, cols), lambda j: (j, 0, 0)),
         ],
         out_specs=[whole((parts, count, cols)), *[whole((count, width))] * 3],
-        out_shape=[jax.ShapeDtypeStruct((parts, count, cols), BF16), square, square, square],
+        out_shape=[pltpu.HBM((parts, count, cols), BF16), square, square, square],
         scratch_shapes=[pltpu.VMEM((count, width), F32)] * 3,
         compiler_params=pltpu.CompilerParams(
             dimension_semantics=("arbitrary",), vmem_limit_bytes=32 * 1024 * 1024
@@ -115,17 +115,37 @@
             flops=10 * parts * count * cols * width, bytes_accessed=11_000_000, transcendentals=count * width
         ),
     )(rows, both_in, down)
+
+
+def tokens_kernel(pick, back, out):
+    tok = out.shape[1]
+    for far in range(N_FAR):
+        group, within = divmod(far, GROUP)
+        chosen = pick[group, :, tok * within : tok * (within + 1)]
+        out[far] = dot(chosen, back[group], ((0,), (0,))).astype(BF16)
+
+
+def token_parts(pick, back):
+    tok = pick.shape[2] // GROUP
+    shape = N_FAR, tok, back.shape[2]
+    return pl.pallas_call(
+        tokens_kernel,
+        out_shape=pltpu.HBM(shape, BF16),
+        compiler_params=pltpu.CompilerParams(vmem_limit_bytes=32 * 1024 * 1024),
+        cost_estimate=pl.CostEstimate(
+            flops=2 * back.size * tok * GROUP, bytes_accessed=4_000_000, transcendentals=0
+        ),
+    )(pick, back)
 
 
 def shards(tokens, grad_out, routes, gates, w_gate, w_up, w_down):
     me_far, me_x = lax.axis_index("far"), lax.axis_index("x")
     tok, cols = tokens.shape
     both = jnp.concatenate([tokens, grad_out], axis=1)
-    w_in = jnp.concatenate([w_gate[0], w_up[0]], axis=1)
-    both, w_in, w_down = lax.optimization_barrier((both, w_in, w_down[0]))
+    both, w_gate, w_up, w_down = lax.optimization_barrier((both, w_gate[0], w_up[0], w_down[0]))
     column = lax.all_gather(both, "far", axis=0, tiled=True).reshape(N_X, GROUP * tok, 2 * cols)
     pick, row_gate = plan(routes, gates, me_far)
-    full_in = gather_x(w_in, me_x)
+    full_in = gather_x(jnp.concatenate([w_gate, w_up], axis=1), me_x)
     full_down = gather_x(w_down, me_x)
     column, full_in, full_down = lax.optimization_barrier((column, full_in, full_down))
 
@@ -142,8 +162,7 @@
     came_back = lax.all_to_all(
         row_grad.reshape(-1, slots, cols), PLANE, split_axis=0, concat_axis=0, tiled=True
     ).reshape(N_X, count, cols)
-    token_grad = dot(pick, came_back, ((1,), (1,)), ((0,), (0,))).astype(BF16)
-    d_tokens = lax.psum_scatter(token_grad.reshape(-1, cols), "far", scatter_dimension=0, tiled=True)
+    d_tokens = lax.psum_scatter(token_parts(pick, came_back), "far", scatter_dimension=0)
 
     totals = [None, None, None]
     for by in (1, 3, 2, 0):

time: 237 us -> 237 us (level)
  Pallas kernels: 6.4 us -> 11.1 us
  other arithmetic: 6.05 us -> 3.63 us
  matrix products: 15 us -> 12.6 us
    pallas_call x0 -> x1, Pallas kernels: none -> 3.26 us  [token_parts(): pl.pallas_call(tokens_kernel, out_shape=pltpu.HBM(shape, BF16), compiler_...]
    ppermute x15, waiting for transfers between devices: 21 us -> 18.1 us  [shift(): return lax.ppermute(value, 'x', [(i, (i + by) % N_X) for i in range(N_X)])]
    dot_general x15 -> x14, matrix products: 15 us -> 12.6 us  [dot(): lax.dot_general(left, right, (contract, batch), preferred_element_type=F32)]
  transfers between devices with their start and end apart: 19 -> 19, of which waited for: 9 -> 9; matrix products, arithmetic and copies ran while one was open for 13% -> 13% of each run, Pallas kernels for 0% -> 1%
where the time goes in v4:
time: 237 us; the launch traced here: 235 us
  starting transfers between devices  76.2 us (32%)
  waiting for transfers between devices  51.5 us (22%)
  blocking collectives  47.7 us (20%)
  local copies, waits for them, and re-layouts  17.5 us (7%)
  between operations  14.6 us (6%)
  matrix products  12.6 us (5%)
  Pallas kernels  11.1 us (5%)
  other arithmetic  3.63 us (2%)
    ppermute x15, starting transfers between devices, shift(): return lax.ppermute(value, 'x', [(i, (i + by) % N_X) for i in range(N_X)])  58.9 us
    all_to_all x1, blocking collectives, shards(): lax.all_to_all(rows.reshape(-1, slots, 2 * cols), PLANE, split_axis=0, co...  47.7 us
    ppermute x15, waiting for transfers between devices, shift(): return lax.ppermute(value, 'x', [(i, (i + by) % N_X) for i in range(N_X)])  18.1 us
    dot_general x14, matrix products, dot(): lax.dot_general(left, right, (contract, batch), preferred_element_type=F32)  12.6 us
    all_to_all x1, waiting for transfers between devices, shards(): lax.all_to_all(row_grad.reshape(-1, slots, cols), PLANE, split_axis=0, co...  12.3 us
    dynamic_update_slice x8, local copies, waits for them, and re-layouts, gather_x(): lax.dynamic_update_slice_in_dim(whole, piece[None], (me - by) % N_X, 0)  10.9 us
    all_to_all x1, waiting for transfers between devices, plan(): lax.all_to_all(jnp.broadcast_to(mine[None], (N_FAR,) + mine.shape), 'far'...  10.2 us
    all_to_all x1, starting transfers between devices, plan(): lax.all_to_all(jnp.broadcast_to(mine[None], (N_FAR,) + mine.shape), 'far'...  9.86 us
  transfers between devices with their start and end apart: 19, of which 9 were waited for; matrix products, arithmetic and copies ran while one was open for 13% of the time, Pallas kernels for 1%

profile of v4, /device:TPU:6, one launch (start us, length us, event | category | flops | bytes accessed | tf_op | source)
XLA Modules:
  0.0 234.9 jit_solution(1194926317920135956)
XLA Ops:
  11.6 7.7 %collective-permute-start = (bf16[512,768]{1,0:T(8,128)(2,1)}, bf16[512,768]{1,0:T(8,128)(2,1)}, u32[]{:S(2)}, u32[]{:S(2)}) collective-permute-start(bf16[512,768]{1,0:T(8,128)(2,1)} %constant_dynamic-update-slice_fusion), channel_id=1, source_target_pairs={{0,1},{1,2},{2,3},{3,0},{4,5},{5,6},{6,7},{7,4},{8,9},{9,10},{10,1... | collective-permute-start | bytes 2359304 | tf_op jit(solution)/shard_map/ppermute | solution.py:23
  21.3 2.8 %collective-permute-start.2 = (bf16[512,768]{1,0:T(8,128)(2,1)}, bf16[512,768]{1,0:T(8,128)(2,1)}, u32[]{:S(2)}, u32[]{:S(2)}) collective-permute-start(bf16[512,768]{1,0:T(8,128)(2,1)} %constant_dynamic-update-slice_fusion), channel_id=1, source_target_pairs={{0,3},{1,0},{2,1},{3,2},{4,7},{5,4},{6,5},{7,6},{8,11},{9,8},{10,9... | collective-permute-start | bytes 2359304 | tf_op jit(solution)/shard_map/ppermute | solution.py:23
  24.1 4.3 %collective-permute-start.3 = (bf16[384,512]{1,0:T(8,128)(2,1)}, bf16[384,512]{1,0:T(8,128)(2,1)}, u32[]{:S(2)}, u32[]{:S(2)}) collective-permute-start(bf16[384,512]{1,0:T(8,128)(2,1)} %bitcast.8), channel_id=1, source_target_pairs={{0,1},{1,2},{2,3},{3,0},{4,5},{5,6},{6,7},{7,4},{8,9},{9,10},{10,1... | collective-permute-start | bytes 1179656 | tf_op jit(solution)/shard_map/ppermute | solution.py:23
  28.4 4.2 %collective-permute-start.4 = (bf16[384,512]{1,0:T(8,128)(2,1)}, bf16[384,512]{1,0:T(8,128)(2,1)}, u32[]{:S(2)}, u32[]{:S(2)}) collective-permute-start(bf16[384,512]{1,0:T(8,128)(2,1)} %bitcast.8), channel_id=1, source_target_pairs={{0,2},{1,3},{2,0},{3,1},{4,6},{5,7},{6,4},{7,5},{8,10},{9,11},{10,... | collective-permute-start | bytes 1179656 | tf_op jit(solution)/shard_map/ppermute | solution.py:23
  33.3 9.9 %all-to-all-start = ((f32[8,16,128]{2,1,0:T(8,128)}), f32[8,16,128]{2,1,0:T(8,128)S(1)}, u32[]{:S(2)}, u32[]{:S(2)}) async-start(f32[8,16,128]{2,1,0:T(8,128)} %broadcast_in_dim.103), calls=%async_computation | async-start | bytes 131072 | tf_op jit(solution)/shard_map/all_to_all | solution.py:37
  47.8 10.2 %all-to-all-done = f32[8,16,128]{2,1,0:T(8,128)S(1)} async-done(((f32[8,16,128]{2,1,0:T(8,128)}), f32[8,16,128]{2,1,0:T(8,128)S(1)}, u32[]{:S(2)}, u32[]{:S(2)}) %all-to-all-start) | async-done | bytes 65568 | tf_op jit(solution)/shard_map/all_to_all | solution.py:37
  60.3 5.0 %collective-permute-start.5 = (bf16[384,512]{1,0:T(8,128)(2,1)}, bf16[384,512]{1,0:T(8,128)(2,1)S(1)}, u32[]{:S(2)}, u32[]{:S(2)}) collective-permute-start(bf16[384,512]{1,0:T(8,128)(2,1)} %bitcast.8), channel_id=1, source_target_pairs={{0,3},{1,0},{2,1},{3,2},{4,7},{5,4},{6,5},{7,6},{8,11},{9,8},{10,9... | collective-permute-start | bytes 1179656 | tf_op jit(solution)/shard_map/ppermute | solution.py:23
  68.9 3.9 %collective-permute-done.5 = bf16[384,512]{1,0:T(8,128)(2,1)S(1)} collective-permute-done((bf16[384,512]{1,0:T(8,128)(2,1)}, bf16[384,512]{1,0:T(8,128)(2,1)S(1)}, u32[]{:S(2)}, u32[]{:S(2)}) %collective-permute-start.5) | collective-permute-done | bytes 393248 | tf_op jit(solution)/shard_map/ppermute | solution.py:23
  77.3 4.2 %all-gather.2.cloned.1.call-done = bf16[1024,1024]{1,0:T(8,128)(2,1)} async-done(((bf16[128,1024]{1,0:T(8,128)(2,1)}), bf16[1024,1024]{1,0:T(8,128)(2,1)}) %all-gather.2.cloned.1.call-update) | async-done | bytes 2097168 | tf_op jit(solution)/shard_map/all_gather | solution.py:146
  84.2 47.7 %all_to_all.15 = bf16[64,24,1024]{2,1,0:T(8,128)(2,1)S(1)} all-to-all(bf16[64,24,1024]{2,1,0:T(8,128)(2,1)S(1)} %bitcast.106), channel_id=1, replica_groups=mesh['far'=8,'near'=2,'y'=4,'c'=2,'x'=4] {'x','near','y','c'}, dimensions={0} | all-to-all | bytes 6291456 | tf_op jit(solution)/shard_map/all_to_all | solution.py:157
  131.9 7.8 %shard_map.102 = (bf16[4,384,512]{2,1,0:T(8,128)(2,1)}, bf16[384,384]{1,0:T(8,128)(2,1)}, bf16[384,384]{1,0:T(8,128)(2,1)}, bf16[384,384]{1,0:T(8,128)(2,1)}) custom-call(bf16[4,384,1024]{2,1,0:T(8,128)(2,1)S(1)} %bitcast.104, bf16[4,512,768]{2,1,0:T(8,128)(2,1)S(1)} %copy-done.1, bf16[4,384,512]{2,1,0:T(8,128)(2,1)} %bitcast_dynamic-update-slice_fusion.4.down), custom_call_target="tpu_custom_call" | custom-call | flops 3019898880 | bytes 11000000 | tf_op jit(solution)/shard_map/pallas_call | solution.py:100
  139.7 7.4 %all-to-all-start.2 = ((bf16[64,24,512]{2,1,0:T(8,128)(2,1)}), bf16[64,24,512]{2,1,0:T(8,128)(2,1)}, u32[]{:S(2)}, u32[]{:S(2)}) async-start(bf16[64,24,512]{2,1,0:T(8,128)(2,1)} %bitcast.107), calls=%async_computation.2 | async-start | bytes 3145728 | tf_op jit(solution)/shard_map/all_to_all | solution.py:162
  149.8 3.1 %collective-permute-start.8 = (bf16[512,384]{1,0:T(8,128)(2,1)}, bf16[512,384]{1,0:T(8,128)(2,1)S(1)}, u32[]{:S(2)}, u32[]{:S(2)}) collective-permute-start(bf16[512,384]{1,0:T(8,128)(2,1)} %convolution_convert_fusion.9), channel_id=1, source_target_pairs={{0,2},{1,3},{2,0},{3,1},{4,6},{5,7},{6,4},{7,5},{8,10},{9,11},{10,... | collective-permute-start | bytes 1179656 | tf_op jit(solution)/shard_map/ppermute | solution.py:23
  156.1 12.3 %all-to-all-done.2 = bf16[64,24,512]{2,1,0:T(8,128)(2,1)} async-done(((bf16[64,24,512]{2,1,0:T(8,128)(2,1)}), bf16[64,24,512]{2,1,0:T(8,128)(2,1)}, u32[]{:S(2)}, u32[]{:S(2)}) %all-to-all-start.2) | async-done | bytes 1572896 | tf_op jit(solution)/shard_map/all_to_all | solution.py:162
  168.4 3.3 %shard_map.103 = bf16[8,128,512]{2,1,0:T(8,128)(2,1)} custom-call(bf16[4,384,256]{2,1,0:T(8,128)(2,1)S(1)} %copy-done.2, bf16[4,384,512]{2,1,0:T(8,128)(2,1)} %bitcast.23.back), custom_call_target="tpu_custom_call" | custom-call | flops 402653184 | bytes 4000000 | tf_op jit(solution)/shard_map/pallas_call | solution.py:131
  172.2 7.5 %collective-permute-start.14 = (bf16[384,512]{1,0:T(8,128)(2,1)S(1)}, bf16[384,512]{1,0:T(8,128)(2,1)S(1)}, u32[]{:S(2)}, u32[]{:S(2)}) collective-permute-start(bf16[384,512]{1,0:T(8,128)(2,1)S(1)} %convolution_convert_fusion.1), channel_id=1, source_target_pairs={{0,2},{1,3},{2,0},{3,1},{4,6},{5,7},{6,4},{7,5},{8,10},{9,11},{10,... | collective-permute-start | bytes 1179656 | tf_op jit(solution)/shard_map/ppermute | solution.py:23
  182.3 5.3 %collective-permute-start.12 = (bf16[384,512]{1,0:T(8,128)(2,1)S(1)}, bf16[384,512]{1,0:T(8,128)(2,1)S(1)}, u32[]{:S(2)}, u32[]{:S(2)}) collective-permute-start(bf16[384,512]{1,0:T(8,128)(2,1)S(1)} %convolution_convert_fusion.3), channel_id=1, source_target_pairs={{0,1},{1,2},{2,3},{3,0},{4,5},{5,6},{6,7},{7,4},{8,9},{9,10},{10,1... | collective-permute-start | bytes 1179656 | tf_op jit(solution)/shard_map/ppermute | solution.py:23
  191.7 4.2 %collective-permute-start.11 = (bf16[512,384]{1,0:T(8,128)(2,1)S(1)}, bf16[512,384]{1,0:T(8,128)(2,1)S(1)}, u32[]{:S(2)}, u32[]{:S(2)}) collective-permute-start(bf16[512,384]{1,0:T(8,128)(2,1)S(1)} %convolution_convert_fusion.5), channel_id=1, source_target_pairs={{0,2},{1,3},{2,0},{3,1},{4,6},{5,7},{6,4},{7,5},{8,10},{9,11},{10,... | collective-permute-start | bytes 1179656 | tf_op jit(solution)/shard_map/ppermute | solution.py:23
  195.9 3.6 %collective-permute-done.13 = bf16[384,512]{1,0:T(8,128)(2,1)S(1)} collective-permute-done((bf16[384,512]{1,0:T(8,128)(2,1)S(1)}, bf16[384,512]{1,0:T(8,128)(2,1)S(1)}, u32[]{:S(2)}, u32[]{:S(2)}) %collective-permute-start.13) | collective-permute-done | bytes 393248 | tf_op jit(solution)/shard_map/ppermute | solution.py:23
  199.5 3.3 %collective-permute-start.10 = (bf16[512,384]{1,0:T(8,128)(2,1)S(1)}, bf16[512,384]{1,0:T(8,128)(2,1)S(1)}, u32[]{:S(2)}, u32[]{:S(2)}) collective-permute-start(bf16[512,384]{1,0:T(8,128)(2,1)S(1)} %convolution_convert_fusion.6), channel_id=1, source_target_pairs={{0,3},{1,0},{2,1},{3,2},{4,7},{5,4},{6,5},{7,6},{8,11},{9,8},{10,9... | collective-permute-start | bytes 1179656 | tf_op jit(solution)/shard_map/ppermute | solution.py:23
  202.8 3.7 %collective-permute-start.9 = (bf16[512,384]{1,0:T(8,128)(2,1)S(1)}, bf16[512,384]{1,0:T(8,128)(2,1)S(1)}, u32[]{:S(2)}, u32[]{:S(2)}) collective-permute-start(bf16[512,384]{1,0:T(8,128)(2,1)S(1)} %convolution_convert_fusion.7), channel_id=1, source_target_pairs={{0,1},{1,2},{2,3},{3,0},{4,5},{5,6},{6,7},{7,4},{8,9},{9,10},{10,1... | collective-permute-start | bytes 1179656 | tf_op jit(solution)/shard_map/ppermute | solution.py:23
  209.9 6.6 %collective-permute-done.10 = bf16[512,384]{1,0:T(8,128)(2,1)S(1)} collective-permute-done((bf16[512,384]{1,0:T(8,128)(2,1)S(1)}, bf16[512,384]{1,0:T(8,128)(2,1)S(1)}, u32[]{:S(2)}, u32[]{:S(2)}) %collective-permute-start.10) | collective-permute-done | bytes 393248 | tf_op jit(solution)/shard_map/ppermute | solution.py:23
  216.5 3.7 %collective-permute-done.9 = bf16[512,384]{1,0:T(8,128)(2,1)S(1)} collective-permute-done((bf16[512,384]{1,0:T(8,128)(2,1)S(1)}, bf16[512,384]{1,0:T(8,128)(2,1)S(1)}, u32[]{:S(2)}, u32[]{:S(2)}) %collective-permute-start.9) | collective-permute-done | bytes 393248 | tf_op jit(solution)/shard_map/ppermute | solution.py:23
  221.4 6.7 %reduce-scatter.2.cloned.1.call-done = bf16[1,128,512]{2,1,0:T(8,128)(2,1)} async-done(((bf16[8,128,512]{2,1,0:T(8,128)(2,1)}), bf16[1,128,512]{2,1,0:T(8,128)(2,1)}) %reduce-scatter.2.cloned.1.call-update) | async-done | bytes 131088 | tf_op jit(solution)/shard_map/reduce_scatter | solution.py:165
  (90 shorter events, 41.8 us)
Async XLA Ops:
  7.2 25.4 %copy-start.11 = (s32[128,8]{0,1:T(8,128)S(1)}, s32[128,8]{0,1:T(8,128)}, u32[]{:S(2)}) copy-start(s32[128,8]{0,1:T(8,128)} %param.9) | copy-start | bytes 12292
  7.2 25.4 %copy-start.12 = (f32[128,8]{0,1:T(8,128)S(1)}, f32[128,8]{0,1:T(8,128)}, u32[]{:S(2)}) copy-start(f32[128,8]{0,1:T(8,128)} %param.10) | copy-start | bytes 12292
  7.2 74.3 %all-gather.2.cloned.1.call-start = ((), (), s32[]{:S(2)}) async-start(), calls=%async_computation.4 | async-start | bytes 2359296 | tf_op jit(solution)/shard_map/all_gather | solution.py:146
  11.6 62.0 %collective-permute-start = (bf16[512,768]{1,0:T(8,128)(2,1)}, bf16[512,768]{1,0:T(8,128)(2,1)}, u32[]{:S(2)}, u32[]{:S(2)}) collective-permute-start(bf16[512,768]{1,0:T(8,128)(2,1)} %constant_dynamic-update-slice_fusion), channel_id=1, source_target_pairs={{0,1},{1,2},{2,3},{3,0},{4,5},{5,6},{6,7},{7,4},{8,9},{9,10},{10,1... | collective-permute-start | bytes 2359304 | tf_op jit(solution)/shard_map/ppermute | solution.py:23
  19.4 55.4 %collective-permute-start.1 = (bf16[512,768]{1,0:T(8,128)(2,1)}, bf16[512,768]{1,0:T(8,128)(2,1)}, u32[]{:S(2)}, u32[]{:S(2)}) collective-permute-start(bf16[512,768]{1,0:T(8,128)(2,1)} %constant_dynamic-update-slice_fusion), channel_id=1, source_target_pairs={{0,2},{1,3},{2,0},{3,1},{4,6},{5,7},{6,4},{7,5},{8,10},{9,11},{10,... | collective-permute-start | bytes 2359304 | tf_op jit(solution)/shard_map/ppermute | solution.py:23
  21.3 54.8 %collective-permute-start.2 = (bf16[512,768]{1,0:T(8,128)(2,1)}, bf16[512,768]{1,0:T(8,128)(2,1)}, u32[]{:S(2)}, u32[]{:S(2)}) collective-permute-start(bf16[512,768]{1,0:T(8,128)(2,1)} %constant_dynamic-update-slice_fusion), channel_id=1, source_target_pairs={{0,3},{1,0},{2,1},{3,2},{4,7},{5,4},{6,5},{7,6},{8,11},{9,8},{10,9... | collective-permute-start | bytes 2359304 | tf_op jit(solution)/shard_map/ppermute | solution.py:23
  24.1 36.2 %collective-permute-start.3 = (bf16[384,512]{1,0:T(8,128)(2,1)}, bf16[384,512]{1,0:T(8,128)(2,1)}, u32[]{:S(2)}, u32[]{:S(2)}) collective-permute-start(bf16[384,512]{1,0:T(8,128)(2,1)} %bitcast.8), channel_id=1, source_target_pairs={{0,1},{1,2},{2,3},{3,0},{4,5},{5,6},{6,7},{7,4},{8,9},{9,10},{10,1... | collective-permute-start | bytes 1179656 | tf_op jit(solution)/shard_map/ppermute | solution.py:23
  28.4 38.7 %collective-permute-start.4 = (bf16[384,512]{1,0:T(8,128)(2,1)}, bf16[384,512]{1,0:T(8,128)(2,1)}, u32[]{:S(2)}, u32[]{:S(2)}) collective-permute-start(bf16[384,512]{1,0:T(8,128)(2,1)} %bitcast.8), channel_id=1, source_target_pairs={{0,2},{1,3},{2,0},{3,1},{4,6},{5,7},{6,4},{7,5},{8,10},{9,11},{10,... | collective-permute-start | bytes 1179656 | tf_op jit(solution)/shard_map/ppermute | solution.py:23
  33.3 24.8 %all-to-all-start = ((f32[8,16,128]{2,1,0:T(8,128)}), f32[8,16,128]{2,1,0:T(8,128)S(1)}, u32[]{:S(2)}, u32[]{:S(2)}) async-start(f32[8,16,128]{2,1,0:T(8,128)} %broadcast_in_dim.103), calls=%async_computation | async-start | bytes 131072 | tf_op jit(solution)/shard_map/all_to_all | solution.py:37
  60.3 12.5 %collective-permute-start.5 = (bf16[384,512]{1,0:T(8,128)(2,1)}, bf16[384,512]{1,0:T(8,128)(2,1)S(1)}, u32[]{:S(2)}, u32[]{:S(2)}) collective-permute-start(bf16[384,512]{1,0:T(8,128)(2,1)} %bitcast.8), channel_id=1, source_target_pairs={{0,3},{1,0},{2,1},{3,2},{4,7},{5,4},{6,5},{7,6},{8,11},{9,8},{10,9... | collective-permute-start | bytes 1179656 | tf_op jit(solution)/shard_map/ppermute | solution.py:23
  84.2 47.7 %copy-start.1 = (bf16[4,512,768]{2,1,0:T(8,128)(2,1)S(1)}, bf16[4,512,768]{2,1,0:T(8,128)(2,1)}, u32[]{:S(2)}) copy-start(bf16[4,512,768]{2,1,0:T(8,128)(2,1)} %copy-done) | copy-start | bytes 9437188
  139.7 28.7 %all-to-all-start.2 = ((bf16[64,24,512]{2,1,0:T(8,128)(2,1)}), bf16[64,24,512]{2,1,0:T(8,128)(2,1)}, u32[]{:S(2)}, u32[]{:S(2)}) async-start(bf16[64,24,512]{2,1,0:T(8,128)(2,1)} %bitcast.107), calls=%async_computation.2 | async-start | bytes 3145728 | tf_op jit(solution)/shard_map/all_to_all | solution.py:162
  147.1 80.9 %reduce-scatter.2.cloned.1.call-start = ((), (), s32[]{:S(2)}) async-start(), calls=%async_computation.5 | async-start | bytes 1179648 | tf_op jit(solution)/shard_map/reduce_scatter | solution.py:165
  148.6 19.8 %copy-start.2 = (bf16[4,384,256]{2,1,0:T(8,128)(2,1)S(1)}, bf16[4,384,256]{2,1,0:T(8,128)(2,1)}, u32[]{:S(2)}) copy-start(bf16[4,384,256]{2,1,0:T(8,128)(2,1)} %get-tuple-element.31.pick) | copy-start | bytes 2359300
  149.8 39.2 %collective-permute-start.8 = (bf16[512,384]{1,0:T(8,128)(2,1)}, bf16[512,384]{1,0:T(8,128)(2,1)S(1)}, u32[]{:S(2)}, u32[]{:S(2)}) collective-permute-start(bf16[512,384]{1,0:T(8,128)(2,1)} %convolution_convert_fusion.9), channel_id=1, source_target_pairs={{0,2},{1,3},{2,0},{3,1},{4,6},{5,7},{6,4},{7,5},{8,10},{9,11},{10,... | collective-permute-start | bytes 1179656 | tf_op jit(solution)/shard_map/ppermute | solution.py:23
  154.2 53.5 %collective-permute-start.7 = (bf16[512,384]{1,0:T(8,128)(2,1)}, bf16[512,384]{1,0:T(8,128)(2,1)}, u32[]{:S(2)}, u32[]{:S(2)}) collective-permute-start(bf16[512,384]{1,0:T(8,128)(2,1)} %convolution_convert_fusion.10), channel_id=1, source_target_pairs={{0,3},{1,0},{2,1},{3,2},{4,7},{5,4},{6,5},{7,6},{8,11},{9,8},{10,9... | collective-permute-start | bytes 1179656 | tf_op jit(solution)/shard_map/ppermute | solution.py:23
  172.1 16.0 %copy-start.6 = (bf16[384,384]{1,0:T(8,128)(2,1)S(1)}, bf16[384,384]{1,0:T(8,128)(2,1)}, u32[]{:S(2)}) copy-start(bf16[384,384]{1,0:T(8,128)(2,1)} %get-tuple-element.24) | copy-start | bytes 884740
  172.2 19.5 %collective-permute-start.14 = (bf16[384,512]{1,0:T(8,128)(2,1)S(1)}, bf16[384,512]{1,0:T(8,128)(2,1)S(1)}, u32[]{:S(2)}, u32[]{:S(2)}) collective-permute-start(bf16[384,512]{1,0:T(8,128)(2,1)S(1)} %convolution_convert_fusion.1), channel_id=1, source_target_pairs={{0,2},{1,3},{2,0},{3,1},{4,6},{5,7},{6,4},{7,5},{8,10},{9,11},{10,... | collective-permute-start | bytes 1179656 | tf_op jit(solution)/shard_map/ppermute | solution.py:23
  180.0 19.5 %collective-permute-start.13 = (bf16[384,512]{1,0:T(8,128)(2,1)S(1)}, bf16[384,512]{1,0:T(8,128)(2,1)S(1)}, u32[]{:S(2)}, u32[]{:S(2)}) collective-permute-start(bf16[384,512]{1,0:T(8,128)(2,1)S(1)} %convolution_convert_fusion.2), channel_id=1, source_target_pairs={{0,3},{1,0},{2,1},{3,2},{4,7},{5,4},{6,5},{7,6},{8,11},{9,8},{10,9... | collective-permute-start | bytes 1179656 | tf_op jit(solution)/shard_map/ppermute | solution.py:23
  182.3 20.5 %collective-permute-start.12 = (bf16[384,512]{1,0:T(8,128)(2,1)S(1)}, bf16[384,512]{1,0:T(8,128)(2,1)S(1)}, u32[]{:S(2)}, u32[]{:S(2)}) collective-permute-start(bf16[384,512]{1,0:T(8,128)(2,1)S(1)} %convolution_convert_fusion.3), channel_id=1, source_target_pairs={{0,1},{1,2},{2,3},{3,0},{4,5},{5,6},{6,7},{7,4},{8,9},{9,10},{10,1... | collective-permute-start | bytes 1179656 | tf_op jit(solution)/shard_map/ppermute | solution.py:23
  189.1 18.6 %collective-permute-start.6 = (bf16[512,384]{1,0:T(8,128)(2,1)S(1)}, bf16[512,384]{1,0:T(8,128)(2,1)S(1)}, u32[]{:S(2)}, u32[]{:S(2)}) collective-permute-start(bf16[512,384]{1,0:T(8,128)(2,1)S(1)} %convolution_convert_fusion.11), channel_id=1, source_target_pairs={{0,1},{1,2},{2,3},{3,0},{4,5},{5,6},{6,7},{7,4},{8,9},{9,10},{10,1... | collective-permute-start | bytes 1179656 | tf_op jit(solution)/shard_map/ppermute | solution.py:23
  191.7 18.2 %collective-permute-start.11 = (bf16[512,384]{1,0:T(8,128)(2,1)S(1)}, bf16[512,384]{1,0:T(8,128)(2,1)S(1)}, u32[]{:S(2)}, u32[]{:S(2)}) collective-permute-start(bf16[512,384]{1,0:T(8,128)(2,1)S(1)} %convolution_convert_fusion.5), channel_id=1, source_target_pairs={{0,2},{1,3},{2,0},{3,1},{4,6},{5,7},{6,4},{7,5},{8,10},{9,11},{10,... | collective-permute-start | bytes 1179656 | tf_op jit(solution)/shard_map/ppermute | solution.py:23
  199.5 17.0 %collective-permute-start.10 = (bf16[512,384]{1,0:T(8,128)(2,1)S(1)}, bf16[512,384]{1,0:T(8,128)(2,1)S(1)}, u32[]{:S(2)}, u32[]{:S(2)}) collective-permute-start(bf16[512,384]{1,0:T(8,128)(2,1)S(1)} %convolution_convert_fusion.6), channel_id=1, source_target_pairs={{0,3},{1,0},{2,1},{3,2},{4,7},{5,4},{6,5},{7,6},{8,11},{9,8},{10,9... | collective-permute-start | bytes 1179656 | tf_op jit(solution)/shard_map/ppermute | solution.py:23
  202.8 17.4 %collective-permute-start.9 = (bf16[512,384]{1,0:T(8,128)(2,1)S(1)}, bf16[512,384]{1,0:T(8,128)(2,1)S(1)}, u32[]{:S(2)}, u32[]{:S(2)}) collective-permute-start(bf16[512,384]{1,0:T(8,128)(2,1)S(1)} %convolution_convert_fusion.7), channel_id=1, source_target_pairs={{0,1},{1,2},{2,3},{3,0},{4,5},{5,6},{6,7},{7,4},{8,9},{9,10},{10,1... | collective-permute-start | bytes 1179656 | tf_op jit(solution)/shard_map/ppermute | solution.py:23
  (8 other events, 45.5 us)
Sparse Core Ops, SparseCore 0:
  10.7 70.8 all-gather.1
  171.8 56.1 reduce-scatter.1

commit v5 on v4

--- a/solution.py
+++ b/solution.py
@@ -119,21 +119,26 @@
 
 def tokens_kernel(pick, back, out):
     tok = out.shape[1]
-    for far in range(N_FAR):
-        group, within = divmod(far, GROUP)
-        chosen = pick[group, :, tok * within : tok * (within + 1)]
-        out[far] = dot(chosen, back[group], ((0,), (0,))).astype(BF16)
+    for u in range(GROUP):
+        chosen = pick[0, :, tok * u : tok * (u + 1)]
+        out[u] = dot(chosen, back[0], ((0,), (0,))).astype(BF16)
 
 
 def token_parts(pick, back):
-    tok = pick.shape[2] // GROUP
-    shape = N_FAR, tok, back.shape[2]
+    groups, count, toks = pick.shape
+    cols = back.shape[2]
+    grouped = lambda *shape: pl.BlockSpec(shape, lambda i: (i, 0, 0))
     return pl.pallas_call(
         tokens_kernel,
-        out_shape=pltpu.HBM(shape, BF16),
-        compiler_params=pltpu.CompilerParams(vmem_limit_bytes=32 * 1024 * 1024),
+        grid=(groups,),
+        in_specs=[grouped(1, count, toks), grouped(1, count, cols)],
+        out_specs=grouped(GROUP, toks // GROUP, cols),
+        out_shape=pltpu.HBM((N_FAR, toks // GROUP, cols), BF16),
+        compiler_params=pltpu.CompilerParams(
+            dimension_semantics=("arbitrary",), vmem_limit_bytes=32 * 1024 * 1024
+        ),
         cost_estimate=pl.CostEstimate(
-            flops=2 * back.size * tok * GROUP, bytes_accessed=4_000_000, transcendentals=0
+            flops=2 * back.size * toks, bytes_accessed=4_000_000, transcendentals=0
         ),
     )(pick, back)
 

time: 237 us -> 237 us (level)
  transfers between devices with their start and end apart: 19 -> 19, of which waited for: 9 -> 8; matrix products, arithmetic and copies ran while one was open for 13% -> 12% of each run, Pallas kernels for 1% -> 2%
where the time goes in v5:
time: 237 us; the launch traced here: 236 us
  starting transfers between devices  75.6 us (32%)
  waiting for transfers between devices  52 us (22%)
  blocking collectives  47.7 us (20%)
  local copies, waits for them, and re-layouts  17.5 us (7%)
  between operations  14.6 us (6%)
  matrix products  12.6 us (5%)
  Pallas kernels  12.1 us (5%)
  other arithmetic  3.63 us (2%)
    ppermute x15, starting transfers between devices, shift(): return lax.ppermute(value, 'x', [(i, (i + by) % N_X) for i in range(N_X)])  58.3 us
    all_to_all x1, blocking collectives, shards(): lax.all_to_all(rows.reshape(-1, slots, 2 * cols), PLANE, split_axis=0, co...  47.7 us
    ppermute x15, waiting for transfers between devices, shift(): return lax.ppermute(value, 'x', [(i, (i + by) % N_X) for i in range(N_X)])  18.6 us
    dot_general x14, matrix products, dot(): lax.dot_general(left, right, (contract, batch), preferred_element_type=F32)  12.6 us
    all_to_all x1, waiting for transfers between devices, shards(): lax.all_to_all(row_grad.reshape(-1, slots, cols), PLANE, split_axis=0, co...  12.3 us
    dynamic_update_slice x8, local copies, waits for them, and re-layouts, gather_x(): lax.dynamic_update_slice_in_dim(whole, piece[None], (me - by) % N_X, 0)  10.9 us
    all_to_all x1, waiting for transfers between devices, plan(): lax.all_to_all(jnp.broadcast_to(mine[None], (N_FAR,) + mine.shape), 'far'...  10.2 us
    all_to_all x1, starting transfers between devices, plan(): lax.all_to_all(jnp.broadcast_to(mine[None], (N_FAR,) + mine.shape), 'far'...  9.86 us
  transfers between devices with their start and end apart: 19, of which 8 were waited for; matrix products, arithmetic and copies ran while one was open for 12% of the time, Pallas kernels for 2%

profile of v5, /device:TPU:6, one launch (start us, length us, event | category | flops | bytes accessed | tf_op | source)
XLA Modules:
  0.0 235.7 jit_solution(10246237270900106587)
XLA Ops:
  11.6 7.7 %collective-permute-start = (bf16[512,768]{1,0:T(8,128)(2,1)}, bf16[512,768]{1,0:T(8,128)(2,1)}, u32[]{:S(2)}, u32[]{:S(2)}) collective-permute-start(bf16[512,768]{1,0:T(8,128)(2,1)} %constant_dynamic-update-slice_fusion), channel_id=1, source_target_pairs={{0,1},{1,2},{2,3},{3,0},{4,5},{5,6},{6,7},{7,4},{8,9},{9,10},{10,1... | collective-permute-start | bytes 2359304 | tf_op jit(solution)/shard_map/ppermute | solution.py:23
  21.3 2.8 %collective-permute-start.2 = (bf16[512,768]{1,0:T(8,128)(2,1)}, bf16[512,768]{1,0:T(8,128)(2,1)}, u32[]{:S(2)}, u32[]{:S(2)}) collective-permute-start(bf16[512,768]{1,0:T(8,128)(2,1)} %constant_dynamic-update-slice_fusion), channel_id=1, source_target_pairs={{0,3},{1,0},{2,1},{3,2},{4,7},{5,4},{6,5},{7,6},{8,11},{9,8},{10,9... | collective-permute-start | bytes 2359304 | tf_op jit(solution)/shard_map/ppermute | solution.py:23
  24.1 4.3 %collective-permute-start.3 = (bf16[384,512]{1,0:T(8,128)(2,1)}, bf16[384,512]{1,0:T(8,128)(2,1)}, u32[]{:S(2)}, u32[]{:S(2)}) collective-permute-start(bf16[384,512]{1,0:T(8,128)(2,1)} %bitcast.8), channel_id=1, source_target_pairs={{0,1},{1,2},{2,3},{3,0},{4,5},{5,6},{6,7},{7,4},{8,9},{9,10},{10,1... | collective-permute-start | bytes 1179656 | tf_op jit(solution)/shard_map/ppermute | solution.py:23
  28.4 4.2 %collective-permute-start.4 = (bf16[384,512]{1,0:T(8,128)(2,1)}, bf16[384,512]{1,0:T(8,128)(2,1)}, u32[]{:S(2)}, u32[]{:S(2)}) collective-permute-start(bf16[384,512]{1,0:T(8,128)(2,1)} %bitcast.8), channel_id=1, source_target_pairs={{0,2},{1,3},{2,0},{3,1},{4,6},{5,7},{6,4},{7,5},{8,10},{9,11},{10,... | collective-permute-start | bytes 1179656 | tf_op jit(solution)/shard_map/ppermute | solution.py:23
  33.3 9.9 %all-to-all-start = ((f32[8,16,128]{2,1,0:T(8,128)}), f32[8,16,128]{2,1,0:T(8,128)S(1)}, u32[]{:S(2)}, u32[]{:S(2)}) async-start(f32[8,16,128]{2,1,0:T(8,128)} %broadcast_in_dim.103), calls=%async_computation | async-start | bytes 131072 | tf_op jit(solution)/shard_map/all_to_all | solution.py:37
  47.8 10.2 %all-to-all-done = f32[8,16,128]{2,1,0:T(8,128)S(1)} async-done(((f32[8,16,128]{2,1,0:T(8,128)}), f32[8,16,128]{2,1,0:T(8,128)S(1)}, u32[]{:S(2)}, u32[]{:S(2)}) %all-to-all-start) | async-done | bytes 65568 | tf_op jit(solution)/shard_map/all_to_all | solution.py:37
  60.3 5.0 %collective-permute-start.5 = (bf16[384,512]{1,0:T(8,128)(2,1)}, bf16[384,512]{1,0:T(8,128)(2,1)S(1)}, u32[]{:S(2)}, u32[]{:S(2)}) collective-permute-start(bf16[384,512]{1,0:T(8,128)(2,1)} %bitcast.8), channel_id=1, source_target_pairs={{0,3},{1,0},{2,1},{3,2},{4,7},{5,4},{6,5},{7,6},{8,11},{9,8},{10,9... | collective-permute-start | bytes 1179656 | tf_op jit(solution)/shard_map/ppermute | solution.py:23
  68.9 3.9 %collective-permute-done.5 = bf16[384,512]{1,0:T(8,128)(2,1)S(1)} collective-permute-done((bf16[384,512]{1,0:T(8,128)(2,1)}, bf16[384,512]{1,0:T(8,128)(2,1)S(1)}, u32[]{:S(2)}, u32[]{:S(2)}) %collective-permute-start.5) | collective-permute-done | bytes 393248 | tf_op jit(solution)/shard_map/ppermute | solution.py:23
  77.3 4.2 %all-gather.2.cloned.1.call-done = bf16[1024,1024]{1,0:T(8,128)(2,1)} async-done(((bf16[128,1024]{1,0:T(8,128)(2,1)}), bf16[1024,1024]{1,0:T(8,128)(2,1)}) %all-gather.2.cloned.1.call-update) | async-done | bytes 2097168 | tf_op jit(solution)/shard_map/all_gather | solution.py:151
  84.2 47.7 %all_to_all.15 = bf16[64,24,1024]{2,1,0:T(8,128)(2,1)S(1)} all-to-all(bf16[64,24,1024]{2,1,0:T(8,128)(2,1)S(1)} %bitcast.106), channel_id=1, replica_groups=mesh['far'=8,'near'=2,'y'=4,'c'=2,'x'=4] {'x','near','y','c'}, dimensions={0} | all-to-all | bytes 6291456 | tf_op jit(solution)/shard_map/all_to_all | solution.py:162
  131.9 7.8 %shard_map.102 = (bf16[4,384,512]{2,1,0:T(8,128)(2,1)}, bf16[384,384]{1,0:T(8,128)(2,1)}, bf16[384,384]{1,0:T(8,128)(2,1)}, bf16[384,384]{1,0:T(8,128)(2,1)}) custom-call(bf16[4,384,1024]{2,1,0:T(8,128)(2,1)S(1)} %bitcast.104, bf16[4,512,768]{2,1,0:T(8,128)(2,1)S(1)} %copy-done.1, bf16[4,384,512]{2,1,0:T(8,128)(2,1)} %bitcast_dynamic-update-slice_fusion.4.down), custom_call_target="tpu_custom_call" | custom-call | flops 3019898880 | bytes 11000000 | tf_op jit(solution)/shard_map/pallas_call | solution.py:100
  139.7 7.4 %all-to-all-start.2 = ((bf16[64,24,512]{2,1,0:T(8,128)(2,1)}), bf16[64,24,512]{2,1,0:T(8,128)(2,1)}, u32[]{:S(2)}, u32[]{:S(2)}) async-start(bf16[64,24,512]{2,1,0:T(8,128)(2,1)} %bitcast.107), calls=%async_computation.2 | async-start | bytes 3145728 | tf_op jit(solution)/shard_map/all_to_all | solution.py:167
  149.8 3.1 %collective-permute-start.8 = (bf16[512,384]{1,0:T(8,128)(2,1)}, bf16[512,384]{1,0:T(8,128)(2,1)S(1)}, u32[]{:S(2)}, u32[]{:S(2)}) collective-permute-start(bf16[512,384]{1,0:T(8,128)(2,1)} %convolution_convert_fusion.9), channel_id=1, source_target_pairs={{0,2},{1,3},{2,0},{3,1},{4,6},{5,7},{6,4},{7,5},{8,10},{9,11},{10,... | collective-permute-start | bytes 1179656 | tf_op jit(solution)/shard_map/ppermute | solution.py:23
  156.1 12.3 %all-to-all-done.2 = bf16[64,24,512]{2,1,0:T(8,128)(2,1)} async-done(((bf16[64,24,512]{2,1,0:T(8,128)(2,1)}), bf16[64,24,512]{2,1,0:T(8,128)(2,1)}, u32[]{:S(2)}, u32[]{:S(2)}) %all-to-all-start.2) | async-done | bytes 1572896 | tf_op jit(solution)/shard_map/all_to_all | solution.py:167
  168.4 4.3 %shard_map.103 = bf16[8,128,512]{2,1,0:T(8,128)(2,1)} custom-call(bf16[4,384,256]{2,1,0:T(8,128)(2,1)S(1)} %copy-done.2, bf16[4,384,512]{2,1,0:T(8,128)(2,1)} %bitcast.23.back), custom_call_target="tpu_custom_call" | custom-call | flops 402653184 | bytes 4000000 | tf_op jit(solution)/shard_map/pallas_call | solution.py:131
  173.1 7.5 %collective-permute-start.14 = (bf16[384,512]{1,0:T(8,128)(2,1)S(1)}, bf16[384,512]{1,0:T(8,128)(2,1)S(1)}, u32[]{:S(2)}, u32[]{:S(2)}) collective-permute-start(bf16[384,512]{1,0:T(8,128)(2,1)S(1)} %convolution_convert_fusion.1), channel_id=1, source_target_pairs={{0,2},{1,3},{2,0},{3,1},{4,6},{5,7},{6,4},{7,5},{8,10},{9,11},{10,... | collective-permute-start | bytes 1179656 | tf_op jit(solution)/shard_map/ppermute | solution.py:23
  183.3 5.3 %collective-permute-start.12 = (bf16[384,512]{1,0:T(8,128)(2,1)S(1)}, bf16[384,512]{1,0:T(8,128)(2,1)S(1)}, u32[]{:S(2)}, u32[]{:S(2)}) collective-permute-start(bf16[384,512]{1,0:T(8,128)(2,1)S(1)} %convolution_convert_fusion.3), channel_id=1, source_target_pairs={{0,1},{1,2},{2,3},{3,0},{4,5},{5,6},{6,7},{7,4},{8,9},{9,10},{10,1... | collective-permute-start | bytes 1179656 | tf_op jit(solution)/shard_map/ppermute | solution.py:23
  192.5 3.6 %collective-permute-start.11 = (bf16[512,384]{1,0:T(8,128)(2,1)S(1)}, bf16[512,384]{1,0:T(8,128)(2,1)S(1)}, u32[]{:S(2)}, u32[]{:S(2)}) collective-permute-start(bf16[512,384]{1,0:T(8,128)(2,1)S(1)} %convolution_convert_fusion.5), channel_id=1, source_target_pairs={{0,2},{1,3},{2,0},{3,1},{4,6},{5,7},{6,4},{7,5},{8,10},{9,11},{10,... | collective-permute-start | bytes 1179656 | tf_op jit(solution)/shard_map/ppermute | solution.py:23
  196.1 3.9 %collective-permute-done.13 = bf16[384,512]{1,0:T(8,128)(2,1)S(1)} collective-permute-done((bf16[384,512]{1,0:T(8,128)(2,1)S(1)}, bf16[384,512]{1,0:T(8,128)(2,1)S(1)}, u32[]{:S(2)}, u32[]{:S(2)}) %collective-permute-start.13) | collective-permute-done | bytes 393248 | tf_op jit(solution)/shard_map/ppermute | solution.py:23
  200.0 3.0 %collective-permute-start.10 = (bf16[512,384]{1,0:T(8,128)(2,1)S(1)}, bf16[512,384]{1,0:T(8,128)(2,1)S(1)}, u32[]{:S(2)}, u32[]{:S(2)}) collective-permute-start(bf16[512,384]{1,0:T(8,128)(2,1)S(1)} %convolution_convert_fusion.6), channel_id=1, source_target_pairs={{0,3},{1,0},{2,1},{3,2},{4,7},{5,4},{6,5},{7,6},{8,11},{9,8},{10,9... | collective-permute-start | bytes 1179656 | tf_op jit(solution)/shard_map/ppermute | solution.py:23
  203.0 4.0 %collective-permute-start.9 = (bf16[512,384]{1,0:T(8,128)(2,1)S(1)}, bf16[512,384]{1,0:T(8,128)(2,1)S(1)}, u32[]{:S(2)}, u32[]{:S(2)}) collective-permute-start(bf16[512,384]{1,0:T(8,128)(2,1)S(1)} %convolution_convert_fusion.7), channel_id=1, source_target_pairs={{0,1},{1,2},{2,3},{3,0},{4,5},{5,6},{6,7},{7,4},{8,9},{9,10},{10,1... | collective-permute-start | bytes 1179656 | tf_op jit(solution)/shard_map/ppermute | solution.py:23
  210.4 6.0 %collective-permute-done.10 = bf16[512,384]{1,0:T(8,128)(2,1)S(1)} collective-permute-done((bf16[512,384]{1,0:T(8,128)(2,1)S(1)}, bf16[512,384]{1,0:T(8,128)(2,1)S(1)}, u32[]{:S(2)}, u32[]{:S(2)}) %collective-permute-start.10) | collective-permute-done | bytes 393248 | tf_op jit(solution)/shard_map/ppermute | solution.py:23
  216.5 4.7 %collective-permute-done.9 = bf16[512,384]{1,0:T(8,128)(2,1)S(1)} collective-permute-done((bf16[512,384]{1,0:T(8,128)(2,1)S(1)}, bf16[512,384]{1,0:T(8,128)(2,1)S(1)}, u32[]{:S(2)}, u32[]{:S(2)}) %collective-permute-start.9) | collective-permute-done | bytes 393248 | tf_op jit(solution)/shard_map/ppermute | solution.py:23
  222.4 6.5 %reduce-scatter.2.cloned.1.call-done = bf16[1,128,512]{2,1,0:T(8,128)(2,1)} async-done(((bf16[8,128,512]{2,1,0:T(8,128)(2,1)}), bf16[1,128,512]{2,1,0:T(8,128)(2,1)}) %reduce-scatter.2.cloned.1.call-update) | async-done | bytes 131088 | tf_op jit(solution)/shard_map/reduce_scatter | solution.py:170
  (90 shorter events, 41.6 us)
Async XLA Ops:
  7.2 25.4 %copy-start.11 = (s32[128,8]{0,1:T(8,128)S(1)}, s32[128,8]{0,1:T(8,128)}, u32[]{:S(2)}) copy-start(s32[128,8]{0,1:T(8,128)} %param.9) | copy-start | bytes 12292
  7.2 25.4 %copy-start.12 = (f32[128,8]{0,1:T(8,128)S(1)}, f32[128,8]{0,1:T(8,128)}, u32[]{:S(2)}) copy-start(f32[128,8]{0,1:T(8,128)} %param.10) | copy-start | bytes 12292
  7.2 74.3 %all-gather.2.cloned.1.call-start = ((), (), s32[]{:S(2)}) async-start(), calls=%async_computation.4 | async-start | bytes 2359296 | tf_op jit(solution)/shard_map/all_gather | solution.py:151
  11.6 62.0 %collective-permute-start = (bf16[512,768]{1,0:T(8,128)(2,1)}, bf16[512,768]{1,0:T(8,128)(2,1)}, u32[]{:S(2)}, u32[]{:S(2)}) collective-permute-start(bf16[512,768]{1,0:T(8,128)(2,1)} %constant_dynamic-update-slice_fusion), channel_id=1, source_target_pairs={{0,1},{1,2},{2,3},{3,0},{4,5},{5,6},{6,7},{7,4},{8,9},{9,10},{10,1... | collective-permute-start | bytes 2359304 | tf_op jit(solution)/shard_map/ppermute | solution.py:23
  19.4 55.4 %collective-permute-start.1 = (bf16[512,768]{1,0:T(8,128)(2,1)}, bf16[512,768]{1,0:T(8,128)(2,1)}, u32[]{:S(2)}, u32[]{:S(2)}) collective-permute-start(bf16[512,768]{1,0:T(8,128)(2,1)} %constant_dynamic-update-slice_fusion), channel_id=1, source_target_pairs={{0,2},{1,3},{2,0},{3,1},{4,6},{5,7},{6,4},{7,5},{8,10},{9,11},{10,... | collective-permute-start | bytes 2359304 | tf_op jit(solution)/shard_map/ppermute | solution.py:23
  21.3 54.8 %collective-permute-start.2 = (bf16[512,768]{1,0:T(8,128)(2,1)}, bf16[512,768]{1,0:T(8,128)(2,1)}, u32[]{:S(2)}, u32[]{:S(2)}) collective-permute-start(bf16[512,768]{1,0:T(8,128)(2,1)} %constant_dynamic-update-slice_fusion), channel_id=1, source_target_pairs={{0,3},{1,0},{2,1},{3,2},{4,7},{5,4},{6,5},{7,6},{8,11},{9,8},{10,9... | collective-permute-start | bytes 2359304 | tf_op jit(solution)/shard_map/ppermute | solution.py:23
  24.1 36.2 %collective-permute-start.3 = (bf16[384,512]{1,0:T(8,128)(2,1)}, bf16[384,512]{1,0:T(8,128)(2,1)}, u32[]{:S(2)}, u32[]{:S(2)}) collective-permute-start(bf16[384,512]{1,0:T(8,128)(2,1)} %bitcast.8), channel_id=1, source_target_pairs={{0,1},{1,2},{2,3},{3,0},{4,5},{5,6},{6,7},{7,4},{8,9},{9,10},{10,1... | collective-permute-start | bytes 1179656 | tf_op jit(solution)/shard_map/ppermute | solution.py:23
  28.4 38.7 %collective-permute-start.4 = (bf16[384,512]{1,0:T(8,128)(2,1)}, bf16[384,512]{1,0:T(8,128)(2,1)}, u32[]{:S(2)}, u32[]{:S(2)}) collective-permute-start(bf16[384,512]{1,0:T(8,128)(2,1)} %bitcast.8), channel_id=1, source_target_pairs={{0,2},{1,3},{2,0},{3,1},{4,6},{5,7},{6,4},{7,5},{8,10},{9,11},{10,... | collective-permute-start | bytes 1179656 | tf_op jit(solution)/shard_map/ppermute | solution.py:23
  33.3 24.8 %all-to-all-start = ((f32[8,16,128]{2,1,0:T(8,128)}), f32[8,16,128]{2,1,0:T(8,128)S(1)}, u32[]{:S(2)}, u32[]{:S(2)}) async-start(f32[8,16,128]{2,1,0:T(8,128)} %broadcast_in_dim.103), calls=%async_computation | async-start | bytes 131072 | tf_op jit(solution)/shard_map/all_to_all | solution.py:37
  60.3 12.5 %collective-permute-start.5 = (bf16[384,512]{1,0:T(8,128)(2,1)}, bf16[384,512]{1,0:T(8,128)(2,1)S(1)}, u32[]{:S(2)}, u32[]{:S(2)}) collective-permute-start(bf16[384,512]{1,0:T(8,128)(2,1)} %bitcast.8), channel_id=1, source_target_pairs={{0,3},{1,0},{2,1},{3,2},{4,7},{5,4},{6,5},{7,6},{8,11},{9,8},{10,9... | collective-permute-start | bytes 1179656 | tf_op jit(solution)/shard_map/ppermute | solution.py:23
  84.2 47.7 %copy-start.1 = (bf16[4,512,768]{2,1,0:T(8,128)(2,1)S(1)}, bf16[4,512,768]{2,1,0:T(8,128)(2,1)}, u32[]{:S(2)}) copy-start(bf16[4,512,768]{2,1,0:T(8,128)(2,1)} %copy-done) | copy-start | bytes 9437188
  139.7 28.7 %all-to-all-start.2 = ((bf16[64,24,512]{2,1,0:T(8,128)(2,1)}), bf16[64,24,512]{2,1,0:T(8,128)(2,1)}, u32[]{:S(2)}, u32[]{:S(2)}) async-start(bf16[64,24,512]{2,1,0:T(8,128)(2,1)} %bitcast.107), calls=%async_computation.2 | async-start | bytes 3145728 | tf_op jit(solution)/shard_map/all_to_all | solution.py:167
  147.1 81.8 %reduce-scatter.2.cloned.1.call-start = ((), (), s32[]{:S(2)}) async-start(), calls=%async_computation.5 | async-start | bytes 1179648 | tf_op jit(solution)/shard_map/reduce_scatter | solution.py:170
  148.6 19.8 %copy-start.2 = (bf16[4,384,256]{2,1,0:T(8,128)(2,1)S(1)}, bf16[4,384,256]{2,1,0:T(8,128)(2,1)}, u32[]{:S(2)}) copy-start(bf16[4,384,256]{2,1,0:T(8,128)(2,1)} %get-tuple-element.31.pick) | copy-start | bytes 2359300
  149.8 40.2 %collective-permute-start.8 = (bf16[512,384]{1,0:T(8,128)(2,1)}, bf16[512,384]{1,0:T(8,128)(2,1)S(1)}, u32[]{:S(2)}, u32[]{:S(2)}) collective-permute-start(bf16[512,384]{1,0:T(8,128)(2,1)} %convolution_convert_fusion.9), channel_id=1, source_target_pairs={{0,2},{1,3},{2,0},{3,1},{4,6},{5,7},{6,4},{7,5},{8,10},{9,11},{10,... | collective-permute-start | bytes 1179656 | tf_op jit(solution)/shard_map/ppermute | solution.py:23
  154.2 54.0 %collective-permute-start.7 = (bf16[512,384]{1,0:T(8,128)(2,1)}, bf16[512,384]{1,0:T(8,128)(2,1)}, u32[]{:S(2)}, u32[]{:S(2)}) collective-permute-start(bf16[512,384]{1,0:T(8,128)(2,1)} %convolution_convert_fusion.10), channel_id=1, source_target_pairs={{0,3},{1,0},{2,1},{3,2},{4,7},{5,4},{6,5},{7,6},{8,11},{9,8},{10,9... | collective-permute-start | bytes 1179656 | tf_op jit(solution)/shard_map/ppermute | solution.py:23
  173.1 16.0 %copy-start.6 = (bf16[384,384]{1,0:T(8,128)(2,1)S(1)}, bf16[384,384]{1,0:T(8,128)(2,1)}, u32[]{:S(2)}) copy-start(bf16[384,384]{1,0:T(8,128)(2,1)} %get-tuple-element.24) | copy-start | bytes 884740
  173.1 19.3 %collective-permute-start.14 = (bf16[384,512]{1,0:T(8,128)(2,1)S(1)}, bf16[384,512]{1,0:T(8,128)(2,1)S(1)}, u32[]{:S(2)}, u32[]{:S(2)}) collective-permute-start(bf16[384,512]{1,0:T(8,128)(2,1)S(1)} %convolution_convert_fusion.1), channel_id=1, source_target_pairs={{0,2},{1,3},{2,0},{3,1},{4,6},{5,7},{6,4},{7,5},{8,10},{9,11},{10,... | collective-permute-start | bytes 1179656 | tf_op jit(solution)/shard_map/ppermute | solution.py:23
  181.0 19.0 %collective-permute-start.13 = (bf16[384,512]{1,0:T(8,128)(2,1)S(1)}, bf16[384,512]{1,0:T(8,128)(2,1)S(1)}, u32[]{:S(2)}, u32[]{:S(2)}) collective-permute-start(bf16[384,512]{1,0:T(8,128)(2,1)S(1)} %convolution_convert_fusion.2), channel_id=1, source_target_pairs={{0,3},{1,0},{2,1},{3,2},{4,7},{5,4},{6,5},{7,6},{8,11},{9,8},{10,9... | collective-permute-start | bytes 1179656 | tf_op jit(solution)/shard_map/ppermute | solution.py:23
  183.3 19.7 %collective-permute-start.12 = (bf16[384,512]{1,0:T(8,128)(2,1)S(1)}, bf16[384,512]{1,0:T(8,128)(2,1)S(1)}, u32[]{:S(2)}, u32[]{:S(2)}) collective-permute-start(bf16[384,512]{1,0:T(8,128)(2,1)S(1)} %convolution_convert_fusion.3), channel_id=1, source_target_pairs={{0,1},{1,2},{2,3},{3,0},{4,5},{5,6},{6,7},{7,4},{8,9},{9,10},{10,1... | collective-permute-start | bytes 1179656 | tf_op jit(solution)/shard_map/ppermute | solution.py:23
  190.1 18.2 %collective-permute-start.6 = (bf16[512,384]{1,0:T(8,128)(2,1)S(1)}, bf16[512,384]{1,0:T(8,128)(2,1)S(1)}, u32[]{:S(2)}, u32[]{:S(2)}) collective-permute-start(bf16[512,384]{1,0:T(8,128)(2,1)S(1)} %convolution_convert_fusion.11), channel_id=1, source_target_pairs={{0,1},{1,2},{2,3},{3,0},{4,5},{5,6},{6,7},{7,4},{8,9},{9,10},{10,1... | collective-permute-start | bytes 1179656 | tf_op jit(solution)/shard_map/ppermute | solution.py:23
  192.5 18.0 %collective-permute-start.11 = (bf16[512,384]{1,0:T(8,128)(2,1)S(1)}, bf16[512,384]{1,0:T(8,128)(2,1)S(1)}, u32[]{:S(2)}, u32[]{:S(2)}) collective-permute-start(bf16[512,384]{1,0:T(8,128)(2,1)S(1)} %convolution_convert_fusion.5), channel_id=1, source_target_pairs={{0,2},{1,3},{2,0},{3,1},{4,6},{5,7},{6,4},{7,5},{8,10},{9,11},{10,... | collective-permute-start | bytes 1179656 | tf_op jit(solution)/shard_map/ppermute | solution.py:23
  200.0 16.5 %collective-permute-start.10 = (bf16[512,384]{1,0:T(8,128)(2,1)S(1)}, bf16[512,384]{1,0:T(8,128)(2,1)S(1)}, u32[]{:S(2)}, u32[]{:S(2)}) collective-permute-start(bf16[512,384]{1,0:T(8,128)(2,1)S(1)} %convolution_convert_fusion.6), channel_id=1, source_target_pairs={{0,3},{1,0},{2,1},{3,2},{4,7},{5,4},{6,5},{7,6},{8,11},{9,8},{10,9... | collective-permute-start | bytes 1179656 | tf_op jit(solution)/shard_map/ppermute | solution.py:23
  203.0 18.1 %collective-permute-start.9 = (bf16[512,384]{1,0:T(8,128)(2,1)S(1)}, bf16[512,384]{1,0:T(8,128)(2,1)S(1)}, u32[]{:S(2)}, u32[]{:S(2)}) collective-permute-start(bf16[512,384]{1,0:T(8,128)(2,1)S(1)} %convolution_convert_fusion.7), channel_id=1, source_target_pairs={{0,1},{1,2},{2,3},{3,0},{4,5},{5,6},{6,7},{7,4},{8,9},{9,10},{10,1... | collective-permute-start | bytes 1179656 | tf_op jit(solution)/shard_map/ppermute | solution.py:23
  (8 other events, 47.5 us)
Sparse Core Ops, SparseCore 0:
  10.7 70.8 all-gather.1
  172.8 56.0 reduce-scatter.1
